TPU v7x, 32 devices: a whole 2x2x4 slice. The times are simulated.
32 devices in a mesh: dp: 8 (over y, x, core), mp: 4 (over z).
Axes of the slice: x: 2, y: 2, z: 4, core: 2. Of those that a mesh axis runs over, the one named last changes fastest.
Arguments:
- tokens: bfloat16 [16384, 768], P(('dp', 'mp')), may hold values from -6 to 6
- segment_ids: int32 [16384], P('dp'), may hold values from 0 to 1663, as said below
- w_query: bfloat16 [768, 768], P(None, 'mp'), may hold values from -0.21875 to 0.21875
- b_query: float32 [768], P('mp'), may hold values from -3 to 3
- w_key: bfloat16 [768, 768], P(None, 'mp'), may hold values from -0.21875 to 0.21875
- w_value: bfloat16 [768, 768], P(None, 'mp'), may hold values from -0.21875 to 0.21875
- b_value: float32 [768], P('mp'), may hold values from -3 to 3
- w_out: bfloat16 [768, 768], P('mp'), may hold values from -1.75 to 1.75
- b_out: float32 [768], replicated, may hold values from -3 to 3
- gain_one: float32 [768], replicated, may hold values from 0.5 to 1.5
- shift_one: float32 [768], replicated, may hold values from -3 to 3
- w_up: bfloat16 [768, 3072], P(None, 'mp'), may hold values from -0.21875 to 0.21875
- b_up: float32 [3072], P('mp'), may hold values from -3 to 3
- w_down: bfloat16 [3072, 768], P('mp'), may hold values from -0.109375 to 0.109375
- b_down: float32 [768], replicated, may hold values from -3 to 3
- gain_two: float32 [768], replicated, may hold values from 0.5 to 1.5
- shift_two: float32 [768], replicated, may hold values from -3 to 3
- cotangent: bfloat16 [16384, 768], P(('dp', 'mp')), may hold values from -6 to 6
Outputs:
- output: bfloat16 [16384, 768], P(('dp', 'mp'))
- grad_tokens: float32 [16384, 768], P(('dp', 'mp'))
- grad_w_query: float32 [768, 768], P(None, 'mp')
- grad_b_query: float32 [768], P('mp')
- grad_w_key: float32 [768, 768], P(None, 'mp')
- grad_w_value: float32 [768, 768], P(None, 'mp')
- grad_b_value: float32 [768], P('mp')
- grad_w_out: float32 [768, 768], P('mp')
- grad_b_out: float32 [768], replicated
- grad_gain_one: float32 [768], replicated
- grad_shift_one: float32 [768], replicated
- grad_w_up: float32 [768, 3072], P(None, 'mp')
- grad_b_up: float32 [3072], P('mp')
- grad_w_down: float32 [3072, 768], P('mp')
- grad_b_down: float32 [768], replicated
- grad_gain_two: float32 [768], replicated
- grad_shift_two: float32 [768], replicated
Inputs may be any that keep to these rules, and one draw needn't show every extreme that they name: `segment_ids`: never falling along the tokens, rising by one at each fragment start; fragments never cross the edge of a packed row of 512 tokens, a fragment starts at every multiple of 128, each fragment covers 1 to 128 consecutive tokens, each packed row has one of exactly 128 and holds exactly 4 + 3 * (16) fragments.
All inputs are finite; a program needn't handle non-finite values.
Results may differ from a plain program's by a relative error of at most 0.012.
Values may be sent and summed in bfloat16 or wider, within the bound.
A program may use at most 128 MiB of HBM per device.

v0:
```python
from functools import partial

import jax
import jax.numpy as jnp
from jax import lax
from jax.sharding import PartitionSpec as P

HD = 64
SEQ = 512


def matmul(left, right):
    return jnp.dot(left, right, preferred_element_type=jnp.float32)


def rows_product(left, right):
    return lax.dot_general(
        left, right, (((0,), (0,)), ((), ())), preferred_element_type=jnp.float32
    )


def times_transpose(left, right):
    return lax.dot_general(
        left, right, (((1,), (1,)), ((), ())), preferred_element_type=jnp.float32
    )


def norm_forward(value, gain, shift):
    center = value - jnp.mean(value, axis=-1, keepdims=True)
    variance = jnp.mean(center * center, axis=-1, keepdims=True)
    inverse = lax.rsqrt(variance + 1e-05)
    unit = center * inverse
    return (unit * gain + shift, unit, inverse)


def norm_backward(grad, unit, inverse, gain):
    scaled = grad * gain
    inner = (
        scaled
        - jnp.mean(scaled, axis=-1, keepdims=True)
        - unit * jnp.mean(scaled * unit, axis=-1, keepdims=True)
    )
    return (inverse * inner, jnp.sum(grad * unit, axis=0), jnp.sum(grad, axis=0))


def row_scores(query, key, segment):
    score = jnp.einsum("qhd,khd->hqk", query, key, preferred_element_type=jnp.float32) * HD ** (
        -0.5
    )
    same = segment[:, None] == segment[None, :]
    return jnp.where(same[None], score, -1000000000.0)


def attend_forward(inputs):
    query, key, value, segment = inputs
    score = row_scores(query, key, segment)
    top = jnp.max(score, axis=-1, keepdims=True)
    expo = jnp.exp(score - top)
    total = jnp.sum(expo, axis=-1, keepdims=True)
    prob_low = (expo / total).astype(jnp.bfloat16)
    context = jnp.einsum("hqk,khd->qhd", prob_low, value, preferred_element_type=jnp.float32)
    return (context.astype(jnp.bfloat16), (top + jnp.log(total))[..., 0])


def attend_backward(inputs):
    query, key, value, segment, log_total, grad_context = inputs
    score = row_scores(query, key, segment)
    prob = jnp.exp(score - log_total[..., None])
    prob_low = prob.astype(jnp.bfloat16)
    grad_prob = jnp.einsum("qhd,khd->hqk", grad_context, value, preferred_element_type=jnp.float32)
    grad_value = jnp.einsum(
        "hqk,qhd->khd", prob_low, grad_context, preferred_element_type=jnp.float32
    )
    grad_score = (prob * (grad_prob - jnp.sum(grad_prob * prob, axis=-1, keepdims=True))).astype(
        jnp.bfloat16
    )
    grad_query = jnp.einsum(
        "hqk,khd->qhd", grad_score, key, preferred_element_type=jnp.float32
    ) * HD ** (-0.5)
    grad_key = jnp.einsum(
        "hqk,qhd->khd", grad_score, query, preferred_element_type=jnp.float32
    ) * HD ** (-0.5)
    return (
        grad_query.astype(jnp.bfloat16),
        grad_key.astype(jnp.bfloat16),
        grad_value.astype(jnp.bfloat16),
    )


def per_device(
    tokens,
    segment_ids,
    w_query,
    b_query,
    w_key,
    w_value,
    b_value,
    w_out,
    b_out,
    gain_one,
    shift_one,
    w_up,
    b_up,
    w_down,
    b_down,
    gain_two,
    shift_two,
    cotangent,
):
    rows_whole = segment_ids.shape[0]
    row_count = rows_whole // SEQ
    heads_local = w_query.shape[1] // HD
    shape4 = (row_count, SEQ, heads_local, HD)
    whole_in = lax.all_gather(tokens, "mp", axis=0, tiled=True)
    query = (matmul(whole_in, w_query) + b_query).astype(jnp.bfloat16)
    key = matmul(whole_in, w_key).astype(jnp.bfloat16)
    value = (matmul(whole_in, w_value) + b_value).astype(jnp.bfloat16)
    query_rows = query.reshape(shape4)
    key_rows = key.reshape(shape4)
    value_rows = value.reshape(shape4)
    segments = segment_ids.reshape(row_count, SEQ)
    context, log_total = lax.map(attend_forward, (query_rows, key_rows, value_rows, segments))
    context = context.reshape(rows_whole, heads_local * HD)
    attn = lax.psum_scatter(matmul(context, w_out), "mp", scatter_dimension=0, tiled=True)
    normed_one, unit_one, inverse_one = norm_forward(
        tokens.astype(jnp.float32) + attn + b_out, gain_one, shift_one
    )
    normed_low = normed_one.astype(jnp.bfloat16)
    normed_whole = lax.all_gather(normed_low, "mp", axis=0, tiled=True)
    up_value = matmul(normed_whole, w_up) + b_up
    act_low = jax.nn.gelu(up_value, approximate=True).astype(jnp.bfloat16)
    ffn = lax.psum_scatter(matmul(act_low, w_down), "mp", scatter_dimension=0, tiled=True)
    out_value, unit_two, inverse_two = norm_forward(normed_one + ffn + b_down, gain_two, shift_two)
    grad_resid_two, grad_gain_two, grad_shift_two = norm_backward(
        cotangent.astype(jnp.float32), unit_two, inverse_two, gain_two
    )
    grad_b_down = jnp.sum(grad_resid_two, axis=0)
    grad_down_whole = lax.all_gather(grad_resid_two.astype(jnp.bfloat16), "mp", axis=0, tiled=True)
    grad_w_down = rows_product(act_low, grad_down_whole)
    grad_act = times_transpose(grad_down_whole, w_down)
    unused, gelu_pull = jax.vjp(partial(jax.nn.gelu, approximate=True), up_value)
    grad_up = gelu_pull(grad_act)[0].astype(jnp.bfloat16)
    grad_b_up = jnp.sum(grad_up.astype(jnp.float32), axis=0)
    grad_w_up = rows_product(normed_whole, grad_up)
    grad_normed_one = grad_resid_two + lax.psum_scatter(
        times_transpose(grad_up, w_up), "mp", scatter_dimension=0, tiled=True
    )
    grad_resid_one, grad_gain_one, grad_shift_one = norm_backward(
        grad_normed_one, unit_one, inverse_one, gain_one
    )
    grad_b_out = jnp.sum(grad_resid_one, axis=0)
    grad_one_low = grad_resid_one.astype(jnp.bfloat16)
    grad_attn_whole = lax.all_gather(grad_one_low, "mp", axis=0, tiled=True)
    grad_w_out = rows_product(context, grad_attn_whole)
    grad_context = times_transpose(grad_attn_whole, w_out).astype(jnp.bfloat16)
    grad_query, grad_key, grad_value = lax.map(
        attend_backward,
        (query_rows, key_rows, value_rows, segments, log_total, grad_context.reshape(shape4)),
    )
    grad_query = grad_query.reshape(rows_whole, heads_local * HD)
    grad_key = grad_key.reshape(rows_whole, heads_local * HD)
    grad_value = grad_value.reshape(rows_whole, heads_local * HD)
    grad_w_query = rows_product(whole_in, grad_query)
    grad_w_key = rows_product(whole_in, grad_key)
    grad_w_value = rows_product(whole_in, grad_value)
    grad_b_query = jnp.sum(grad_query.astype(jnp.float32), axis=0)
    grad_b_value = jnp.sum(grad_value.astype(jnp.float32), axis=0)
    total = times_transpose(grad_query, w_query)
    total = total + times_transpose(grad_key, w_key)
    grad_tokens = grad_resid_one + lax.psum_scatter(
        total + times_transpose(grad_value, w_value), "mp", scatter_dimension=0, tiled=True
    )
    (
        grad_w_query,
        grad_w_key,
        grad_w_value,
        grad_b_query,
        grad_b_value,
        grad_w_out,
        grad_w_up,
        grad_b_up,
        grad_w_down,
    ) = lax.psum(
        (
            grad_w_query,
            grad_w_key,
            grad_w_value,
            grad_b_query,
            grad_b_value,
            grad_w_out,
            grad_w_up,
            grad_b_up,
            grad_w_down,
        ),
        "dp",
    )
    grad_b_out, grad_gain_one, grad_shift_one, grad_b_down, grad_gain_two, grad_shift_two = (
        lax.psum(
            (grad_b_out, grad_gain_one, grad_shift_one, grad_b_down, grad_gain_two, grad_shift_two),
            ("dp", "mp"),
        )
    )
    return (
        out_value.astype(jnp.bfloat16),
        grad_tokens,
        grad_w_query,
        grad_b_query,
        grad_w_key,
        grad_w_value,
        grad_b_value,
        grad_w_out,
        grad_b_out,
        grad_gain_one,
        grad_shift_one,
        grad_w_up,
        grad_b_up,
        grad_w_down,
        grad_b_down,
        grad_gain_two,
        grad_shift_two,
    )


def solution(mesh):
    return jax.shard_map(
        per_device,
        mesh=mesh,
        in_specs=(
            P(("dp", "mp"), None),
            P("dp"),
            P(None, "mp"),
            P("mp"),
            P(None, "mp"),
            P(None, "mp"),
            P("mp"),
            P("mp", None),
            P(),
            P(),
            P(),
            P(None, "mp"),
            P("mp"),
            P("mp", None),
            P(),
            P(),
            P(),
            P(("dp", "mp"), None),
        ),
        out_specs=(
            P(("dp", "mp"), None),
            P(("dp", "mp"), None),
            P(None, "mp"),
            P("mp"),
            P(None, "mp"),
            P(None, "mp"),
            P("mp"),
            P("mp", None),
            P(),
            P(),
            P(),
            P(None, "mp"),
            P("mp"),
            P("mp", None),
            P(),
            P(),
            P(),
        ),
        check_vma=False,
    )
```

profile of v0, /device:TPU:0, one launch (start us, length us, event | category | flops | bytes accessed | tf_op | source)
XLA Modules:
  0.0 975.2 jit_solution(13268380016145972109)
XLA Ops:
  8.7 67.1 %all-gather.5.cloned.1.call-done = bf16[2048,768]{1,0:T(8,128)(2,1)} async-done(((bf16[512,768]{1,0:T(8,128)(2,1)}), bf16[2048,768]{1,0:T(8,128)(2,1)}) %all-gather.5.cloned.1.call-update) | async-done | bytes 3145744 | tf_op jit(solution)/shard_map/all_gather | solution.py:114
  75.8 3.1 convolution_convert_fusion.1
  79.9 3.1 fusion.62
  83.7 3.1 fusion.61
  90.5 16.3 %while.26 = (s32[]{:T(128)}, bf16[4,512,3,64]{1,3,2,0:T(8,128)(2,1)}, f32[4,3,512]{2,1,0:T(4,128)}, bf16[4,512,3,64]{1,3,2,0:T(8,128)(2,1)S(1)}, s32[4,512]{1,0:...) while((s32[]{:T(128)}, ...), condition=%wide.region_3.4_spmd, body=%wide.region_0.3_spmd.sunk | while | flops 211122688 | bytes 11335781 | solution.py:122
  92.2 1.8 fusion.141
  96.3 1.8 fusion.141
  100.4 1.8 fusion.141
  104.4 1.8 fusion.141
  106.8 2.3 copy.53
  109.4 3.7 fusion.77
  113.2 109.5 %reduce-scatter.5.cloned.1.call-done = f32[512,768]{1,0:T(8,128)} async-done(((f32[2048,768]{1,0:T(8,128)}), f32[512,768]{1,0:T(8,128)}) %reduce-scatter.5.cloned.1.call-update) | async-done | bytes 1572880 | tf_op jit(solution)/shard_map/reduce_scatter | solution.py:124
  222.7 1.9 fusion.76
  225.5 1.9 fusion.70
  227.6 64.0 %all-gather.7.cloned.1.call-done = bf16[2048,768]{1,0:T(8,128)(2,1)} async-done(((bf16[512,768]{1,0:T(8,128)(2,1)}), bf16[2048,768]{1,0:T(8,128)(2,1)}) %all-gather.7.cloned.1.call-update) | async-done | bytes 3145744 | tf_op jit(solution)/shard_map/all_gather | solution.py:129
  291.6 8.4 multiply_convert_fusion.1
  300.0 1.7 copy-done.42
  301.7 4.4 fusion.78
  306.2 109.5 %reduce-scatter.7.cloned.1.call-done = f32[512,768]{1,0:T(8,128)} async-done(((f32[2048,768]{1,0:T(8,128)}), f32[512,768]{1,0:T(8,128)}) %reduce-scatter.7.cloned.1.call-update) | async-done | bytes 1572880 | tf_op jit(solution)/shard_map/reduce_scatter | solution.py:132
  415.7 2.0 fusion.75
  419.4 2.1 fusion.71
  423.7 64.1 %all-gather.9.cloned.1.call-done = bf16[2048,768]{1,0:T(8,128)(2,1)} async-done(((bf16[512,768]{1,0:T(8,128)(2,1)}), bf16[2048,768]{1,0:T(8,128)(2,1)}) %all-gather.9.cloned.1.call-update) | async-done | bytes 3145744 | tf_op jit(solution)/shard_map/all_gather | solution.py:138
  487.9 9.4 convert_reduce_fusion
  497.3 1.6 copy-done.43
  498.9 4.6 fusion.79
  503.8 109.3 %reduce-scatter.9.cloned.1.call-done = f32[512,768]{1,0:T(8,128)} async-done(((f32[2048,768]{1,0:T(8,128)}), f32[512,768]{1,0:T(8,128)}) %reduce-scatter.9.cloned.1.call-update) | async-done | bytes 1572880 | tf_op jit(solution)/shard_map/reduce_scatter | solution.py:145
  613.0 3.3 multiply_reduce_fusion.1
  619.7 64.1 %all-gather.11.cloned.1.call-done = bf16[2048,768]{1,0:T(8,128)(2,1)} async-done(((bf16[512,768]{1,0:T(8,128)(2,1)}), bf16[2048,768]{1,0:T(8,128)(2,1)}) %all-gather.11.cloned.1.call-update) | async-done | bytes 3145744 | tf_op jit(solution)/shard_map/all_gather | solution.py:153
  683.8 3.1 convolution_convert_fusion
  689.6 29.0 %while.27 = (s32[]{:T(128)}, bf16[4,512,3,64]{1,3,2,0:T(8,128)(2,1)}, bf16[4,512,3,64]{1,3,2,0:T(8,128)(2,1)}, bf16[4,512,3,64]{1,3,2,0:T(8,128)(2,1)S(1)}, bf16...) while((s32[]{:T(128)}, ...), condition=%wide.region_17.18_spmd, body=%wide.region_15.17_spmd.sunk | while | flops 511146496 | bytes 26127484 | solution.py:156
  699.3 1.6 multiply_reduce_fusion.7
  713.8 1.6 multiply_reduce_fusion.7
  718.6 2.1 copy.59
  724.6 3.8 add_add_fusion
  728.7 7.1 fusion.84
  735.8 4.2 fusion.83
  740.0 1.6 fusion.82
  742.1 1.6 convolution_bitcast_fusion.2
  743.7 1.6 convolution_bitcast_fusion
  745.3 1.6 convolution_bitcast_fusion.1
  747.7 47.7 %all-reduce = (f32[768]{0:T(1024)}, f32[768]{0:T(1024)}, f32[768]{0:T(1024)}, f32[768]{0:T(1024)}, f32[768]{0:T(1024)}, /*index=5*/f32[768]{0:T(1024)}) all-reduce(f32[768]{0:T(1024)S(1)} %copy-done.30, f32[768]{0:T(1024)S(1)} %copy-done.33, f32[768]{0:T(1024)S(1)} %copy-done.34, ...), channel_id=1, replica_groups=mesh['dp'=8,'mp'=4] {'dp','mp'}, use_global_device_ids=true, to_apply=%region_28.29 | all-reduce | flops 4608 | bytes 36864 | tf_op jit(solution)/shard_map/psum | solution.py:198
  795.9 14.7 %all-reduce.1 = (f32[192]{0:T(256)}, f32[192]{0:T(256)}, f32[768]{0:T(1024)}) all-reduce(f32[192]{0:T(256)S(1)} %reduce_sum.184, f32[192]{0:T(256)S(1)} %reduce_sum.186, f32[768]{0:T(1024)S(1)} %copy-done.35), channel_id=1, replica_groups=mesh['dp'=8,'mp'=4] {'dp'}, use_global_device_ids=true, to_apply=%region_21.22 | all-reduce | flops 1152 | bytes 9216 | tf_op jit(solution)/shard_map/psum | solution.py:183
  810.6 28.4 %reduce-scatter.11.cloned.1.call-done = f32[512,768]{1,0:T(8,128)} async-done(((f32[2048,768]{1,0:T(8,128)}), f32[512,768]{1,0:T(8,128)}) %reduce-scatter.11.cloned.1.call-update) | async-done | bytes 1572880 | tf_op jit(solution)/shard_map/reduce_scatter | solution.py:170
  839.0 2.7 add.181
  841.8 116.9 %all-reduce.5.cloned.1.call-done = (f32[768,192]{0,1:T(8,128)}, f32[768,192]{0,1:T(8,128)}, f32[768,192]{0,1:T(8,128)}, f32[192,768]{1,0:T(8,128)}, f32[768,768]{1,0:T(8,128)}, /*index=5*/f32[768,768]{1,0:T(8,128)}) async-done(((f32[768,192]{0,1:T(8,128)}, f32[768,192]{0,1:T(8,128)}, f32[768,192]{0,1:T(8,128)}, f32[192,768]{1,0:T(8,128)}, f32[768,768]{1,0:T(8,128)}, /*index=5*/f32[768,768]{1,0:T(8,128)}), ...) | async-done | bytes 7077904 | tf_op jit(solution)/shard_map/psum | solution.py:183
  958.7 2.1 copy.103
  960.8 1.9 copy.104
  962.7 1.9 copy.105
  (202 shorter events, 62.8 us)
Async XLA Ops:
  7.2 284.4 %copy-start = (bf16[768,768]{1,0:T(8,128)(2,1)S(1)}, bf16[768,768]{1,0:T(8,128)(2,1)}, u32[]{:S(2)}) copy-start(bf16[768,768]{1,0:T(8,128)(2,1)} %param.33) | copy-start | bytes 3538948
  7.2 68.6 %all-gather.5.cloned.1.call-start = ((), (), s32[]{:S(2)}) async-start(), calls=%async_computation.4 | async-start | bytes 3932160 | tf_op jit(solution)/shard_map/all_gather | solution.py:114
  7.9 214.7 %reduce-scatter.5.cloned.1.call-start = ((), (), s32[]{:S(2)}) async-start(), calls=%async_computation.5 | async-start | bytes 7864320 | tf_op jit(solution)/shard_map/reduce_scatter | solution.py:124
  78.9 1.0 copy-start.22
  78.9 1.0 copy-start.40
  83.0 0.8 copy-start.41
  106.8 2.3 copy-start.13
  106.8 6.3 copy-start.6
  106.8 2.5 copy-start.19
  109.4 3.7 copy-start.8
  113.1 109.6 %copy-start.36 = (f32[768]{0:T(1024)S(1)}, f32[768]{0:T(1024)}, u32[]{:S(2)}) copy-start(f32[768]{0:T(1024)} %param.30) | copy-start | bytes 9220
  113.1 112.4 %copy-start.25 = (f32[768]{0:T(1024)S(1)}, f32[768]{0:T(1024)}, u32[]{:S(2)}) copy-start(f32[768]{0:T(1024)} %param.31) | copy-start | bytes 9220
  113.1 178.4 %all-gather.7.cloned.1.call-start = ((), (), s32[]{:S(2)}) async-start(), calls=%async_computation.6 | async-start | bytes 3932160 | tf_op jit(solution)/shard_map/all_gather | solution.py:129
  227.4 188.3 %reduce-scatter.7.cloned.1.call-start = ((), (), s32[]{:S(2)}) async-start(), calls=%async_computation.7 | async-start | bytes 7864320 | tf_op jit(solution)/shard_map/reduce_scatter | solution.py:132
  291.6 10.1 %copy-start.39 = (bf16[768,768]{1,0:T(8,128)(2,1)S(1)}, bf16[768,768]{1,0:T(8,128)(2,1)}, u32[]{:S(2)}) copy-start(bf16[768,768]{1,0:T(8,128)(2,1)} %param.35) | copy-start | bytes 3538948
  300.0 1.7 copy-start.42
  306.1 181.7 %all-gather.9.cloned.1.call-start = ((), (), s32[]{:S(2)}) async-start(), calls=%async_computation.8 | async-start | bytes 3932160 | tf_op jit(solution)/shard_map/all_gather | solution.py:138
  415.7 2.4 copy-start.15
  415.7 2.4 copy-start.31
  417.8 1.7 copy-start.37
  421.6 1.1 copy-start.5
  423.7 189.3 %reduce-scatter.9.cloned.1.call-start = ((), (), s32[]{:S(2)}) async-start(), calls=%async_computation.9 | async-start | bytes 7864320 | tf_op jit(solution)/shard_map/reduce_scatter | solution.py:145
  497.3 1.6 copy-start.43
  503.5 109.6 %copy-start.27 = (f32[512]{0:T(512)S(1)}, f32[512]{0:T(512)}, u32[]{:S(2)}) copy-start(f32[512]{0:T(512)} %copy-done.26) | copy-start | bytes 6148
  503.5 180.3 %all-gather.11.cloned.1.call-start = ((), (), s32[]{:S(2)}) async-start(), calls=%async_computation.10 | async-start | bytes 3932160 | tf_op jit(solution)/shard_map/all_gather | solution.py:153
  616.4 67.4 %copy-start.20 = (bf16[192,768]{1,0:T(8,128)(2,1)S(1)}, bf16[192,768]{1,0:T(8,128)(2,1)}, u32[]{:S(2)}) copy-start(bf16[192,768]{1,0:T(8,128)(2,1)} %param.29) | copy-start | bytes 884740
  617.5 1.1 copy-start.3
  619.6 219.4 %reduce-scatter.11.cloned.1.call-start = ((), (), s32[]{:S(2)}) async-start(), calls=%async_computation.11 | async-start | bytes 7864320 | tf_op jit(solution)/shard_map/reduce_scatter | solution.py:170
  686.8 2.7 copy-start.7
  718.6 3.1 copy-start.10
  718.6 3.1 copy-start.12
  720.8 1.6 copy-start.21
  722.5 1.1 copy-start.23
  723.5 1.1 copy-start.24
  728.4 230.3 %all-reduce.5.cloned.1.call-start = ((), (), s32[]{:S(2)}) async-start(), calls=%async_computation.12 | async-start | bytes 14155776 | tf_op jit(solution)/shard_map/psum | solution.py:183
  728.7 7.1 copy-start.38
  728.7 7.1 copy-start.44
  735.8 4.2 copy-start.9
  735.8 4.2 copy-start.14
  740.0 2.1 copy-start.2
  746.9 0.7 copy-start.34
  746.9 48.4 %copy-start.11 = (bf16[4,512,3,64]{1,3,2,0:T(8,128)(2,1)S(1)}, bf16[4,512,3,64]{1,3,2,0:T(8,128)(2,1)}, u32[]{:S(2)}) copy-start(bf16[4,512,3,64]{1,3,2,0:T(8,128)(2,1)} %copy-done.10) | copy-start | bytes 2359300
  746.9 49.0 %copy-start.35 = (f32[768]{0:T(1024)S(1)}, f32[768]{0:T(1024)}, u32[]{:S(2)}) copy-start(f32[768]{0:T(1024)} %get-tuple-element.209) | copy-start | bytes 9220
  747.0 92.1 %copy-start.4 = (f32[512,768]{1,0:T(8,128)S(1)}, f32[512,768]{1,0:T(8,128)}, u32[]{:S(2)}) copy-start(f32[512,768]{1,0:T(8,128)} %copy-done.3) | copy-start | bytes 4718596
  958.7 5.9 copy-start.18
  958.7 6.7 copy-start.17
  964.6 2.2 copy-start.16
  965.4 2.8 copy-start.1
  (6 other events, 4.2 us)
Sparse Core Ops, SparseCore 0:
  9.6 66.1 all-gather.4
  113.2 109.3 reduce-scatter.4
  227.5 64.0 all-gather.6
  306.3 109.3 reduce-scatter.6
  423.8 64.0 all-gather.8
  503.6 109.3 reduce-scatter.8
  619.7 64.0 all-gather.10
  728.5 110.4 reduce-scatter.10
  844.3 114.3 all-reduce.4
where the time goes:
time: 983 us; the launch traced here: 975 us
  waiting for transfers between devices  734 us (75%)
  matrix products  98.4 us (10%)
  blocking collectives  62.4 us (6%)
  local copies, waits for them, and re-layouts  35.1 us (4%)
  other arithmetic  29.6 us (3%)
  between operations  14.8 us (2%)
    psum x1, waiting for transfers between devices, per_device(): lax.psum((grad_w_query, grad_w_key, grad_w_value, grad_b_query, grad_b_va...  117 us
    reduce_scatter x1, waiting for transfers between devices, per_device(): lax.psum_scatter(matmul(act_low, w_down), 'mp', scatter_dimension=0, tile...  110 us
    reduce_scatter x1, waiting for transfers between devices, per_device(): lax.psum_scatter(matmul(context, w_out), 'mp', scatter_dimension=0, tiled...  109 us
    reduce_scatter x1, waiting for transfers between devices, per_device(): lax.psum_scatter(times_transpose(grad_up, w_up), 'mp', scatter_dimension=...  109 us
    all_gather x1, waiting for transfers between devices, per_device(): whole_in = lax.all_gather(tokens, 'mp', axis=0, tiled=True)  67.1 us
    all_gather x1, waiting for transfers between devices, per_device(): lax.all_gather(grad_resid_two.astype(jnp.bfloat16), 'mp', axis=0, tiled=T...  64.1 us
    all_gather x1, waiting for transfers between devices, per_device(): grad_attn_whole = lax.all_gather(grad_one_low, 'mp', axis=0, tiled=True)  64.1 us
    all_gather x1, waiting for transfers between devices, per_device(): normed_whole = lax.all_gather(normed_low, 'mp', axis=0, tiled=True)  64 us
  transfers between devices with their start and end apart: 9, of which 9 were waited for; matrix products, arithmetic and copies ran while one was open for 2% of the time, Pallas kernels for 0%

commit v1 on v0

v1 whole, which is shorter than its diff:
```python
from functools import partial

import jax
import jax.numpy as jnp
from jax import lax
from jax.sharding import PartitionSpec as P

HD = 64
BLOCK = 128


def matmul(left, right):
    return jnp.dot(left, right, preferred_element_type=jnp.float32)


def rows_product(left, right):
    return lax.dot_general(
        left, right, (((0,), (0,)), ((), ())), preferred_element_type=jnp.float32
    )


def times_transpose(left, right):
    return lax.dot_general(
        left, right, (((1,), (1,)), ((), ())), preferred_element_type=jnp.float32
    )


def norm_forward(value, gain, shift):
    center = value - jnp.mean(value, axis=-1, keepdims=True)
    variance = jnp.mean(center * center, axis=-1, keepdims=True)
    inverse = lax.rsqrt(variance + 1e-05)
    unit = center * inverse
    return (unit * gain + shift, unit, inverse)


def norm_backward(grad, unit, inverse, gain):
    scaled = grad * gain
    inner = (
        scaled
        - jnp.mean(scaled, axis=-1, keepdims=True)
        - unit * jnp.mean(scaled * unit, axis=-1, keepdims=True)
    )
    return (inverse * inner, jnp.sum(grad * unit, axis=0), jnp.sum(grad, axis=0))


def einsum(spec, left, right):
    return jnp.einsum(spec, left, right, preferred_element_type=jnp.float32)


def per_device(
    tokens,
    segment_ids,
    w_query,
    b_query,
    w_key,
    w_value,
    b_value,
    w_out,
    b_out,
    gain_one,
    shift_one,
    w_up,
    b_up,
    w_down,
    b_down,
    gain_two,
    shift_two,
    cotangent,
):
    rows, width = tokens.shape
    heads = width // HD
    blocks = rows // BLOCK
    low = jnp.bfloat16

    def whole(array, axis):
        return lax.all_gather(array, "mp", axis=axis, tiled=True)

    w_query, w_key, w_value = whole(w_query, 1), whole(w_key, 1), whole(w_value, 1)
    b_query, b_value, b_up = whole(b_query, 0), whole(b_value, 0), whole(b_up, 0)
    w_out, w_up, w_down = whole(w_out, 0), whole(w_up, 1), whole(w_down, 0)

    segment = lax.dynamic_slice(segment_ids, (lax.axis_index("mp") * rows,), (rows,))
    segment = segment.reshape(blocks, BLOCK)
    shape4 = (blocks, BLOCK, heads, HD)
    query = (matmul(tokens, w_query) + b_query).astype(low).reshape(shape4)
    key = matmul(tokens, w_key).astype(low).reshape(shape4)
    value = (matmul(tokens, w_value) + b_value).astype(low).reshape(shape4)
    score = einsum("bqhd,bkhd->bhqk", query, key) * HD ** (-0.5)
    same = segment[:, :, None] == segment[:, None, :]
    score = jnp.where(same[:, None], score, -1000000000.0)
    expo = jnp.exp(score - jnp.max(score, axis=-1, keepdims=True))
    prob = expo / jnp.sum(expo, axis=-1, keepdims=True)
    prob_low = prob.astype(low)
    context = einsum("bhqk,bkhd->bqhd", prob_low, value).astype(low).reshape(rows, width)
    normed_one, unit_one, inverse_one = norm_forward(
        tokens.astype(jnp.float32) + matmul(context, w_out) + b_out, gain_one, shift_one
    )
    normed_low = normed_one.astype(low)
    up_value = matmul(normed_low, w_up) + b_up
    act_low = jax.nn.gelu(up_value, approximate=True).astype(low)
    out_value, unit_two, inverse_two = norm_forward(
        normed_one + matmul(act_low, w_down) + b_down, gain_two, shift_two
    )
    grad_resid_two, grad_gain_two, grad_shift_two = norm_backward(
        cotangent.astype(jnp.float32), unit_two, inverse_two, gain_two
    )
    grad_b_down = jnp.sum(grad_resid_two, axis=0)
    grad_two_low = grad_resid_two.astype(low)
    grad_w_down = rows_product(act_low, grad_two_low)
    grad_act = times_transpose(grad_two_low, w_down)
    unused, gelu_pull = jax.vjp(partial(jax.nn.gelu, approximate=True), up_value)
    grad_up = gelu_pull(grad_act)[0].astype(low)
    grad_b_up = jnp.sum(grad_up.astype(jnp.float32), axis=0)
    grad_w_up = rows_product(normed_low, grad_up)
    grad_normed_one = grad_resid_two + times_transpose(grad_up, w_up)
    grad_resid_one, grad_gain_one, grad_shift_one = norm_backward(
        grad_normed_one, unit_one, inverse_one, gain_one
    )
    grad_b_out = jnp.sum(grad_resid_one, axis=0)
    grad_one_low = grad_resid_one.astype(low)
    grad_w_out = rows_product(context, grad_one_low)
    grad_context = times_transpose(grad_one_low, w_out).astype(low).reshape(shape4)
    grad_prob = einsum("bqhd,bkhd->bhqk", grad_context, value)
    grad_value = einsum("bhqk,bqhd->bkhd", prob_low, grad_context).astype(low)
    grad_score = prob * (grad_prob - jnp.sum(grad_prob * prob, axis=-1, keepdims=True))
    grad_score = grad_score.astype(low)
    grad_query = (einsum("bhqk,bkhd->bqhd", grad_score, key) * HD ** (-0.5)).astype(low)
    grad_key = (einsum("bhqk,bqhd->bkhd", grad_score, query) * HD ** (-0.5)).astype(low)
    grad_query = grad_query.reshape(rows, width)
    grad_key = grad_key.reshape(rows, width)
    grad_value = grad_value.reshape(rows, width)
    grad_w_query = rows_product(tokens, grad_query)
    grad_w_key = rows_product(tokens, grad_key)
    grad_w_value = rows_product(tokens, grad_value)
    grad_b_query = jnp.sum(grad_query.astype(jnp.float32), axis=0)
    grad_b_value = jnp.sum(grad_value.astype(jnp.float32), axis=0)
    grad_tokens = (
        grad_resid_one
        + times_transpose(grad_query, w_query)
        + times_transpose(grad_key, w_key)
        + times_transpose(grad_value, w_value)
    )

    def share(array, axis):
        part = lax.psum_scatter(
            array.astype(low), "mp", scatter_dimension=axis, tiled=True
        )
        return lax.psum(part, "dp").astype(jnp.float32)

    def share_small(array):
        return lax.psum_scatter(array, "mp", scatter_dimension=0, tiled=True)

    grad_w_down = share(grad_w_down, 0)
    grad_w_up = share(grad_w_up, 1)
    grad_w_out = share(grad_w_out, 0)
    grad_w_query = share(grad_w_query, 1)
    grad_w_key = share(grad_w_key, 1)
    grad_w_value = share(grad_w_value, 1)
    grad_b_query, grad_b_value, grad_b_up = lax.psum(
        (share_small(grad_b_query), share_small(grad_b_value), share_small(grad_b_up)), "dp"
    )
    grad_b_out, grad_gain_one, grad_shift_one, grad_b_down, grad_gain_two, grad_shift_two = (
        lax.psum(
            (grad_b_out, grad_gain_one, grad_shift_one, grad_b_down, grad_gain_two, grad_shift_two),
            ("dp", "mp"),
        )
    )
    return (
        out_value.astype(low),
        grad_tokens,
        grad_w_query,
        grad_b_query,
        grad_w_key,
        grad_w_value,
        grad_b_value,
        grad_w_out,
        grad_b_out,
        grad_gain_one,
        grad_shift_one,
        grad_w_up,
        grad_b_up,
        grad_w_down,
        grad_b_down,
        grad_gain_two,
        grad_shift_two,
    )


def solution(mesh):
    return jax.shard_map(
        per_device,
        mesh=mesh,
        in_specs=(
            P(("dp", "mp"), None),
            P("dp"),
            P(None, "mp"),
            P("mp"),
            P(None, "mp"),
            P(None, "mp"),
            P("mp"),
            P("mp", None),
            P(),
            P(),
            P(),
            P(None, "mp"),
            P("mp"),
            P("mp", None),
            P(),
            P(),
            P(),
            P(("dp", "mp"), None),
        ),
        out_specs=(
            P(("dp", "mp"), None),
            P(("dp", "mp"), None),
            P(None, "mp"),
            P("mp"),
            P(None, "mp"),
            P(None, "mp"),
            P("mp"),
            P("mp", None),
            P(),
            P(),
            P(),
            P(None, "mp"),
            P("mp"),
            P("mp", None),
            P(),
            P(),
            P(),
        ),
        check_vma=False,
    )
```

time: 983 us -> 734 us (0.75)
  waiting for transfers between devices: 734 us -> 513 us
  blocking collectives: 62.4 us -> 97.2 us
  matrix products: 98.4 us -> 73.8 us
  local copies, waits for them, and re-layouts: 35.1 us -> 13.3 us
  other arithmetic: 29.6 us -> 13.6 us
    psum x1, waiting for transfers between devices: 117 us -> 3.65 us  [share(): return lax.psum(part, 'dp').astype(jnp.float32)]
    reduce_scatter x4 -> x6, waiting for transfers between devices: 357 us -> 253 us  [share(): lax.psum_scatter(array.astype(low), 'mp', scatter_dimension=axis, tiled=T...]
    unnamed x0 -> x2, blocking collectives: none -> 32.3 us
    dot_general x28 -> x6, matrix products: 32.1 us -> 10.4 us  [einsum(): return jnp.einsum(spec, left, right, preferred_element_type=jnp.float32)]
    all_gather x0 -> x1, blocking collectives: none -> 13.4 us  [whole(): return lax.all_gather(array, 'mp', axis=axis, tiled=True)]
    all_gather x4 -> x6, waiting for transfers between devices: 259 us -> 253 us  [whole(): return lax.all_gather(array, 'mp', axis=axis, tiled=True)]
  transfers between devices with their start and end apart: 9 -> 13, of which waited for: 9 -> 12; matrix products, arithmetic and copies ran while one was open for 2% -> 9% of each run, Pallas kernels for 0% -> 0%
where the time goes in v1:
time: 734 us; the launch traced here: 729 us
  waiting for transfers between devices  513 us (70%)
  blocking collectives  97.2 us (13%)
  matrix products  73.8 us (10%)
  between operations  17.1 us (2%)
  other arithmetic  13.6 us (2%)
  local copies, waits for them, and re-layouts  13.3 us (2%)
    all_gather x6, waiting for transfers between devices, whole(): return lax.all_gather(array, 'mp', axis=axis, tiled=True)  253 us
    reduce_scatter x6, waiting for transfers between devices, share(): lax.psum_scatter(array.astype(low), 'mp', scatter_dimension=axis, tiled=T...  253 us
    psum x1, blocking collectives, per_device(): lax.psum((grad_b_out, grad_gain_one, grad_shift_one, grad_b_down, grad_ga...  38.3 us
    unnamed x2, blocking collectives  32.3 us
    dot_general x6, matrix products, matmul(): return jnp.dot(left, right, preferred_element_type=jnp.float32)  23.7 us
    dot_general x6, matrix products, rows_product(): lax.dot_general(left, right, (((0,), (0,)), ((), ())), preferred_element_...  22.6 us
    dot_general x6, matrix products, times_transpose(): lax.dot_general(left, right, (((1,), (1,)), ((), ())), preferred_element_...  17 us
  transfers between devices with their start and end apart: 13, of which 12 were waited for; matrix products, arithmetic and copies ran while one was open for 9% of the time, Pallas kernels for 0%

profile of v1, /device:TPU:0, one launch (start us, length us, event | category | flops | bytes accessed | tf_op | source)
XLA Modules:
  0.0 729.1 jit_solution(1909958408877032229)
XLA Ops:
  13.1 14.1 %all-reduce.8 = (f32[768]{0:T(1024)S(1)}, f32[768]{0:T(1024)S(1)}) all-reduce(f32[768]{0:T(1024)S(1)} %dynamic-update-slice, f32[768]{0:T(1024)S(1)} %dynamic-update-slice.1), channel_id=1, replica_groups=mesh['dp'=8,'mp'=4] {'mp'}, use_global_device_ids=true, to_apply=%add | all-reduce | flops 1536 | bytes 12288
  27.2 13.4 %all-gather = f32[4,1,768]{2,1,0:T(1,128)S(1)} all-gather(f32[1,1,768]{2,1,0:T(1,128)S(1)} %reshape.129), channel_id=1, replica_groups=mesh['dp'=8,'mp'=4] {'mp'}, dimensions={0}, use_global_device_ids=true | all-gather | bytes 15360 | tf_op jit(solution)/shard_map/all_gather | solution.py:76
  40.8 1.9 all-gather.10.cloned.1.call-done
  42.7 2.1 add_convert_fusion.1
  45.3 29.1 %all-gather.12.cloned.1.call-done = bf16[768,768]{0,1:T(8,128)(2,1)} async-done(((bf16[768,192]{0,1:T(8,128)(2,1)}), bf16[768,768]{0,1:T(8,128)(2,1)}) %all-gather.12.cloned.1.call-update) | async-done | bytes 1179664 | tf_op jit(solution)/shard_map/all_gather | solution.py:76
  74.4 2.1 convolution_convert_fusion.7
  76.9 28.6 %all-gather.8.cloned.1.call-done = bf16[768,768]{0,1:T(8,128)(2,1)} async-done(((bf16[768,192]{0,1:T(8,128)(2,1)}), bf16[768,768]{0,1:T(8,128)(2,1)}) %all-gather.8.cloned.1.call-update) | async-done | bytes 1179664 | tf_op jit(solution)/shard_map/all_gather | solution.py:76
  105.5 2.3 add_convert_fusion.2
  109.0 1.1 fusion.73
  110.7 1.0 copy-done.9
  112.4 24.2 %all-gather.14.cloned.1.call-done = bf16[768,768]{1,0:T(8,128)(2,1)} async-done(((bf16[192,768]{1,0:T(8,128)(2,1)}), bf16[768,768]{1,0:T(8,128)(2,1)}) %all-gather.14.cloned.1.call-update) | async-done | bytes 1179664 | tf_op jit(solution)/shard_map/all_gather | solution.py:76
  136.6 2.4 fusion.74
  139.4 87.2 %all-gather.16.cloned.1.call-done = bf16[768,3072]{1,0:T(8,128)(2,1)} async-done(((bf16[768,768]{1,0:T(8,128)(2,1)}), bf16[768,3072]{1,0:T(8,128)(2,1)}) %all-gather.16.cloned.1.call-update) | async-done | bytes 4718608 | tf_op jit(solution)/shard_map/all_gather | solution.py:76
  226.5 7.1 fusion.67
  233.6 82.2 %all-gather.18.cloned.1.call-done = bf16[3072,768]{1,0:T(8,128)(2,1)} async-done(((bf16[768,768]{1,0:T(8,128)(2,1)}), bf16[3072,768]{1,0:T(8,128)(2,1)}) %all-gather.18.cloned.1.call-update) | async-done | bytes 4718608 | tf_op jit(solution)/shard_map/all_gather | solution.py:76
  315.8 7.8 %fusion.75 = (f32[512]{0:T(512)S(1)}, f32[512,768]{1,0:T(8,128)S(1)}) fusion(f32[768]{0:T(1024)S(1)} %copy-done.42, bf16[3072,768]{1,0:T(8,128)(2,1)} %all-gather.18.cloned.1.call-done, f32[512,3072]{1,0:T(8,128)} %fusion.67, f32[3072]{0:T(1024)S(1)} %bitcast.95, f32[768]{0:T(1024)S(1)} %copy-done.43, f32[768]{0:T(1024)S(1)} %copy-done.29, ...), kind=kOutput, calls=%fused_computation.122 | convolution fusion | flops 2434399744 | bytes 14183424 | tf_op jit(solution)/shard_map/dot_general | solution.py:13
  325.6 1.5 fusion.69
  327.1 6.7 convert_reduce_fusion
  333.9 3.1 multiply_reduce_fusion.1
  338.2 1.8 convolution_convert_fusion.2
  340.0 2.1 convolution_convert_fusion.6
  342.6 3.2 convert_reduce_fusion.2
  346.5 0.9 copy-done.12
  347.4 1.8 fusion.21
  349.3 3.0 multiply_reduce_fusion
  352.3 1.0 multiply_convert_fusion.1
  354.7 0.9 copy-done.18
  355.6 1.8 fusion.19
  357.7 2.4 fusion.26
  360.7 0.9 copy-done.20
  361.6 1.9 fusion.20
  363.6 6.5 convolution_convert_fusion.1
  370.2 1.3 copy-done.15
  371.5 8.8 %convolution_convert_fusion = bf16[3072,768]{1,0:T(8,128)(2,1)} fusion(f32[512,768]{1,0:T(8,128)S(1)} %copy-done.15, f32[512,3072]{1,0:T(8,128)} %fusion.67, f32[3072]{0:T(1024)S(1)} %bitcast.97), kind=kOutput, calls=%fused_computation.12 | convolution fusion | flops 2434400256 | bytes 12595200 | tf_op jit(solution)/shard_map/dot_general | solution.py:17
  380.4 17.6 %reduce-scatter.11.cloned.1.call-done = bf16[768,192]{0,1:T(8,128)(2,1)} async-done(((bf16[768,768]{0,1:T(8,128)(2,1)}), bf16[768,192]{0,1:T(8,128)(2,1)}) %reduce-scatter.11.cloned.1.call-update) | async-done | bytes 294928 | tf_op jit(solution)/shard_map/reduce_scatter | solution.py:145
  398.0 30.8 %reduce-scatter.7.cloned.1.call-done = bf16[768,192]{0,1:T(8,128)(2,1)} async-done(((bf16[768,768]{0,1:T(8,128)(2,1)}), bf16[768,192]{0,1:T(8,128)(2,1)}) %reduce-scatter.7.cloned.1.call-update) | async-done | bytes 294928 | tf_op jit(solution)/shard_map/reduce_scatter | solution.py:145
  428.8 30.1 %reduce-scatter.9.cloned.1.call-done = bf16[768,192]{0,1:T(8,128)(2,1)} async-done(((bf16[768,768]{0,1:T(8,128)(2,1)}), bf16[768,192]{0,1:T(8,128)(2,1)}) %reduce-scatter.9.cloned.1.call-update) | async-done | bytes 294928 | tf_op jit(solution)/shard_map/reduce_scatter | solution.py:145
  458.9 86.3 %reduce-scatter.15.cloned.1.call-done = bf16[768,768]{1,0:T(8,128)(2,1)} async-done(((bf16[768,3072]{1,0:T(8,128)(2,1)}), bf16[768,768]{1,0:T(8,128)(2,1)}) %reduce-scatter.15.cloned.1.call-update) | async-done | bytes 1179664 | tf_op jit(solution)/shard_map/reduce_scatter | solution.py:145
  545.2 88.0 %reduce-scatter.17.cloned.1.call-done = bf16[768,768]{1,0:T(8,128)(2,1)} async-done(((bf16[3072,768]{1,0:T(8,128)(2,1)}), bf16[768,768]{1,0:T(8,128)(2,1)}) %reduce-scatter.17.cloned.1.call-update) | async-done | bytes 1179664 | tf_op jit(solution)/shard_map/reduce_scatter | solution.py:145
  634.7 18.2 %all-reduce.7 = (f32[768]{0:T(1024)S(1)}, f32[768]{0:T(1024)S(1)}, f32[3072]{0:T(1024)S(1)}) all-reduce(f32[768]{0:T(1024)S(1)} %reduce_sum.186, f32[768]{0:T(1024)S(1)} %reduce_sum.188, f32[3072]{0:T(1024)S(1)} %get-tuple-element.65), channel_id=3, replica_groups=mesh['dp'=8,'mp'=4] {'mp'}, use_global_device_ids=true, to_apply=%region_14.15.clone | all-reduce | flops 4608 | bytes 36864
  653.1 13.3 %all-reduce.6 = (f32[192]{0:T(256)}, f32[192]{0:T(256)}, f32[768]{0:T(1024)}) all-reduce(f32[192]{0:T(256)S(1)} %dynamic-slice.3, f32[192]{0:T(256)S(1)} %dynamic-slice.5, f32[768]{0:T(1024)S(1)} %dynamic-slice.7), channel_id=1, replica_groups=mesh['dp'=8,'mp'=4] {'dp'}, use_global_device_ids=true, to_apply=%region_15.16 | all-reduce | flops 1152 | bytes 9216 | tf_op jit(solution)/shard_map/psum | solution.py:159
  666.4 38.3 %all-reduce.5 = (f32[768]{0:T(1024)}, f32[768]{0:T(1024)}, f32[768]{0:T(1024)}, f32[768]{0:T(1024)}, f32[768]{0:T(1024)}, /*index=5*/f32[768]{0:T(1024)}) all-reduce(f32[768]{0:T(1024)S(1)} %get-tuple-element.47, f32[768]{0:T(1024)S(1)} %get-tuple-element.17, ...), channel_id=1, replica_groups=mesh['dp'=8,'mp'=4] {'dp','mp'}, use_global_device_ids=true, to_apply=%region_26.27 | all-reduce | flops 4608 | bytes 36864 | tf_op jit(solution)/shard_map/psum | solution.py:163
  704.6 2.2 fusion.33
  708.5 2.1 add_add_fusion
  710.5 3.6 all-reduce.12.cloned.1.call-done
  714.2 2.9 convert_element_type.158
  717.1 1.6 convert_element_type.161
  718.7 0.9 convert_element_type.146
  (162 shorter events, 20.2 us)
Async XLA Ops:
  7.2 33.4 %copy-start = (s32[2048]{0:T(1024)S(1)}, s32[2048]{0:T(1024)}, u32[]{:S(2)}) copy-start(s32[2048]{0:T(1024)} %param.19) | copy-start | bytes 24580
  7.2 35.5 %all-gather.10.cloned.1.call-start = ((), (), s32[]{:S(2)}) async-start(), calls=%async_computation.7 | async-start | bytes 1474560 | tf_op jit(solution)/shard_map/all_gather | solution.py:76
  7.9 3.3 copy-start.30
  8.0 3.4 copy-start.32
  8.0 66.4 %all-gather.12.cloned.1.call-start = ((), (), s32[]{:S(2)}) async-start(), calls=%async_computation.8 | async-start | bytes 1474560 | tf_op jit(solution)/shard_map/all_gather | solution.py:76
  8.7 3.9 copy-start.33
  8.7 4.1 copy-start.34
  8.7 34.0 %copy-start.37 = (bf16[512,768]{1,0:T(8,128)(2,1)S(1)}, bf16[512,768]{1,0:T(8,128)(2,1)}, u32[]{:S(2)}) copy-start(bf16[512,768]{1,0:T(8,128)(2,1)} %param.18) | copy-start | bytes 2359300
  8.7 96.8 %all-gather.8.cloned.1.call-start = ((), (), s32[]{:S(2)}) async-start(), calls=%async_computation.6 | async-start | bytes 1474560 | tf_op jit(solution)/shard_map/all_gather | solution.py:76
  9.5 127.1 %all-gather.14.cloned.1.call-start = ((), (), s32[]{:S(2)}) async-start(), calls=%async_computation.9 | async-start | bytes 1474560 | tf_op jit(solution)/shard_map/all_gather | solution.py:76
  10.1 216.5 %all-gather.16.cloned.1.call-start = ((), (), s32[]{:S(2)}) async-start(), calls=%async_computation.10 | async-start | bytes 5898240 | tf_op jit(solution)/shard_map/all_gather | solution.py:76
  10.6 305.2 %all-gather.18.cloned.1.call-start = ((), (), s32[]{:S(2)}) async-start(), calls=%async_computation.11 | async-start | bytes 5898240 | tf_op jit(solution)/shard_map/all_gather | solution.py:76
  11.2 369.2 %reduce-scatter.13.cloned.1.call-start = ((), (), s32[]{:S(2)}) async-start(), calls=%async_computation.15 | async-start | bytes 1474560 | tf_op jit(solution)/shard_map/reduce_scatter | solution.py:145
  45.3 63.1 %copy-start.2 = (bf16[4,128,12,64]{1,0,3,2:T(4,128)(2,1)}, bf16[4,128,12,64]{1,0,3,2:T(4,128)(2,1)S(1)}, u32[]{:S(2)}) copy-start(bf16[4,128,12,64]{1,0,3,2:T(4,128)(2,1)S(1)} %reshape.116) | copy-start | bytes 2359300
  76.9 31.4 %copy-start.3 = (bf16[4,128,12,64]{1,0,3,2:T(4,128)(2,1)}, bf16[4,128,12,64]{1,0,3,2:T(4,128)(2,1)S(1)}, u32[]{:S(2)}) copy-start(bf16[4,128,12,64]{1,0,3,2:T(4,128)(2,1)S(1)} %reshape.117) | copy-start | bytes 2359300
  108.4 1.8 copy-start.22
  110.1 1.7 copy-start.9
  111.8 24.8 %copy-start.41 = (f32[768]{0:T(1024)S(1)}, f32[768]{0:T(1024)}, u32[]{:S(2)}) copy-start(f32[768]{0:T(1024)} %param.26) | copy-start | bytes 9220
  112.4 26.6 %copy-start.7 = (bf16[4,128,12,64]{1,0,3,2:T(4,128)(2,1)}, bf16[4,128,12,64]{1,0,3,2:T(4,128)(2,1)S(1)}, u32[]{:S(2)}) copy-start(bf16[4,128,12,64]{1,0,3,2:T(4,128)(2,1)S(1)} %copy.74) | copy-start | bytes 2359300
  139.0 198.0 %copy-start.5 = (f32[512,768]{1,0:T(8,128)}, f32[512,768]{1,0:T(8,128)S(1)}, u32[]{:S(2)}) copy-start(f32[512,768]{1,0:T(8,128)S(1)} %get-tuple-element.55) | copy-start | bytes 4718596
  139.0 87.5 %copy-start.29 = (f32[768]{0:T(1024)S(1)}, f32[768]{0:T(1024)}, u32[]{:S(2)}) copy-start(f32[768]{0:T(1024)} %param.27) | copy-start | bytes 9220
  139.0 87.5 %copy-start.43 = (f32[768]{0:T(1024)S(1)}, f32[768]{0:T(1024)}, u32[]{:S(2)}) copy-start(f32[768]{0:T(1024)} %param.28) | copy-start | bytes 9220
  139.4 176.5 %copy-start.42 = (f32[768]{0:T(1024)S(1)}, f32[768]{0:T(1024)}, u32[]{:S(2)}) copy-start(f32[768]{0:T(1024)} %param.32) | copy-start | bytes 9220
  315.8 11.3 %copy-start.44 = (f32[512,3072]{1,0:T(8,128)S(1)}, f32[512,3072]{1,0:T(8,128)}, u32[]{:S(2)}) copy-start(f32[512,3072]{1,0:T(8,128)} %fusion.67) | copy-start | bytes 18874372
  324.0 1.6 copy-start.31
  324.8 2.4 copy-start.35
  325.6 8.3 %slice-start = ((s8[4718592]{0:T(1024)(128)(4,1)}), s8[4194304]{0:T(1024)(128)(4,1)S(1)}, s32[]{:S(2)}) async-start(s8[4718592]{0:T(1024)(128)(4,1)} %bitcast.98), calls=%async_computation.19 | async-start | bytes 8388608
  327.1 6.8 copy-start.14
  327.1 6.8 slice-start.1
  333.9 3.1 copy-start.45
  340.0 58.0 %reduce-scatter.11.cloned.1.call-start = ((), (), s32[]{:S(2)}) async-start(), calls=%async_computation.14 | async-start | bytes 1474560 | tf_op jit(solution)/shard_map/reduce_scatter | solution.py:145
  347.4 1.9 copy-start.23
  349.2 79.6 %reduce-scatter.7.cloned.1.call-start = ((), (), s32[]{:S(2)}) async-start(), calls=%async_computation.12 | async-start | bytes 1474560 | tf_op jit(solution)/shard_map/reduce_scatter | solution.py:145
  349.2 3.0 copy-start.10
  357.4 101.5 %reduce-scatter.9.cloned.1.call-start = ((), (), s32[]{:S(2)}) async-start(), calls=%async_computation.13 | async-start | bytes 1474560 | tf_op jit(solution)/shard_map/reduce_scatter | solution.py:145
  361.6 2.0 copy-start.6
  363.5 181.7 %reduce-scatter.15.cloned.1.call-start = ((), (), s32[]{:S(2)}) async-start(), calls=%async_computation.16 | async-start | bytes 5898240 | tf_op jit(solution)/shard_map/reduce_scatter | solution.py:145
  370.2 263.0 %reduce-scatter.17.cloned.1.call-start = ((), (), s32[]{:S(2)}) async-start(), calls=%async_computation.17 | async-start | bytes 5898240 | tf_op jit(solution)/shard_map/reduce_scatter | solution.py:145
  380.4 333.8 %all-reduce.12.cloned.1.call-start = ((), (), s32[]{:S(2)}) async-start(), calls=%async_computation.18 | async-start | bytes 7077888 | tf_op jit(solution)/shard_map/psum | solution.py:148
  633.2 71.4 %copy-start.19 = (bf16[4,128,12,64]{1,0,3,2:T(4,128)(2,1)S(1)}, bf16[4,128,12,64]{1,0,3,2:T(4,128)(2,1)}, u32[]{:S(2)}) copy-start(bf16[4,128,12,64]{1,0,3,2:T(4,128)(2,1)} %copy-done.18) | copy-start | bytes 2359300
  704.6 2.2 copy-start.21
  704.6 2.3 copy-start.36
  714.2 2.9 copy-start.16
  717.1 1.6 copy-start.27
  717.1 2.4 copy-start.26
  718.7 1.7 copy-start.25
  718.7 2.6 copy-start.24
  718.7 3.4 copy-start.1
  (13 other events, 15.9 us)
Sparse Core Ops, SparseCore 0:
  9.6 33.0 all-gather.9
  44.3 30.0 all-gather.11
  76.0 29.5 all-gather.7
  107.0 29.5 all-gather.13
  138.0 88.5 all-gather.15
  228.0 87.8 all-gather.17
  340.1 27.5 reduce-scatter.12
  370.1 27.8 reduce-scatter.10
  400.9 27.8 reduce-scatter.6
  431.0 27.8 reduce-scatter.8
  461.2 83.9 reduce-scatter.14
  547.4 85.7 reduce-scatter.16
  637.2 76.9 all-reduce.11

commit v2 on v1

v2 whole, which is shorter than its diff:
```python
import functools

import jax
import jax.numpy as jnp
from jax import lax
from jax.experimental import pallas as pl
from jax.experimental.pallas import tpu as pltpu
from jax.sharding import PartitionSpec as P

HD = 64
BLOCK = 128
TILE = 256
ROWS = 64
PLANE = 8
MASKED = -1000000000.0
MESH = pl.DeviceIdType.MESH
F32 = jnp.float32
LOW = jnp.bfloat16


def dot(left, right):
    return jnp.dot(left, right, preferred_element_type=F32)


def dot_nt(left, right):
    return lax.dot_general(left, right, (((1,), (1,)), ((), ())), preferred_element_type=F32)


def mean(value):
    return jnp.mean(value, axis=-1, keepdims=True)


def total(value):
    return jnp.sum(value, axis=0, keepdims=True)


def at(start, size, unit):
    return pl.ds(pl.multiple_of(start, unit), size)


def loop(count, body, unroll=1):
    def step(index, carry):
        body(index)
        return carry

    lax.fori_loop(0, count, step, 0, unroll=unroll)


class Links:
    def __init__(self, send, recv):
        self.send, self.recv = send, recv
        self.names = {}
        self.open = []

    def index(self, name):
        return self.names.setdefault(name, len(self.names))

    def copy(self, name, src, dst, device):
        k = self.index(name)
        return pltpu.make_async_remote_copy(
            src_ref=src,
            dst_ref=dst,
            send_sem=self.send.at[k],
            recv_sem=self.recv.at[k],
            device_id=device,
            device_id_type=MESH,
        )

    def start(self, name, src, dst, device):
        copy = self.copy(name, src, dst, device)
        copy.start()
        self.open.append(copy)

    def wait(self, name, dst, device):
        self.copy(name, dst, dst, device).wait_recv()

    def drain(self):
        for copy in self.open:
            copy.wait_send()
        self.open = []


def layer_kernel(
    n_mp,
    tok,
    cot,
    seg,
    w_query,
    w_key,
    w_value,
    b_query,
    b_value,
    b_up,
    b_out,
    gain_one,
    shift_one,
    b_down,
    gain_two,
    shift_two,
    w_out,
    w_up,
    w_down,
    out,
    grad_tok,
    grad_w,
    grad_small,
    w,
    half_in,
    quarter_in,
    eighth_in,
    plane_in,
    qkv,
    grad_qkv_t,
    prob,
    ctx,
    ctx_t,
    unit_one,
    inv_one,
    normed,
    normed_t,
    acc,
    grad_low,
    act,
    act_t,
    slope,
    up_tmp,
    mask,
    bias_in,
    qkv_bias,
    up_bias,
    small,
    small_in,
    small_up,
    small_plane,
    local_sem,
    send_sem,
    recv_sem,
):
    rows, d = tok.shape
    group = n_mp * d
    shard = d // n_mp
    piece = d // 16
    tiles = d // TILE
    pairs = d // BLOCK
    blocks = rows // BLOCK

    dp, me = lax.axis_index("dp"), lax.axis_index("mp")
    c, x, y = dp % 2, dp // 2 % 2, dp // 4 % 2
    core = (dp + 1 - 2 * c, me)
    x_side = (dp + 2 - 4 * x, me)
    y_side = (dp + 4 - 8 * y, me)

    def plane(step):
        return (me + step) % n_mp

    def rows_of(start, size):
        return at(start, size, 16)

    local = [
        pltpu.make_async_copy(w_out, w.at[rows_of(3 * d + me * shard, shard)], local_sem.at[0]),
        pltpu.make_async_copy(w_up, w.at[rows_of(group + me * d, d)], local_sem.at[1]),
        pltpu.make_async_copy(w_down, w.at[rows_of(2 * group + me * d, d)], local_sem.at[2]),
    ]
    for copy in local:
        copy.start()

    barrier = pltpu.get_barrier_semaphore()
    partners = [core, x_side, y_side] + [(dp, plane(s)) for s in range(1, n_mp)]
    for partner in partners:
        pl.semaphore_signal(barrier, inc=1, device_id=partner, device_id_type=MESH)

    for kind, ref in enumerate((w_query, w_key, w_value)):
        w[rows_of(kind * d + me * shard, shard), :] = ref[...].T

    pad = jnp.zeros((1, d - shard), F32)
    for k, ref in enumerate((b_query, b_value)):
        placed = jnp.broadcast_to(jnp.concatenate([ref[...], pad], axis=1), (8, d))
        bias_in[me, k : k + 1, :] = pltpu.roll(placed, me * shard, 1)[0:1, :]
    bias_in[me, 2:3, :] = b_up[...]

    pl.semaphore_wait(barrier, len(partners))
    for copy in local:
        copy.wait()

    links = Links(send_sem, recv_sem)

    def region(g, m, core_of, side):
        if g == 0:
            return (2 * core_of + side) * d + m * shard
        return g * group + m * d + core_of * (d // 2) + side * (d // 4)

    class Gather:
        def __init__(self, name, ref, mine, theirs):
            self.name, self.ref = name, ref
            self.mine, self.theirs = mine, theirs

        def at(self, start, size):
            return self.ref.at[rows_of(start, size)]

        def one(self):
            a = self.at(self.mine[0] + (2 * x + y) * piece, piece)
            b = self.at(self.mine[1] + (2 * y + x) * piece, piece)
            links.start((self.name, 1, 0), a, a, y_side)
            links.start((self.name, 1, 1), b, b, x_side)

        def two(self):
            links.wait(
                (self.name, 1, 0), self.at(self.mine[0] + (2 * x + 1 - y) * piece, piece), y_side
            )
            a = self.at(self.mine[0] + 2 * x * piece, 2 * piece)
            links.start((self.name, 2, 0), a, a, x_side)
            links.wait(
                (self.name, 1, 1), self.at(self.mine[1] + (2 * y + 1 - x) * piece, piece), x_side
            )
            b = self.at(self.mine[1] + 2 * y * piece, 2 * piece)
            links.start((self.name, 2, 1), b, b, y_side)

        def three(self):
            links.wait(
                (self.name, 2, 0), self.at(self.mine[0] + 2 * (1 - x) * piece, 2 * piece), x_side
            )
            a = self.at(self.mine[0], 4 * piece)
            links.start((self.name, 3, 0), a, a, core)
            links.wait(
                (self.name, 2, 1), self.at(self.mine[1] + 2 * (1 - y) * piece, 2 * piece), y_side
            )
            b = self.at(self.mine[1], 4 * piece)
            links.start((self.name, 3, 1), b, b, core)

        def done(self):
            for side in range(2):
                links.wait((self.name, 3, side), self.at(self.theirs[side], 4 * piece), core)

    for s in range(1, n_mp):
        links.start(("bias", s), bias_in.at[me], bias_in.at[me], (dp, plane(s)))
    for g in range(3):
        for s in range(1, n_mp):
            a = w.at[rows_of(region(g, me, c, 0) + (2 * x + y) * piece, piece)]
            b = w.at[rows_of(region(g, me, c, 1) + (2 * y + x) * piece, piece)]
            links.start(("w", g, s, 0), a, a, (dp, plane(s)))
            links.start(("w", g, s, 1), b, b, (dp, plane(s)))

    gathers = {}
    for g in range(3):
        for s in range(1, n_mp):
            m = plane(n_mp - s)
            gathers[g, s] = Gather(
                ("in", g, s),
                w,
                [region(g, m, c, side) for side in range(2)],
                [region(g, m, 1 - c, side) for side in range(2)],
            )

    def arrive(g, s):
        m = plane(n_mp - s)
        from_plane = (dp, m)
        a = w.at[rows_of(region(g, m, c, 0) + (2 * x + y) * piece, piece)]
        b = w.at[rows_of(region(g, m, c, 1) + (2 * y + x) * piece, piece)]
        links.wait(("w", g, s, 0), a, from_plane)
        links.wait(("w", g, s, 1), b, from_plane)
        gathers[g, s].one()

    keys = list(gathers)
    ticks = []
    for t in range(len(keys) + 3):
        step = []
        if t < len(keys):
            step.append(functools.partial(arrive, *keys[t]))
        if 0 <= t - 1 < len(keys):
            step.append(gathers[keys[t - 1]].two)
        if 0 <= t - 2 < len(keys):
            step.append(gathers[keys[t - 2]].three)
        if 0 <= t - 3 < len(keys):
            step.append(gathers[keys[t - 3]].done)
        ticks.append(step)

    def tick(count):
        for _ in range(count):
            for action in ticks.pop(0):
                action()

    for b in range(blocks):
        line = seg[pl.ds(me * blocks + b, 1), :]
        across = jnp.broadcast_to(line, (BLOCK, BLOCK))
        mask[b] = jnp.where(across == across.T, 0.0, MASKED)

    tick(3)
    bias_all = jnp.zeros((8, d), F32)
    for s in range(1, n_mp):
        m = plane(n_mp - s)
        links.wait(("bias", s), bias_in.at[m], (dp, m))
    row_b = jnp.zeros((2, d), F32)
    for m in range(n_mp):
        row_b = row_b + bias_in[m, 0:2, :]
    for t in range(tiles):
        columns = slice(t * TILE, (t + 1) * TILE)
        qkv_bias[t] = row_b[0:1, columns]
        qkv_bias[tiles + t] = jnp.zeros((1, TILE), F32)
        qkv_bias[2 * tiles + t] = row_b[1:2, columns]
        for m in range(n_mp):
            up_bias[m * tiles + t] = bias_in[m, 2:3, columns]
    tick(3)

    def project(n):
        part = dot_nt(tok[...], w[at(n * TILE, TILE, TILE), :]) + qkv_bias[n]
        qkv[2 * n] = part[:, :BLOCK].astype(LOW)
        qkv[2 * n + 1] = part[:, BLOCK:].astype(LOW)

    loop(3 * tiles, project)

    lane = lax.broadcasted_iota(jnp.int32, (1, BLOCK), 1)
    first = jnp.where(lane < HD, 1.0, 0.0).astype(LOW)
    second = jnp.where(lane < HD, 0.0, 1.0).astype(LOW)

    def two_heads(value):
        return jnp.concatenate([value * first, value * second], axis=0)

    def softmax(score):
        expo = jnp.exp(score - jnp.max(score, axis=-1, keepdims=True))
        return expo / jnp.sum(expo, axis=-1, keepdims=True)

    def attend(index):
        b, p = index // pairs, index % pairs
        here = at(b * BLOCK, BLOCK, BLOCK)
        query = qkv[p, here, :]
        key = qkv[pairs + p, here, :]
        value = qkv[2 * pairs + p, here, :]
        score = dot_nt(query, two_heads(key)) * HD**-0.5
        hidden = mask[b]
        both = jnp.concatenate(
            [softmax(score[:, :BLOCK] + hidden), softmax(score[:, BLOCK:] + hidden)], axis=1
        ).astype(LOW)
        prob[index] = both
        context = dot(both, two_heads(value)).astype(LOW)
        ctx[here, at(p * BLOCK, BLOCK, BLOCK)] = context
        ctx_t[at(p * BLOCK, BLOCK, BLOCK), here] = context.T

    for _ in range(3):
        base = _ * (blocks * pairs // 3)
        loop(blocks * pairs // 3, lambda i, base=base: attend(base + i), unroll=2)
        tick(1)

    def attn_out(n):
        columns = at(n * TILE, TILE, TILE)
        acc[:, columns] = dot(ctx[...], w[3 * d : 4 * d, columns])

    loop(tiles, attn_out)

    def norm_one(r):
        here = at(r * ROWS, ROWS, ROWS)
        value = tok[here, :].astype(F32) + acc[here, :] + b_out[...]
        center = value - mean(value)
        inverse = lax.rsqrt(mean(center * center) + 1e-05)
        unit = center * inverse
        unit_one[here, :] = unit
        inv_one[here, :] = jnp.broadcast_to(inverse, (ROWS, BLOCK))
        normed[here, :] = (unit * gain_one[...] + shift_one[...]).astype(LOW)

    loop(rows // ROWS, norm_one)

    def turn(r):
        here = at(r * BLOCK, BLOCK, BLOCK)
        normed_t[:, here] = normed[here, :].T

    loop(blocks, turn)

    def feed_up(m):
        def one(n):
            t = m * tiles + n
            weight = w[rows_of(group + m * d, d), at(n * TILE, TILE, TILE)]
            up_tmp[...] = dot(normed[...], weight) + up_bias[t]

            def gelu(r):
                here = at(r * ROWS, ROWS, ROWS)
                u = up_tmp[here, :]
                square = u * u
                inner = jnp.tanh(0.7978845608028654 * (u + 0.044715 * (square * u)))
                cdf = 0.5 + 0.5 * inner
                act[t, here, :] = (u * cdf).astype(LOW)
                slope_in = 0.7978845608028654 + (3 * 0.044715 * 0.7978845608028654) * square
                slope[t, here, :] = (cdf + 0.5 * u * (1.0 - inner * inner) * slope_in).astype(LOW)

            loop(rows // ROWS, gelu)
            for k in range(TILE // BLOCK):
                act_t[t, k * BLOCK : (k + 1) * BLOCK, :] = act[
                    t, :, k * BLOCK : (k + 1) * BLOCK
                ].T

        loop(tiles, one)

    def columns_of(m):
        return jnp.concatenate([act[m * tiles + t] for t in range(tiles)], axis=1)

    def feed_down(m, opening):
        whole = columns_of(m)

        def one(n):
            columns = at(n * TILE, TILE, TILE)
            part = dot(whole, w[rows_of(2 * group + m * d, d), columns])
            acc[:, columns] = part if opening else acc[:, columns] + part

        loop(tiles, one)

    feed_up(me)
    for s in range(1, n_mp):
        if len(ticks) > 3:
            tick(1)
        feed_up(plane(n_mp - s))
    feed_down(me, True)
    for s in range(1, n_mp):
        while len(ticks) > n_mp - 1 - s:
            tick(1)
        feed_down(plane(n_mp - s), False)
    links.drain()

    small[...] = jnp.zeros(small.shape, F32)

    def add_small(row, value):
        small[0, row : row + 1, :] = small[0, row : row + 1, :] + value

    def norm_two(r):
        here = at(r * ROWS, ROWS, ROWS)
        unit = unit_one[here, :]
        value = unit * gain_one[...] + shift_one[...] + acc[here, :] + b_down[...]
        center = value - mean(value)
        inverse = lax.rsqrt(mean(center * center) + 1e-05)
        unit = center * inverse
        out[here, :] = (unit * gain_two[...] + shift_two[...]).astype(LOW)
        grad = cot[here, :].astype(F32)
        scaled = grad * gain_two[...]
        grad_resid = inverse * (scaled - mean(scaled) - unit * mean(scaled * unit))
        acc[here, :] = grad_resid
        grad_low[here, :] = grad_resid.astype(LOW)
        add_small(5, total(grad_resid))
        add_small(6, total(grad * unit))
        add_small(7, total(grad))

    loop(rows // ROWS, norm_two)

    def block_of(g, s):
        return g * n_mp + s

    def add_rows(start, source, offset, size):
        def one(k):
            here = rows_of(start + k * 16, 16)
            there = rows_of(offset + k * 16, 16)
            w[here, :] = (w[here, :].astype(F32) + source[there, :].astype(F32)).astype(LOW)

        loop(size // 16, one)

    def halve(g, s):
        m, k = plane(s), block_of(g, s)
        for side in range(2):
            links.start(
                ("half", k, side),
                w.at[rows_of(region(g, m, 1 - c, side), 4 * piece)],
                half_in.at[k, side],
                core,
            )

    def quarter(g, s):
        m, k = plane(s), block_of(g, s)
        for side, (bit, device) in enumerate(((x, x_side), (y, y_side))):
            start = region(g, m, c, side)
            links.wait(("half", k, side), half_in.at[k, side], core)
            other = 2 * (1 - bit) * piece
            add_rows(start + other, half_in.at[k, side], other, 2 * piece)
            links.start(
                ("quarter", k, side),
                w.at[rows_of(start + other, 2 * piece)],
                quarter_in.at[k, side],
                device,
            )
        for side, bit in enumerate((x, y)):
            start = region(g, m, c, side)
            own = 2 * bit * piece
            add_rows(start + own, half_in.at[k, side], own, 2 * piece)

    def eighth(g, s):
        m, k = plane(s), block_of(g, s)
        sides = ((x, y, x_side, y_side), (y, x, y_side, x_side))
        for side, (high, bit, before, device) in enumerate(sides):
            start = region(g, m, c, side) + 2 * high * piece
            links.wait(("quarter", k, side), quarter_in.at[k, side], before)
            other = (1 - bit) * piece
            add_rows(start + other, quarter_in.at[k, side], other, piece)
            links.start(
                ("eighth", k, side),
                w.at[rows_of(start + other, piece)],
                eighth_in.at[k, side],
                device,
            )
        for side, (high, bit, before, device) in enumerate(sides):
            start = region(g, m, c, side) + 2 * high * piece
            own = bit * piece
            add_rows(start + own, quarter_in.at[k, side], own, piece)

    def to_plane(g, s):
        m, k = plane(s), block_of(g, s)
        for side, (first_bit, bit, device) in enumerate(((x, y, y_side), (y, x, x_side))):
            start = region(g, m, c, side) + (2 * first_bit + bit) * piece
            links.wait(("eighth", k, side), eighth_in.at[k, side], device)
            add_rows(start, eighth_in.at[k, side], 0, piece)
            if s:
                links.start(
                    ("plane", g, s, side),
                    w.at[rows_of(start, piece)],
                    plane_in.at[g, s - 1, side],
                    (dp, m),
                )

    outs = [
        Gather(
            ("out", g),
            grad_w.at[g],
            [c * (d // 2) + side * (d // 4) for side in range(2)],
            [(1 - c) * (d // 2) + side * (d // 4) for side in range(2)],
        )
        for g in range(3)
    ]

    def finish(g):
        for side, (first_bit, bit) in enumerate(((x, y), (y, x))):
            start = region(g, me, c, side) + (2 * first_bit + bit) * piece
            goal = c * (d // 2) + side * (d // 4) + (2 * first_bit + bit) * piece
            for s in range(1, n_mp):
                links.wait(
                    ("plane", g, s, side), plane_in.at[g, s - 1, side], (dp, plane(n_mp - s))
                )

            def one(k):
                value = w[rows_of(start + k * 16, 16), :].astype(F32)
                for s in range(1, n_mp):
                    value = value + plane_in[g, s - 1, side, rows_of(k * 16, 16), :].astype(F32)
                grad_w[g, rows_of(goal + k * 16, 16), :] = value.astype(LOW)

            loop(piece // 16, one)
        outs[g].one()

    order = [s for s in range(1, n_mp)] + [0]
    queue = []

    def advance(count):
        for _ in range(min(count, len(queue))):
            queue.pop(0)()

    def down_back(m):
        def one(n):
            t = m * tiles + n
            here = rows_of(2 * group + t * TILE, TILE)
            grad = grad_low[...]
            grad_up = (dot_nt(grad, w[here, :]) * slope[t].astype(F32)).astype(LOW)
            act[t] = grad_up
            small_up[t] = total(grad_up.astype(F32))
            w[here, :] = dot(act_t[t], grad).astype(LOW)

        loop(tiles, one)

    def up_back(m):
        whole = columns_of(m)

        def one(n):
            here = rows_of(group + m * d + n * TILE, TILE)
            columns = at(n * TILE, TILE, TILE)
            acc[:, columns] = acc[:, columns] + dot_nt(whole, w[here, :])
            w[here, :] = dot(normed_t[columns, :], whole).astype(LOW)

        loop(tiles, one)

    for s in order:
        down_back(plane(s))
        halve(2, s)
        advance(1)
        queue.append(functools.partial(quarter, 2, s))
    for k, s in enumerate(order):
        up_back(plane(s))
        halve(1, s)
        advance(1)
        queue.append(functools.partial(quarter, 1, s))
    queue.extend(functools.partial(eighth, 2, s) for s in order)
    queue.extend(functools.partial(to_plane, 2, s) for s in order)

    def norm_one_back(r):
        here = at(r * ROWS, ROWS, ROWS)
        grad = acc[here, :]
        unit = unit_one[here, :]
        scaled = grad * gain_one[...]
        inverse = inv_one[here, 0:1]
        grad_resid = inverse * (scaled - mean(scaled) - unit * mean(scaled * unit))
        grad_tok[here, :] = grad_resid
        grad_low[here, :] = grad_resid.astype(LOW)
        add_small(2, total(grad_resid))
        add_small(3, total(grad * unit))
        add_small(4, total(grad))

    loop(rows // ROWS, norm_one_back)
    advance(1)

    def out_back(n):
        here = rows_of(3 * d + n * TILE, TILE)
        columns = at(n * TILE, TILE, TILE)
        grad = grad_low[...]
        ctx[:, columns] = dot_nt(grad, w[here, :]).astype(LOW)
        w[here, :] = dot(ctx_t[columns, :], grad).astype(LOW)

    loop(tiles, out_back)
    advance(1)

    def attend_back(index):
        b, p = index // pairs, index % pairs
        here = at(b * BLOCK, BLOCK, BLOCK)
        query = qkv[p, here, :]
        key = qkv[pairs + p, here, :]
        value = qkv[2 * pairs + p, here, :]
        grad = ctx[here, at(p * BLOCK, BLOCK, BLOCK)]
        both = prob[index]
        grad_prob = dot_nt(grad, two_heads(value))
        wide = both.astype(F32)

        def score_back(columns):
            part, grad_part = wide[:, columns], grad_prob[:, columns]
            return part * (grad_part - jnp.sum(part * grad_part, axis=-1, keepdims=True))

        low_score = jnp.concatenate(
            [score_back(slice(0, BLOCK)), score_back(slice(BLOCK, 2 * BLOCK))], axis=1
        ).astype(LOW)

        def turned(pair):
            return jnp.concatenate([pair[:, :BLOCK].T, pair[:, BLOCK:].T], axis=1)

        grads = (
            (dot(low_score, two_heads(key)) * HD**-0.5).astype(LOW),
            (dot(turned(low_score), two_heads(query)) * HD**-0.5).astype(LOW),
            dot(turned(both), two_heads(grad)).astype(LOW),
        )
        for kind, value in enumerate(grads):
            qkv[kind * pairs + p, here, :] = value
            grad_qkv_t[at((kind * pairs + p) * BLOCK, BLOCK, BLOCK), here] = value.T

    parts = 6
    for k in range(parts):
        base = k * (blocks * pairs // parts)
        loop(blocks * pairs // parts, lambda i, base=base: attend_back(base + i), unroll=2)
        advance(2)

    for k in range(pairs):
        columns = slice(k * BLOCK, (k + 1) * BLOCK)
        small[0, 0:1, columns] = total(qkv[k].astype(F32))
        small[0, 1:2, columns] = total(qkv[2 * pairs + k].astype(F32))
    for m in range(n_mp):
        for n in range(tiles):
            small[0, 8 + m : 9 + m, n * TILE : (n + 1) * TILE] = small_up[m * tiles + n]
    links.start(("small", 0), small.at[0], small_in.at[0], core)

    def token_back(kind):
        whole = jnp.concatenate([qkv[kind * pairs + k] for k in range(pairs)], axis=1)

        def one(n):
            columns = at(n * TILE, TILE, TILE)
            grad_tok[:, columns] = grad_tok[:, columns] + dot(
                whole, w[kind * d : (kind + 1) * d, columns]
            )

        loop(tiles, one)

        def weight(n):
            here = rows_of(kind * d + n * TILE, TILE)
            w[here, :] = dot(grad_qkv_t[here, :], tok[...]).astype(LOW)

        loop(tiles, weight)

    for kind in range(3):
        token_back(kind)
        advance(1)
    for s in order:
        halve(0, s)
    queue.extend(functools.partial(quarter, 0, s) for s in order)
    advance(len(queue))

    for k, (before, device) in enumerate(((core, x_side), (x_side, y_side), (y_side, None))):
        links.wait(("small", k), small_in.at[k], before)
        if device is None:
            small_plane[me] = small[k] + small_in[k]
        else:
            small[k + 1] = small[k] + small_in[k]
            links.start(("small", k + 1), small.at[k + 1], small_in.at[k + 1], device)
    for s in range(1, n_mp):
        links.start(("small plane", s), small_plane.at[me], small_plane.at[me], (dp, plane(s)))

    for s in order:
        eighth(1, s)
    for s in order:
        to_plane(1, s)
    for s in order:
        eighth(0, s)
    finish(2)
    outs[2].two()
    for s in order:
        to_plane(0, s)
    finish(1)
    outs[1].two()
    outs[2].three()
    finish(0)
    outs[0].two()
    outs[1].three()
    outs[0].three()

    for s in range(1, n_mp):
        m = plane(n_mp - s)
        links.wait(("small plane", s), small_plane.at[m], (dp, m))
    value = small_plane[0]
    for m in range(1, n_mp):
        value = value + small_plane[m]
    grad_small[...] = value
    ups = value[8:16, :]
    own = total(jnp.where(lax.broadcasted_iota(jnp.int32, ups.shape, 0) == me, ups, 0.0))
    grad_small[8:9, :] = own
    turned = pltpu.roll(value[0:8, :], (n_mp - me) % n_mp * shard, 1)
    grad_small[0:2, :] = turned[0:2, :]

    for gather in outs:
        gather.done()
    links.drain()


def run_kernel(n_mp, tokens, cotangent, segments, weights, vectors, big):
    rows, d = tokens.shape
    vmem = pl.BlockSpec(memory_space=pltpu.VMEM)
    blocks = rows // BLOCK
    pairs = d // BLOCK
    tiles = d // TILE
    ff_tiles = n_mp * tiles
    piece = d // 16
    low = lambda *shape: pltpu.VMEM(shape, LOW)
    full = lambda *shape: pltpu.VMEM(shape, F32)
    block_count = 3 * n_mp
    names = 512
    flops = 2 * rows * d * d * 12 * 3
    return pl.pallas_call(
        functools.partial(layer_kernel, n_mp),
        out_shape=(
            jax.ShapeDtypeStruct((rows, d), LOW),
            jax.ShapeDtypeStruct((rows, d), F32),
            jax.ShapeDtypeStruct((3, d, d), LOW),
            jax.ShapeDtypeStruct((16, d), F32),
        ),
        in_specs=[vmem] * (3 + len(weights) + len(vectors))
        + [pl.BlockSpec(memory_space=pl.ANY)] * len(big),
        out_specs=(vmem,) * 4,
        scratch_shapes=[
            low(3 * n_mp * d, d),
            low(block_count, 2, 4 * piece, d),
            low(block_count, 2, 2 * piece, d),
            low(block_count, 2, piece, d),
            low(3, n_mp - 1, 2, piece, d),
            low(3 * pairs, rows, BLOCK),
            low(3 * d, rows),
            low(blocks * pairs, BLOCK, 2 * BLOCK),
            low(rows, d),
            low(d, rows),
            full(rows, d),
            full(rows, BLOCK),
            low(rows, d),
            low(d, rows),
            full(rows, d),
            low(rows, d),
            low(ff_tiles, rows, TILE),
            low(ff_tiles, TILE, rows),
            low(ff_tiles, rows, TILE),
            full(rows, TILE),
            full(blocks, BLOCK, BLOCK),
            full(n_mp, 8, d),
            full(3 * tiles, 1, TILE),
            full(ff_tiles, 1, TILE),
            full(3, 16, d),
            full(3, 16, d),
            full(ff_tiles, 1, TILE),
            full(n_mp, 16, d),
            pltpu.SemaphoreType.DMA((3,)),
            pltpu.SemaphoreType.DMA((names,)),
            pltpu.SemaphoreType.DMA((names,)),
        ],
        compiler_params=pltpu.CompilerParams(
            collective_id=0, has_side_effects=True, vmem_limit_bytes=63 << 20
        ),
        cost_estimate=pl.CostEstimate(flops=flops, bytes_accessed=1 << 24, transcendentals=1 << 21),
    )(tokens, cotangent, segments, *weights, *vectors, *big)


def per_device(
    n_dp,
    n_mp,
    tokens,
    segment_ids,
    w_query,
    b_query,
    w_key,
    w_value,
    b_value,
    w_out,
    b_out,
    gain_one,
    shift_one,
    w_up,
    b_up,
    w_down,
    b_down,
    gain_two,
    shift_two,
    cotangent,
):
    d = tokens.shape[1]
    shard = d // n_mp
    vectors = (b_query, b_value, b_up, b_out, gain_one, shift_one, b_down, gain_two, shift_two)
    out, grad_tokens, grad_w, small = run_kernel(
        n_mp,
        tokens,
        cotangent,
        segment_ids.reshape(-1, BLOCK),
        (w_query, w_key, w_value),
        tuple(v.reshape(1, -1) for v in vectors),
        (w_out, w_up, w_down),
    )
    grad_w = grad_w.astype(F32)
    if n_dp > PLANE:
        groups = [[k + PLANE * h for h in range(n_dp // PLANE)] for k in range(PLANE)]
        grad_w, small = lax.psum((grad_w, small), "dp", axis_index_groups=groups)
    return (
        out,
        grad_tokens,
        grad_w[0, :shard].T,
        small[0, :shard],
        grad_w[0, shard : 2 * shard].T,
        grad_w[0, 2 * shard : 3 * shard].T,
        small[1, :shard],
        grad_w[0, 3 * shard :],
        small[2],
        small[3],
        small[4],
        grad_w[1],
        small[8],
        grad_w[2],
        small[5],
        small[6],
        small[7],
    )


def solution(mesh):
    n_dp, n_mp = mesh.shape["dp"], mesh.shape["mp"]
    return jax.shard_map(
        functools.partial(per_device, n_dp, n_mp),
        mesh=mesh,
        in_specs=(
            P(("dp", "mp"), None),
            P("dp"),
            P(None, "mp"),
            P("mp"),
            P(None, "mp"),
            P(None, "mp"),
            P("mp"),
            P("mp", None),
            P(),
            P(),
            P(),
            P(None, "mp"),
            P("mp"),
            P("mp", None),
            P(),
            P(),
            P(),
            P(("dp", "mp"), None),
        ),
        out_specs=(
            P(("dp", "mp"), None),
            P(("dp", "mp"), None),
            P(None, "mp"),
            P("mp"),
            P(None, "mp"),
            P(None, "mp"),
            P("mp"),
            P("mp", None),
            P(),
            P(),
            P(),
            P(None, "mp"),
            P("mp"),
            P("mp", None),
            P(),
            P(),
            P(),
        ),
        check_vma=False,
    )
```

time: 734 us -> 241 us (0.33)
  waiting for transfers between devices: 513 us -> 0 us
  Pallas kernels: 0 us -> 212 us
  blocking collectives: 97.2 us -> 0 us
  matrix products: 73.8 us -> 0 us
  between operations: 17.1 us -> 0.68 us
  other arithmetic: 13.6 us -> 2.6 us
  local copies, waits for them, and re-layouts: 13.3 us -> 24.2 us
    all_gather x6 -> x0, waiting for transfers between devices: 253 us -> none  [whole(): return lax.all_gather(array, 'mp', axis=axis, tiled=True)]
    reduce_scatter x6 -> x0, waiting for transfers between devices: 253 us -> none  [share(): lax.psum_scatter(array.astype(low), 'mp', scatter_dimension=axis, tiled=T...]
    pallas_call x0 -> x1, Pallas kernels: none -> 212 us  [run_kernel(): pl.pallas_call(functools.partial(layer_kernel, n_mp), out_shape=(jax.Shap...]
    dot_general x24 -> x0, matrix products: 73.8 us -> none  [the longest x6 23.7 us: matmul(): return jnp.dot(left, right, preferred_element_type=jnp.float32)]
    psum x2 -> x0, blocking collectives: 51.5 us -> none  [the longest x1 38.3 us: per_device(): lax.psum((grad_b_out, grad_gain_one, grad_shift_one, grad_b_down, grad_ga...]
    unnamed x2 -> x0, blocking collectives: 32.3 us -> none
    all_gather x1 -> x0, blocking collectives: 13.4 us -> none  [whole(): return lax.all_gather(array, 'mp', axis=axis, tiled=True)]
    reshape x4 -> x7, local copies, waits for them, and re-layouts: 0.73 us -> 8.87 us  [per_device(): v.reshape(1, -1)]
  transfers between devices with their start and end apart: 13 -> 0, of which waited for: 12 -> 0; matrix products, arithmetic and copies ran while one was open for 9% -> 0% of each run, Pallas kernels for 0% -> 0%
where the time goes in v2:
time: 241 us; the launch traced here: 239 us
  Pallas kernels  212 us (88%)
  local copies, waits for them, and re-layouts  24.2 us (10%)
  other arithmetic  2.6 us (1%)
    pallas_call x1, Pallas kernels, run_kernel(): pl.pallas_call(functools.partial(layer_kernel, n_mp), out_shape=(jax.Shap...  212 us
    reshape x7, local copies, waits for them, and re-layouts, per_device(): v.reshape(1, -1)  8.87 us
    unnamed x9, local copies, waits for them, and re-layouts  8.47 us

profile of v2, /device:TPU:0, one launch (start us, length us, event | category | flops | bytes accessed | tf_op | source)
XLA Modules:
  0.0 239.3 jit_solution(13998586302656074909)
XLA Ops:
  0.7 1.3 reshape.68.b_out
  1.9 1.3 reshape.69.gain_one
  3.2 1.3 reshape.70.shift_one
  4.5 1.3 reshape.67.b_up
  5.7 1.3 reshape.71.b_down
  7.0 1.3 reshape.72.gain_two
  8.3 1.3 reshape.73.shift_two
  9.5 1.9 copy.35.w_query
  11.4 1.9 copy.36.w_key
  13.3 1.9 copy.37.w_value
  15.2 211.8 %shard_map.305 = (bf16[512,768]{1,0:T(8,128)(2,1)}, f32[512,768]{1,0:T(8,128)}, bf16[3,768,768]{2,1,0:T(8,128)(2,1)}, f32[16,768]{1,0:T(8,128)}) custom-call(bf16[512,768]{1,0:T(8,128)(2,1)} %tok.1, bf16[512,768]{1,0:T(8,128)(2,1)} %cot.1, s32[16,128]{1,0:T(8,128)} %bitcast.25, bf16[768,192]{1,0:T(8,128)(2,1)} %copy.35.w_query, ...), custom_call_target="tpu_custom_call" | custom-call | flops 21743271936 | bytes 16777216 | tf_op jit(solution)/shard_map/pallas_call | solution.py:739
  227.0 1.3 fusion
  228.3 1.6 slice_reduce_fusion
  229.9 2.6 %convert_element_type.3 = f32[3,768,768]{2,1,0:T(8,128)S(1)} convert(bf16[3,768,768]{2,1,0:T(8,128)(2,1)} %get-tuple-element.23) | non-fusion elementwise | flops 1769472 | bytes 10616832 | tf_op jit(solution)/shard_map/convert_element_type | solution.py:824
  232.5 1.4 slice_bitcast_fusion.2
  234.0 0.0 copy-start.1
  234.0 2.5 %slice_bitcast_fusion = (f32[768,768]{1,0:T(8,128)}, f32[768,768]{1,0:T(8,128)}) fusion(f32[3,768,768]{2,1,0:T(8,128)S(1)} %convert_element_type.3), kind=kLoop, calls=%fused_computation | loop fusion | bytes 9437184 | tf_op jit(solution)/shard_map/squeeze | solution.py:842
  236.5 0.0 copy-start
  236.5 0.0 copy-done.1
  236.5 0.9 copy.40
  237.3 0.8 copy-done
  238.2 1.1 copy.41
Async XLA Ops:
  234.0 2.5 %copy-start.1 = (bf16[512,768]{1,0:T(8,128)(2,1)S(1)}, bf16[512,768]{1,0:T(8,128)(2,1)}, u32[]{:S(2)}) copy-start(bf16[512,768]{1,0:T(8,128)(2,1)} %get-tuple-element.57) | copy-start | bytes 2359300
  236.5 1.7 copy-start

commit v3 on v2

--- a/solution.py
+++ b/solution.py
@@ -82,60 +82,69 @@
 
 def layer_kernel(
     n_mp,
-    tok,
-    cot,
-    seg,
+    tok_in,
+    cot_in,
+    seg_in,
     w_query,
     w_key,
     w_value,
-    b_query,
-    b_value,
-    b_up,
-    b_out,
-    gain_one,
-    shift_one,
-    b_down,
-    gain_two,
-    shift_two,
     w_out,
     w_up,
     w_down,
-    out,
-    grad_tok,
-    grad_w,
-    grad_small,
-    w,
-    half_in,
-    quarter_in,
-    eighth_in,
-    plane_in,
-    qkv,
-    grad_qkv_t,
-    prob,
-    ctx,
-    ctx_t,
-    unit_one,
-    inv_one,
-    normed,
-    normed_t,
-    acc,
-    grad_low,
-    act,
-    act_t,
-    slope,
-    up_tmp,
-    mask,
-    bias_in,
-    qkv_bias,
-    up_bias,
-    small,
-    small_in,
-    small_up,
-    small_plane,
-    local_sem,
-    send_sem,
-    recv_sem,
+    b_query_in,
+    b_value_in,
+    *refs,
 ):
+    vectors_in, refs = refs[:7], refs[7:]
+    (
+        out_to,
+        grad_tok_to,
+        grad_w_to,
+        grad_small_to,
+        tok,
+        cot,
+        seg,
+        b_query,
+        b_value,
+        vectors,
+        lines,
+        out,
+        grad_tok,
+        grad_w,
+        grad_small,
+        w,
+        half_in,
+        quarter_in,
+        eighth_in,
+        plane_in,
+        qkv,
+        grad_qkv_t,
+        prob,
+        ctx,
+        ctx_t,
+        unit_one,
+        inv_one,
+        normed,
+        normed_t,
+        acc,
+        grad_low,
+        act,
+        act_t,
+        slope,
+        up_tmp,
+        mask,
+        bias_in,
+        qkv_bias,
+        up_bias,
+        small,
+        small_in,
+        small_up,
+        small_plane,
+        local_sem,
+        send_sem,
+        recv_sem,
+    ) = refs
+    b_up, b_out, gain_one, shift_one, b_down, gain_two, shift_two = [lines.at[k] for k in range(7)]
     rows, d = tok.shape
     group = n_mp * d
     shard = d // n_mp
@@ -156,31 +165,44 @@
     def rows_of(start, size):
         return at(start, size, 16)
 
-    local = [
-        pltpu.make_async_copy(w_out, w.at[rows_of(3 * d + me * shard, shard)], local_sem.at[0]),
-        pltpu.make_async_copy(w_up, w.at[rows_of(group + me * d, d)], local_sem.at[1]),
-        pltpu.make_async_copy(w_down, w.at[rows_of(2 * group + me * d, d)], local_sem.at[2]),
+    count = 0
+
+    def fetch(src, dst):
+        nonlocal count
+        copy = pltpu.make_async_copy(src, dst, local_sem.at[count])
+        count += 1
+        copy.start()
+        return copy
+
+    own_w = [
+        fetch(ref, w.at[rows_of(kind * d + me * shard, shard)])
+        for kind, ref in enumerate((w_query, w_key, w_value, w_out))
     ]
-    for copy in local:
-        copy.start()
+    own_b = [fetch(b_query_in, b_query), fetch(b_value_in, b_value)]
+    own_b += [fetch(ref, vectors.at[k]) for k, ref in enumerate(vectors_in)]
+    own_w.append(fetch(w_up, w.at[rows_of(group + me * d, d)]))
+    own_w.append(fetch(w_down, w.at[rows_of(2 * group + me * d, d)]))
+    own_rows = [fetch(seg_in, seg), fetch(tok_in, tok), fetch(cot_in, cot)]
 
     barrier = pltpu.get_barrier_semaphore()
     partners = [core, x_side, y_side] + [(dp, plane(s)) for s in range(1, n_mp)]
     for partner in partners:
         pl.semaphore_signal(barrier, inc=1, device_id=partner, device_id_type=MESH)
 
-    for kind, ref in enumerate((w_query, w_key, w_value)):
-        w[rows_of(kind * d + me * shard, shard), :] = ref[...].T
-
+    for copy in own_b:
+        copy.wait()
+    for k in range(len(vectors_in)):
+        parts = [vectors[k, j : j + 1, :] for j in range(d // BLOCK)]
+        lines[k] = jnp.concatenate(parts, axis=1)
     pad = jnp.zeros((1, d - shard), F32)
     for k, ref in enumerate((b_query, b_value)):
         placed = jnp.broadcast_to(jnp.concatenate([ref[...], pad], axis=1), (8, d))
         bias_in[me, k : k + 1, :] = pltpu.roll(placed, me * shard, 1)[0:1, :]
     bias_in[me, 2:3, :] = b_up[...]
 
+    for copy in own_w:
+        copy.wait()
     pl.semaphore_wait(barrier, len(partners))
-    for copy in local:
-        copy.wait()
 
     links = Links(send_sem, recv_sem)
 
@@ -278,6 +300,9 @@
         for _ in range(count):
             for action in ticks.pop(0):
                 action()
+
+    for copy in own_rows:
+        copy.wait()
 
     for b in range(blocks):
         line = seg[pl.ds(me * blocks + b, 1), :]
@@ -436,6 +461,7 @@
         add_small(7, total(grad))
 
     loop(rows // ROWS, norm_two)
+    leaving = [fetch(out, out_to)]
 
     def block_of(g, s):
         return g * n_mp + s
@@ -672,6 +698,7 @@
     for kind in range(3):
         token_back(kind)
         advance(1)
+    leaving.append(fetch(grad_tok, grad_tok_to))
     for s in order:
         halve(0, s)
     queue.extend(functools.partial(quarter, 0, s) for s in order)
@@ -718,14 +745,18 @@
     turned = pltpu.roll(value[0:8, :], (n_mp - me) % n_mp * shard, 1)
     grad_small[0:2, :] = turned[0:2, :]
 
-    for gather in outs:
-        gather.done()
+    leaving.append(fetch(grad_small, grad_small_to))
+    for g in (2, 1, 0):
+        outs[g].done()
+        leaving.append(fetch(grad_w.at[g], grad_w_to.at[g]))
     links.drain()
-
-
-def run_kernel(n_mp, tokens, cotangent, segments, weights, vectors, big):
+    for copy in leaving:
+        copy.wait()
+
+
+def run_kernel(n_mp, tokens, cotangent, segments, weights, shards, vectors):
     rows, d = tokens.shape
-    vmem = pl.BlockSpec(memory_space=pltpu.VMEM)
+    anywhere = pl.BlockSpec(memory_space=pl.ANY)
     blocks = rows // BLOCK
     pairs = d // BLOCK
     tiles = d // TILE
@@ -734,8 +765,9 @@
     low = lambda *shape: pltpu.VMEM(shape, LOW)
     full = lambda *shape: pltpu.VMEM(shape, F32)
     block_count = 3 * n_mp
-    names = 512
+    names = 256
     flops = 2 * rows * d * d * 12 * 3
+    operands = (tokens, cotangent, segments, *weights, *shards, *vectors)
     return pl.pallas_call(
         functools.partial(layer_kernel, n_mp),
         out_shape=(
@@ -744,10 +776,20 @@
             jax.ShapeDtypeStruct((3, d, d), LOW),
             jax.ShapeDtypeStruct((16, d), F32),
         ),
-        in_specs=[vmem] * (3 + len(weights) + len(vectors))
-        + [pl.BlockSpec(memory_space=pl.ANY)] * len(big),
-        out_specs=(vmem,) * 4,
+        in_specs=[anywhere] * len(operands),
+        out_specs=(anywhere,) * 4,
         scratch_shapes=[
+            low(rows, d),
+            low(rows, d),
+            pltpu.VMEM(segments.shape, jnp.int32),
+            full(*shards[0].shape),
+            full(*shards[1].shape),
+            full(len(vectors), *vectors[0].shape),
+            full(len(vectors), 1, d),
+            low(rows, d),
+            full(rows, d),
+            low(3, d, d),
+            full(16, d),
             low(3 * n_mp * d, d),
             low(block_count, 2, 4 * piece, d),
             low(block_count, 2, 2 * piece, d),
@@ -776,7 +818,7 @@
             full(3, 16, d),
             full(ff_tiles, 1, TILE),
             full(n_mp, 16, d),
-            pltpu.SemaphoreType.DMA((3,)),
+            pltpu.SemaphoreType.DMA((32,)),
             pltpu.SemaphoreType.DMA((names,)),
             pltpu.SemaphoreType.DMA((names,)),
         ],
@@ -784,7 +826,107 @@
             collective_id=0, has_side_effects=True, vmem_limit_bytes=63 << 20
         ),
         cost_estimate=pl.CostEstimate(flops=flops, bytes_accessed=1 << 24, transcendentals=1 << 21),
-    )(tokens, cotangent, segments, *weights, *vectors, *big)
+    )(*operands)
+
+
+def finish_kernel(
+    out,
+    grad_tok,
+    grad_w,
+    small,
+    out_to,
+    grad_tok_to,
+    query_to,
+    key_to,
+    value_to,
+    attn_to,
+    up_to,
+    down_to,
+    b_query_to,
+    b_value_to,
+    *refs,
+
+):
+    vectors_to, refs = refs[:7], refs[7:]
+    held, wide, lines, parts, vectors, low_rows, full_rows, sems = refs
+    d = held.shape[-1]
+    shard = query_to.shape[0]
+    pieces = d // shard
+    count = 0
+
+    def fetch(src, dst):
+        nonlocal count
+        copy = pltpu.make_async_copy(src, dst, sems.at[count])
+        count += 1
+        copy.start()
+        return copy
+
+    first = fetch(small, lines)
+    loads = {}
+    for g in range(3):
+        for k in range(pieces):
+            here = pl.ds(k * shard, shard)
+            loads[g, k] = fetch(grad_w.at[g, here], held.at[g, here])
+    passing = [fetch(out, low_rows), fetch(grad_tok, full_rows)]
+    first.wait()
+    for k in range(2):
+        parts[k] = lines[k : k + 1, :shard]
+    for k in range(vectors.shape[0]):
+        for j in range(d // BLOCK):
+            vectors[k, j : j + 1, :] = lines[2 + k : 3 + k, j * BLOCK : (j + 1) * BLOCK]
+    stores = [fetch(parts.at[0], b_query_to), fetch(parts.at[1], b_value_to)]
+    stores += [fetch(vectors.at[k], ref) for k, ref in enumerate(vectors_to)]
+    for g in range(3):
+        for k in range(pieces):
+            loads[g, k].wait()
+
+            def widen(r, g=g, k=k):
+                here = at(k * shard + r * 16, 16, 16)
+                wide[g, here, :] = held[g, here, :].astype(F32)
+
+            loop(shard // 16, widen, unroll=2)
+            here = pl.ds(k * shard, shard)
+            if g == 0:
+                stores.append(fetch(wide.at[0, here], (query_to, key_to, value_to, attn_to)[k]))
+            else:
+                stores.append(fetch(wide.at[g, here], (up_to, down_to)[g - 1].at[here]))
+        if g == 0:
+            for copy in passing:
+                copy.wait()
+            stores += [fetch(low_rows, out_to), fetch(full_rows, grad_tok_to)]
+    for copy in stores:
+        copy.wait()
+
+
+def run_finish(shard, out, grad_tok, grad_w, small):
+    d = out.shape[1]
+    anywhere = pl.BlockSpec(memory_space=pl.ANY)
+    full = lambda *shape: jax.ShapeDtypeStruct(shape, F32)
+    shapes = (
+        [jax.ShapeDtypeStruct(out.shape, LOW), full(*grad_tok.shape)]
+        + [full(shard, d)] * 4
+        + [full(d, d)] * 2
+        + [full(1, shard)] * 2
+        + [full(d // BLOCK, BLOCK)] * 7
+    )
+    return pl.pallas_call(
+        finish_kernel,
+        out_shape=tuple(shapes),
+        in_specs=[anywhere] * 4,
+        out_specs=(anywhere,) * len(shapes),
+        scratch_shapes=[
+            pltpu.VMEM(grad_w.shape, grad_w.dtype),
+            pltpu.VMEM(grad_w.shape, F32),
+            pltpu.VMEM(small.shape, F32),
+            pltpu.VMEM((2, 1, shard), F32),
+            pltpu.VMEM((7, d // BLOCK, BLOCK), F32),
+            pltpu.VMEM(out.shape, LOW),
+            pltpu.VMEM(grad_tok.shape, F32),
+            pltpu.SemaphoreType.DMA((64,)),
+        ],
+        compiler_params=pltpu.CompilerParams(vmem_limit_bytes=60 << 20),
+        cost_estimate=pl.CostEstimate(flops=0, bytes_accessed=1 << 24, transcendentals=0),
+    )(out, grad_tok, grad_w, small)
 
 
 def per_device(
@@ -811,38 +953,55 @@
 ):
     d = tokens.shape[1]
     shard = d // n_mp
-    vectors = (b_query, b_value, b_up, b_out, gain_one, shift_one, b_down, gain_two, shift_two)
+    vectors = (b_up, b_out, gain_one, shift_one, b_down, gain_two, shift_two)
     out, grad_tokens, grad_w, small = run_kernel(
         n_mp,
         tokens,
         cotangent,
         segment_ids.reshape(-1, BLOCK),
-        (w_query, w_key, w_value),
-        tuple(v.reshape(1, -1) for v in vectors),
-        (w_out, w_up, w_down),
+        (w_query.T, w_key.T, w_value.T, w_out, w_up, w_down),
+        (b_query.reshape(1, -1), b_value.reshape(1, -1)),
+        tuple(v.reshape(-1, BLOCK) for v in vectors),
     )
-    grad_w = grad_w.astype(F32)
     if n_dp > PLANE:
         groups = [[k + PLANE * h for h in range(n_dp // PLANE)] for k in range(PLANE)]
-        grad_w, small = lax.psum((grad_w, small), "dp", axis_index_groups=groups)
+        grad_w, small = lax.psum(
+            (grad_w.astype(F32), small), "dp", axis_index_groups=groups
+        )
+    (
+        out,
+        grad_tokens,
+        grad_w_query,
+        grad_w_key,
+        grad_w_value,
+        grad_w_out,
+        grad_w_up,
+        grad_w_down,
+        grad_b_query,
+        grad_b_value,
+        *grad_vectors,
+    ) = run_finish(shard, out, grad_tokens, grad_w, small)
+    grad_b_out, grad_gain_one, grad_shift_one, grad_b_down, grad_gain_two, grad_shift_two = [
+        grad_vectors[k].reshape(-1) for k in range(6)
+    ]
     return (
         out,
         grad_tokens,
-        grad_w[0, :shard].T,
-        small[0, :shard],
-        grad_w[0, shard : 2 * shard].T,
-        grad_w[0, 2 * shard : 3 * shard].T,
-        small[1, :shard],
-        grad_w[0, 3 * shard :],
-        small[2],
-        small[3],
-        small[4],
-        grad_w[1],
-        small[8],
-        grad_w[2],
-        small[5],
-        small[6],
-        small[7],
+        grad_w_query.T,
+        grad_b_query.reshape(-1),
+        grad_w_key.T,
+        grad_w_value.T,
+        grad_b_value.reshape(-1),
+        grad_w_out,
+        grad_b_out,
+        grad_gain_one,
+        grad_shift_one,
+        grad_w_up,
+        grad_vectors[6].reshape(-1),
+        grad_w_down,
+        grad_b_down,
+        grad_gain_two,
+        grad_shift_two,
     )
 
 

time: 241 us -> 213 us (0.88)
  local copies, waits for them, and re-layouts: 24.2 us -> 0 us
  other arithmetic: 2.6 us -> 0 us
    reshape x7 -> x0, local copies, waits for them, and re-layouts: 8.87 us -> none  [per_device(): v.reshape(1, -1)]
    unnamed x9 -> x0, local copies, waits for them, and re-layouts: 8.47 us -> none
    pallas_call x1, Pallas kernels: 212 us -> 204 us  [run_kernel(): pl.pallas_call(functools.partial(layer_kernel, n_mp), out_shape=(jax.Shap...]
    pallas_call x0 -> x1, Pallas kernels: none -> 7.09 us  [run_finish(): pl.pallas_call(finish_kernel, out_shape=tuple(shapes), in_specs=[anywhere...]
    squeeze x2 -> x0, local copies, waits for them, and re-layouts: 3.92 us -> none  [the longest x1 2.48 us: per_device(): grad_w[2]]
    slice x2 -> x0, local copies, waits for them, and re-layouts: 2.98 us -> none  [the longest x1 1.63 us: per_device(): small[7]]
    convert_element_type x1 -> x0, other arithmetic: 2.6 us -> none  [per_device(): grad_w = grad_w.astype(F32)]
where the time goes in v3:
time: 213 us; the launch traced here: 212 us
  Pallas kernels  211 us (99%)
    pallas_call x1, Pallas kernels, run_kernel(): pl.pallas_call(functools.partial(layer_kernel, n_mp), out_shape=(jax.Shap...  204 us
    pallas_call x1, Pallas kernels, run_finish(): pl.pallas_call(finish_kernel, out_shape=tuple(shapes), in_specs=[anywhere...  7.09 us

profile of v3, /device:TPU:0, one launch (start us, length us, event | category | flops | bytes accessed | tf_op | source)
XLA Modules:
  0.0 211.7 jit_solution(14434250380940272047)
XLA Ops:
  0.7 203.8 %shard_map.305 = (bf16[512,768]{1,0:T(8,128)(2,1)}, f32[512,768]{1,0:T(8,128)}, bf16[3,768,768]{2,1,0:T(8,128)(2,1)}, f32[16,768]{1,0:T(8,128)}) custom-call(bf16[512,768]{1,0:T(8,128)(2,1)} %tok_in.1, bf16[512,768]{1,0:T(8,128)(2,1)} %cot_in.1, s32[16,128]{1,0:T(8,128)} %bitcast.31, bf16[192,768]{1,0:T(8,128)(2,1)} %bitcast.28, bf16[192,768]{1,0:T(8,128)(2,1)} %bitcast.29, ...), custom_call_target="tpu_custom_call" | custom-call | flops 21743271936 | bytes 16777216 | tf_op jit(solution)/shard_map/pallas_call | solution.py:771
  204.4 7.1 %shard_map.306 = (bf16[512,768]{1,0:T(8,128)(2,1)}, f32[512,768]{1,0:T(8,128)}, f32[192,768]{1,0:T(8,128)}, f32[192,768]{1,0:T(8,128)}, f32[192,768]{1,0:T(8,128...) custom-call(bf16[512,768]{1,0:T(8,128)(2,1)} %get-tuple-element.38.o, ...), custom_call_target="tpu_custom_call" | custom-call | bytes 16777216 | tf_op jit(solution)/shard_map/pallas_call | solution.py:912

commit v4 on v3

v4 whole, which is shorter than its diff:
```python
import functools

import jax
import jax.numpy as jnp
from jax import lax
from jax.experimental import pallas as pl
from jax.experimental.pallas import tpu as pltpu
from jax.sharding import PartitionSpec as P

HD = 64
BLOCK = 128
TILE = 256
ROWS = 64
PLANE = 8
ATTEND_PARTS = 2
ATTEND_BACK_PARTS = 6
DOUBLED = (1, 2)
GELU = 0.7978845608028654
FORWARD = (
    ("send", 0), ("masks",), ("one", 0, 0), ("send", 1), ("two", 0, 0), ("one", 0, 1),
    ("biases",), ("three", 0, 0), ("two", 0, 1), ("done", 0, 0), ("project", 0), ("one", 0, 2),
    ("attend", 0, 0), ("attend", 0, 1), ("three", 0, 1), ("two", 0, 2), ("done", 0, 1),
    ("two", 1, 0), ("send", 2), ("three", 0, 2), ("one", 1, 1), ("done", 0, 2), ("project", 1),
    ("three", 1, 0), ("one", 1, 2), ("attend", 1, 0), ("two", 1, 1), ("attend", 1, 1),
    ("done", 1, 0), ("two", 1, 2), ("attn_out",), ("norm_one",), ("three", 1, 1), ("two", 2, 0),
    ("up", 3), ("up", 0), ("done", 1, 1), ("three", 1, 2), ("one", 2, 1), ("up", 1),
    ("three", 2, 0), ("one", 2, 2), ("done", 1, 2), ("up", 2), ("two", 2, 1), ("down", 3),
    ("done", 2, 0), ("two", 2, 2), ("down", 0), ("three", 2, 1), ("done", 2, 1), ("down", 1),
    ("three", 2, 2), ("done", 2, 2), ("down", 2),
)
BACKWARD = (
    ("down", 1), ("halve", 2, 1), ("down", 0), ("halve", 2, 0), ("down", 2), ("quarter", 2, 1),
    ("halve", 2, 2), ("down", 3), ("quarter", 2, 0), ("halve", 2, 3), ("up", 1),
    ("eighth", 2, 1), ("halve", 1, 1), ("quarter", 2, 2), ("up", 0), ("halve", 1, 0), ("up", 2),
    ("plane", 2, 1), ("eighth", 2, 0), ("quarter", 1, 1), ("halve", 1, 2), ("up", 3),
    ("halve", 1, 3), ("norm",), ("eighth", 2, 2), ("plane", 2, 0), ("out",), ("quarter", 1, 0),
    ("attend", 0), ("eighth", 1, 1), ("attend", 1), ("plane", 2, 2), ("quarter", 1, 2),
    ("attend", 2), ("attend", 3), ("eighth", 1, 0), ("attend", 4), ("plane", 1, 1),
    ("quarter", 1, 3), ("attend", 5), ("small_send",), ("token",), ("small_next", 0),
    ("plane", 1, 0), ("eighth", 1, 2), ("quarter", 2, 3), ("project",), ("small_next", 1),
    ("plane", 1, 2), ("eighth", 1, 3), ("halve", 0, 1), ("halve", 0, 0), ("halve", 0, 2),
    ("halve", 0, 3), ("quarter", 0, 1), ("small_next", 2), ("eighth", 2, 3), ("quarter", 0, 0),
    ("eighth", 0, 1), ("quarter", 0, 2), ("small_done",), ("eighth", 0, 0), ("plane", 0, 1),
    ("quarter", 0, 3), ("eighth", 0, 2), ("plane", 0, 0), ("finish", 1), ("finish", 2),
    ("eighth", 0, 3), ("plane", 0, 2), ("two", 1), ("two", 2), ("three", 1), ("finish", 0),
    ("done", 1), ("three", 2), ("two", 0), ("done", 2), ("three", 0), ("done", 0),
)
MASKED = -1000000000.0
MESH = pl.DeviceIdType.MESH
F32 = jnp.float32
LOW = jnp.bfloat16


def dot(left, right):
    return jnp.dot(left, right, preferred_element_type=F32)


def dot_nt(left, right):
    return lax.dot_general(left, right, (((1,), (1,)), ((), ())), preferred_element_type=F32)


def mean(value):
    return jnp.mean(value, axis=-1, keepdims=True)


def total(value):
    return jnp.sum(value, axis=0, keepdims=True)


def at(start, size, unit):
    return pl.ds(pl.multiple_of(start, unit), size)


def loop(count, body, unroll=1):
    def step(index, carry):
        body(index)
        return carry

    lax.fori_loop(0, count, step, 0, unroll=unroll)


class Links:
    def __init__(self, send, recv):
        self.send, self.recv = send, recv
        self.names = {}
        self.used = 0
        self.open = []

    def index(self, name, width):
        if name not in self.names:
            self.names[name] = self.used
            self.used += width
        return self.names[name]

    def copy(self, name, src, dst, device, there=None, here=None):
        first = self.index(name, 1 if there is None else 4)
        going, coming = (first, first) if there is None else (first + there, first + here)
        return pltpu.make_async_remote_copy(
            src_ref=src,
            dst_ref=dst,
            send_sem=self.send.at[going],
            recv_sem=self.recv.at[coming],
            device_id=device,
            device_id_type=MESH,
        )

    def start(self, *args):
        copy = self.copy(*args)
        copy.start()
        self.open.append(copy)

    def wait(self, name, dst, device, there=None):
        self.copy(name, dst, dst, device, there, there).wait_recv()

    def drain(self):
        for copy in self.open:
            copy.wait_send()
        self.open = []


def layer_kernel(
    n_mp,
    tok_in,
    cot_in,
    seg_in,
    w_query,
    w_key,
    w_value,
    w_out,
    w_up,
    w_down,
    b_query_in,
    b_value_in,
    *refs,
):
    vectors_in, refs = refs[:7], refs[7:]
    (
        out_to,
        grad_tok_to,
        grad_w_to,
        grad_small_to,
        tok,
        cot,
        seg,
        b_query,
        b_value,
        vectors,
        lines,
        out,
        grad_tok,
        grad_w,
        grad_small,
        w,
        half_in,
        quarter_in,
        eighth_in,
        plane_in,
        qkv,
        grad_qkv_t,
        prob,
        ctx,
        ctx_t,
        unit_one,
        inv_one,
        normed,
        normed_t,
        acc,
        grad_low,
        act,
        act_t,
        slope,
        mask,
        bias_in,
        qkv_bias,
        small,
        small_in,
        small_up,
        small_plane,
        local_sem,
        send_sem,
        recv_sem,
    ) = refs
    b_up, b_out, gain_one, shift_one, b_down, gain_two, shift_two = [lines.at[k] for k in range(7)]
    rows, d = tok.shape
    group = n_mp * d
    shard = d // n_mp
    piece = d // 16
    pairs = d // BLOCK
    blocks = rows // BLOCK

    dp, me = lax.axis_index("dp"), lax.axis_index("mp")
    c, x, y = dp % 2, dp // 2 % 2, dp // 4 % 2
    core = (dp + 1 - 2 * c, me)
    x_side = (dp + 2 - 4 * x, me)
    y_side = (dp + 4 - 8 * y, me)

    ranks = (me + 1 - 2 * (me % 2), 2 - me // 2, 3 - 3 * (me // 2), me)
    others = range(n_mp - 1)

    def rows_of(start, size):
        return at(start, size, 16)

    count = 0

    def fetch(src, dst):
        nonlocal count
        copy = pltpu.make_async_copy(src, dst, local_sem.at[count])
        count += 1
        copy.start()
        return copy

    own_w = [
        fetch(ref, w.at[rows_of(kind * d + me * shard, shard)])
        for kind, ref in enumerate((w_query, w_key, w_value, w_out))
    ]
    own_b = [fetch(b_query_in, b_query), fetch(b_value_in, b_value)]
    own_b += [fetch(ref, vectors.at[k]) for k, ref in enumerate(vectors_in)]
    own_w.append(fetch(w_up, w.at[rows_of(group + me * d, d)]))
    own_w.append(fetch(w_down, w.at[rows_of(2 * group + me * d, d)]))
    own_rows = [fetch(seg_in, seg), fetch(tok_in, tok), fetch(cot_in, cot)]

    barrier = pltpu.get_barrier_semaphore()
    partners = [core, x_side, y_side] + [(dp, ranks[k]) for k in others]
    for partner in partners:
        pl.semaphore_signal(barrier, inc=1, device_id=partner, device_id_type=MESH)

    for copy in own_b:
        copy.wait()
    for k in range(len(vectors_in)):
        parts = [vectors[k, j : j + 1, :] for j in range(d // BLOCK)]
        lines[k] = jnp.concatenate(parts, axis=1)
    pad = jnp.zeros((1, d - shard), F32)
    for k, ref in enumerate((b_query, b_value)):
        placed = jnp.broadcast_to(jnp.concatenate([ref[...], pad], axis=1), (8, d))
        bias_in[me, k : k + 1, :] = pltpu.roll(placed, me * shard, 1)[0:1, :]
    bias_in[me, 2:3, :] = b_up[...]

    for copy in own_w:
        copy.wait()
    pl.semaphore_wait(barrier, len(partners))

    links = Links(send_sem, recv_sem)

    def region(g, m, core_of, side):
        if g == 0:
            return (2 * core_of + side) * d + m * shard
        return g * group + m * d + core_of * (d // 2) + side * (d // 4)

    class Gather:
        def __init__(self, name, ref, mine, theirs):
            self.name, self.ref = name, ref
            self.mine, self.theirs = mine, theirs

        def at(self, start, size):
            return self.ref.at[rows_of(start, size)]

        def one(self):
            a = self.at(self.mine[0] + (2 * x + y) * piece, piece)
            b = self.at(self.mine[1] + (2 * y + x) * piece, piece)
            links.start((self.name, 1, 0), a, a, y_side)
            links.start((self.name, 1, 1), b, b, x_side)

        def joined(self, side):
            if side == 0:
                start, device = self.mine[0] + (2 * x + 1 - y) * piece, y_side
            else:
                start, device = self.mine[1] + (2 * y + 1 - x) * piece, x_side
            links.wait((self.name, 1, side), self.at(start, piece), device)

        def two(self, joined=None):
            (joined or self.joined)(0)
            a = self.at(self.mine[0] + 2 * x * piece, 2 * piece)
            links.start((self.name, 2, 0), a, a, x_side)
            (joined or self.joined)(1)
            b = self.at(self.mine[1] + 2 * y * piece, 2 * piece)
            links.start((self.name, 2, 1), b, b, y_side)

        def three(self):
            links.wait(
                (self.name, 2, 0), self.at(self.mine[0] + 2 * (1 - x) * piece, 2 * piece), x_side
            )
            a = self.at(self.mine[0], 4 * piece)
            links.start((self.name, 3, 0), a, a, core)
            links.wait(
                (self.name, 2, 1), self.at(self.mine[1] + 2 * (1 - y) * piece, 2 * piece), y_side
            )
            b = self.at(self.mine[1], 4 * piece)
            links.start((self.name, 3, 1), b, b, core)

        def done(self):
            for side in range(2):
                links.wait((self.name, 3, side), self.at(self.theirs[side], 4 * piece), core)

    for k in others:
        m = ranks[k]
        links.start("bias", bias_in.at[me], bias_in.at[me], (dp, m), m, me)

    def share(g, k, m, side):
        start = region(g, m, c, side)
        high, bit = (x, y) if side == 0 else (y, x)
        if k == 0 and g in DOUBLED:
            return w.at[rows_of(start + 2 * high * piece, 2 * piece)]
        return w.at[rows_of(start + (2 * high + bit) * piece, piece)]

    def send(g):
        for k in others:
            for side in range(2):
                rows_in = share(g, k, me, side)
                links.start(("w", g, side), rows_in, rows_in, (dp, ranks[k]), ranks[k], me)

    gathers = {}
    for g in range(3):
        for k in others:
            m = ranks[k]
            gathers[g, k] = Gather(
                ("in", g, k),
                w,
                [region(g, m, c, side) for side in range(2)],
                [region(g, m, 1 - c, side) for side in range(2)],
            )

    def landed(g, k, side):
        m = ranks[k]
        links.wait(("w", g, side), share(g, k, m, side), (dp, m), m)

    def one(g, k):
        for side in range(2):
            landed(g, k, side)
        gathers[g, k].one()

    def two(g, k):
        whole = k == 0 and g in DOUBLED
        gathers[g, k].two(functools.partial(landed, g, k) if whole else None)

    def three(g, k):
        gathers[g, k].three()

    def done(g, k):
        gathers[g, k].done()

    def masks():
        for copy in own_rows:
            copy.wait()
        for b in range(blocks):
            line = seg[pl.ds(me * blocks + b, 1), :]
            across = jnp.broadcast_to(line, (BLOCK, BLOCK))
            mask[b] = jnp.where(across == across.T, 0.0, MASKED)

    def biases():
        for k in others:
            m = ranks[k]
            links.wait("bias", bias_in.at[m], (dp, m), m)
        row = jnp.zeros((2, d), F32)
        for m in range(n_mp):
            row = row + bias_in[m, 0:2, :]
        for h in range(2):
            columns = slice(h * (d // 2), (h + 1) * (d // 2))
            qkv_bias[h] = row[0:1, columns]
            qkv_bias[2 + h] = jnp.zeros((1, d // 2), F32)
            qkv_bias[4 + h] = row[1:2, columns]

    half_pairs = pairs // 2

    def half_of(k):
        return me // 2 if k == 0 else 1 - me // 2

    def project(k):
        half = half_of(k)

        def one_kind(kind):
            here = rows_of(kind * d + half * (d // 2), d // 2)
            part = dot_nt(tok[...], w[here, :]) + qkv_bias[2 * kind + half]
            for j in range(half_pairs):
                columns = part[:, j * BLOCK : (j + 1) * BLOCK]
                qkv[kind * pairs + half * half_pairs + j] = columns.astype(LOW)

        loop(3, one_kind)

    lane = lax.broadcasted_iota(jnp.int32, (1, BLOCK), 1)
    first = jnp.where(lane < HD, 1.0, 0.0).astype(LOW)
    second = jnp.where(lane < HD, 0.0, 1.0).astype(LOW)
    none = jnp.zeros((HD, BLOCK), LOW)

    def two_heads(value):
        return jnp.concatenate([value * first, value * second], axis=0)

    def two_heads_t(value):
        turned = value.T
        upper = jnp.concatenate([turned[:HD], none], axis=1)
        lower = jnp.concatenate([none, turned[HD:]], axis=1)
        return jnp.concatenate([upper, lower], axis=0)

    def softmax(score):
        expo = jnp.exp(score - jnp.max(score, axis=0, keepdims=True))
        return expo * (1.0 / jnp.sum(expo, axis=0, keepdims=True))

    def attend(b, p):
        here = at(b * BLOCK, BLOCK, BLOCK)
        columns = at(p * BLOCK, BLOCK, BLOCK)
        query = qkv[p, here, :]
        key = qkv[pairs + p, here, :]
        value = qkv[2 * pairs + p, here, :]
        score = dot_nt(two_heads(key), query) * HD**-0.5
        hidden = mask[b]
        both = jnp.concatenate(
            [softmax(score[:BLOCK] + hidden), softmax(score[BLOCK:] + hidden)], axis=0
        ).astype(LOW)
        prob[b * pairs + p] = both
        context = dot(two_heads_t(value), both).astype(LOW)
        ctx_t[columns, here] = context
        ctx[here, columns] = context.T

    def attend_part(k, part):
        count = blocks * half_pairs // ATTEND_PARTS

        def step(i):
            i = i + part * count
            attend(i % blocks, half_of(k) * half_pairs + i // blocks)

        loop(count, step, unroll=2)

    def attn_out():
        acc[...] = dot(ctx[...], w[3 * d : 4 * d, :])

    def norm_one():
        def step(r):
            here = at(r * ROWS, ROWS, ROWS)
            value = tok[here, :].astype(F32) + acc[here, :] + b_out[...]
            center = value - mean(value)
            inverse = lax.rsqrt(mean(center * center) + 1e-05)
            unit = center * inverse
            unit_one[here, :] = unit
            inv_one[here, :] = jnp.broadcast_to(inverse, (ROWS, BLOCK))
            normed[here, :] = (unit * gain_one[...] + shift_one[...]).astype(LOW)

        loop(rows // ROWS, step)

        def turn(r):
            here = at(r * BLOCK, BLOCK, BLOCK)
            normed_t[:, here] = normed[here, :].T

        loop(blocks, turn)

    def feed_up(k):
        m = ranks[k]
        acc[...] = dot(normed[...], w[rows_of(group + m * d, d), :]) + bias_in[m, 2:3, :]

        def gelu(r):
            here = at(r * 16, 16, 16)
            u = acc[here, :]
            square = u * u
            inner = jnp.tanh(u * (GELU + GELU * 0.044715 * square))
            cdf = 0.5 + 0.5 * inner
            act[m, here, :] = (u * cdf).astype(LOW)
            slope_in = 0.5 * GELU + (1.5 * 0.044715 * GELU) * square
            slope[m, here, :] = (cdf + u * (1.0 - inner * inner) * slope_in).astype(LOW)

        loop(rows // 16, gelu)

        def turn(r):
            here = at(r * BLOCK, BLOCK, BLOCK)
            act_t[m, :, here] = act[m, here, :].T

        loop(blocks, turn)

    def feed_down(k):
        m = ranks[k]
        part = dot(act[m], w[rows_of(2 * group + m * d, d), :])
        acc[...] = part if k == n_mp - 1 else acc[...] + part

    forward = {
        "send": send,
        "one": one,
        "two": two,
        "three": three,
        "done": done,
        "masks": masks,
        "biases": biases,
        "project": project,
        "attend": attend_part,
        "attn_out": attn_out,
        "norm_one": norm_one,
        "up": feed_up,
        "down": feed_down,
    }
    for name, *args in FORWARD:
        forward[name](*args)
    links.drain()

    small[...] = jnp.zeros(small.shape, F32)

    def add_small(row, value):
        small[0, row : row + 1, :] = small[0, row : row + 1, :] + value

    def norm_two(r):
        here = at(r * ROWS, ROWS, ROWS)
        unit = unit_one[here, :]
        value = unit * gain_one[...] + shift_one[...] + acc[here, :] + b_down[...]
        center = value - mean(value)
        inverse = lax.rsqrt(mean(center * center) + 1e-05)
        unit = center * inverse
        out[here, :] = (unit * gain_two[...] + shift_two[...]).astype(LOW)
        grad = cot[here, :].astype(F32)
        scaled = grad * gain_two[...]
        grad_resid = inverse * (scaled - mean(scaled) - unit * mean(scaled * unit))
        acc[here, :] = grad_resid
        grad_low[here, :] = grad_resid.astype(LOW)
        add_small(5, total(grad_resid))
        add_small(6, total(grad * unit))
        add_small(7, total(grad))

    loop(rows // ROWS, norm_two)
    leaving = [fetch(out, out_to)]

    def block_of(g, s):
        return g * n_mp + s

    def add_rows(start, source, offset, size):
        def one(k):
            here = rows_of(start + k * 16, 16)
            there = rows_of(offset + k * 16, 16)
            w[here, :] = (w[here, :].astype(F32) + source[there, :].astype(F32)).astype(LOW)

        loop(size // 16, one)

    def halve(g, s):
        m, k = ranks[s], block_of(g, s)
        for side in range(2):
            links.start(
                ("half", k, side),
                w.at[rows_of(region(g, m, 1 - c, side), 4 * piece)],
                half_in.at[k, side],
                core,
            )

    def quarter(g, s):
        m, k = ranks[s], block_of(g, s)
        for side, (bit, device) in enumerate(((x, x_side), (y, y_side))):
            start = region(g, m, c, side)
            links.wait(("half", k, side), half_in.at[k, side], core)
            other = 2 * (1 - bit) * piece
            add_rows(start + other, half_in.at[k, side], other, 2 * piece)
            links.start(
                ("quarter", k, side),
                w.at[rows_of(start + other, 2 * piece)],
                quarter_in.at[k, side],
                device,
            )
        for side, bit in enumerate((x, y)):
            start = region(g, m, c, side)
            own = 2 * bit * piece
            add_rows(start + own, half_in.at[k, side], own, 2 * piece)

    def eighth(g, s):
        m, k = ranks[s], block_of(g, s)
        sides = ((x, y, x_side, y_side), (y, x, y_side, x_side))
        for side, (high, bit, before, device) in enumerate(sides):
            start = region(g, m, c, side) + 2 * high * piece
            links.wait(("quarter", k, side), quarter_in.at[k, side], before)
            other = (1 - bit) * piece
            add_rows(start + other, quarter_in.at[k, side], other, piece)
            links.start(
                ("eighth", k, side),
                w.at[rows_of(start + other, piece)],
                eighth_in.at[k, side],
                device,
            )
        for side, (high, bit, before, device) in enumerate(sides):
            start = region(g, m, c, side) + 2 * high * piece
            own = bit * piece
            add_rows(start + own, quarter_in.at[k, side], own, piece)

    def to_plane(g, s):
        m, k = ranks[s], block_of(g, s)
        for side, (high, bit, device) in enumerate(((x, y, y_side), (y, x, x_side))):
            start = region(g, m, c, side) + (2 * high + bit) * piece
            links.wait(("eighth", k, side), eighth_in.at[k, side], device)
            add_rows(start, eighth_in.at[k, side], 0, piece)
            if s < n_mp - 1:
                links.start(
                    ("plane", g, side),
                    w.at[rows_of(start, piece)],
                    plane_in.at[g, me, side],
                    (dp, m),
                    m,
                    me,
                )

    outs = [
        Gather(
            ("out", g),
            grad_w.at[g],
            [c * (d // 2) + side * (d // 4) for side in range(2)],
            [(1 - c) * (d // 2) + side * (d // 4) for side in range(2)],
        )
        for g in range(3)
    ]

    def finish(g):
        to_plane(g, n_mp - 1)
        for side, (high, bit) in enumerate(((x, y), (y, x))):
            start = region(g, me, c, side) + (2 * high + bit) * piece
            goal = c * (d // 2) + side * (d // 4) + (2 * high + bit) * piece
            for k in others:
                m = ranks[k]
                links.wait(("plane", g, side), plane_in.at[g, m, side], (dp, m), m)

            def step(k):
                value = w[rows_of(start + k * 16, 16), :].astype(F32)
                for s in others:
                    value = value + plane_in[g, ranks[s], side, rows_of(k * 16, 16), :].astype(F32)
                grad_w[g, rows_of(goal + k * 16, 16), :] = value.astype(LOW)

            loop(piece // 16, step)
        outs[g].one()

    def spread(g):
        outs[g].two()

    def pair(g):
        outs[g].three()

    def leave(g):
        outs[g].done()
        leaving.append(fetch(grad_w.at[g], grad_w_to.at[g]))

    def down_back(k):
        m = ranks[k]
        here = rows_of(2 * group + m * d, d)
        small_up[m] = jnp.zeros((1, d), F32)

        def step(r):
            tile = rows_of(r * TILE, TILE)
            grad_up = dot_nt(grad_low[tile, :], w[here, :]) * slope[m, tile, :].astype(F32)
            act[m, tile, :] = grad_up.astype(LOW)
            small_up[m] = small_up[m] + total(grad_up)

        loop(rows // TILE, step)

        def weight(r):
            tile = rows_of(r * (d // 2), d // 2)
            there = rows_of(2 * group + m * d + r * (d // 2), d // 2)
            w[there, :] = dot(act_t[m, tile, :], grad_low[...]).astype(LOW)

        loop(2, weight)

    def up_back(k):
        m = ranks[k]
        here = rows_of(group + m * d, d)

        def step(r):
            tile = rows_of(r * TILE, TILE)
            acc[tile, :] = acc[tile, :] + dot_nt(act[m, tile, :], w[here, :])

        loop(rows // TILE, step)

        def weight(r):
            tile = rows_of(r * (d // 2), d // 2)
            there = rows_of(group + m * d + r * (d // 2), d // 2)
            w[there, :] = dot(normed_t[tile, :], act[m]).astype(LOW)

        loop(2, weight)

    def norm_back():
        def step(r):
            here = at(r * ROWS, ROWS, ROWS)
            grad = acc[here, :]
            unit = unit_one[here, :]
            scaled = grad * gain_one[...]
            inverse = inv_one[here, 0:1]
            grad_resid = inverse * (scaled - mean(scaled) - unit * mean(scaled * unit))
            grad_tok[here, :] = grad_resid
            grad_low[here, :] = grad_resid.astype(LOW)
            add_small(2, total(grad_resid))
            add_small(3, total(grad * unit))
            add_small(4, total(grad))

        loop(rows // ROWS, step)

    def out_back():
        def step(r):
            tile = rows_of(r * TILE, TILE)
            ctx[tile, :] = dot_nt(grad_low[tile, :], w[3 * d : 4 * d, :]).astype(LOW)

        loop(rows // TILE, step)

        def weight(r):
            tile = rows_of(r * (d // 2), d // 2)
            there = rows_of(3 * d + r * (d // 2), d // 2)
            w[there, :] = dot(ctx_t[tile, :], grad_low[...]).astype(LOW)

        loop(2, weight)

    def attend_back(index):
        b, p = index // pairs, index % pairs
        here = at(b * BLOCK, BLOCK, BLOCK)
        query = qkv[p, here, :]
        key = qkv[pairs + p, here, :]
        value = qkv[2 * pairs + p, here, :]
        grad = ctx[here, at(p * BLOCK, BLOCK, BLOCK)]
        both = prob[index]
        grad_prob = dot_nt(two_heads(value), grad)
        wide = both.astype(F32)

        def score_back(part, grad_part):
            return part * (grad_part - jnp.sum(part * grad_part, axis=0, keepdims=True))

        low_score = jnp.concatenate(
            [
                score_back(wide[:BLOCK], grad_prob[:BLOCK]),
                score_back(wide[BLOCK:], grad_prob[BLOCK:]),
            ],
            axis=0,
        ).astype(LOW)

        def beside(stack):
            return jnp.concatenate([stack[:BLOCK], stack[BLOCK:]], axis=1)

        def keep(kind, natural, turned):
            qkv[kind * pairs + p, here, :] = natural
            grad_qkv_t[at((kind * pairs + p) * BLOCK, BLOCK, BLOCK), here] = turned

        grad_query = (dot(two_heads_t(key), low_score) * HD**-0.5).astype(LOW)
        grad_key = (dot(beside(low_score), two_heads(query)) * HD**-0.5).astype(LOW)
        grad_value = dot(beside(both), two_heads(grad)).astype(LOW)
        keep(0, grad_query.T, grad_query)
        keep(1, grad_key, grad_key.T)
        keep(2, grad_value, grad_value.T)

    def attend_back_part(part):
        count = blocks * pairs // ATTEND_BACK_PARTS
        loop(count, lambda i: attend_back(part * count + i), unroll=2)

    def small_send():
        for k in range(pairs):
            columns = slice(k * BLOCK, (k + 1) * BLOCK)
            small[0, 0:1, columns] = total(qkv[k].astype(F32))
            small[0, 1:2, columns] = total(qkv[2 * pairs + k].astype(F32))
        for m in range(n_mp):
            small[0, 8 + m : 9 + m, :] = small_up[m]
        links.start(("small", 0), small.at[0], small_in.at[0], core)

    def small_next(k):
        before, device = ((core, x_side), (x_side, y_side), (y_side, None))[k]
        links.wait(("small", k), small_in.at[k], before)
        if device is None:
            small_plane[me] = small[k] + small_in[k]
            for s in others:
                m = ranks[s]
                links.start("small", small_plane.at[me], small_plane.at[me], (dp, m), m, me)
        else:
            small[k + 1] = small[k] + small_in[k]
            links.start(("small", k + 1), small.at[k + 1], small_in.at[k + 1], device)

    def small_done():
        for s in others:
            m = ranks[s]
            links.wait("small", small_plane.at[m], (dp, m), m)
        value = small_plane[0]
        for m in range(1, n_mp):
            value = value + small_plane[m]
        grad_small[...] = value
        ups = value[8:16, :]
        own = total(jnp.where(lax.broadcasted_iota(jnp.int32, ups.shape, 0) == me, ups, 0.0))
        grad_small[8:9, :] = own
        turned = pltpu.roll(value[0:8, :], (n_mp - me) % n_mp * shard, 1)
        grad_small[0:2, :] = turned[0:2, :]
        leaving.append(fetch(grad_small, grad_small_to))

    def token_back():
        def step(kind):
            whole = jnp.concatenate([qkv[kind * pairs + k] for k in range(pairs)], axis=1)
            grad_tok[...] = grad_tok[...] + dot(whole, w[rows_of(kind * d, d), :])

        loop(3, step)
        leaving.append(fetch(grad_tok, grad_tok_to))

    def project_back():
        def step(r):
            here = rows_of(r * (d // 2), d // 2)
            w[here, :] = dot(grad_qkv_t[here, :], tok[...]).astype(LOW)

        loop(6, step)

    backward = {
        "down": down_back,
        "up": up_back,
        "norm": norm_back,
        "out": out_back,
        "attend": attend_back_part,
        "token": token_back,
        "project": project_back,
        "halve": halve,
        "quarter": quarter,
        "eighth": eighth,
        "plane": to_plane,
        "finish": finish,
        "two": spread,
        "three": pair,
        "done": leave,
        "small_send": small_send,
        "small_next": small_next,
        "small_done": small_done,
    }
    for name, *args in BACKWARD:
        backward[name](*args)
    links.drain()
    for copy in leaving:
        copy.wait()


def run_kernel(n_mp, tokens, cotangent, segments, weights, shards, vectors):
    rows, d = tokens.shape
    anywhere = pl.BlockSpec(memory_space=pl.ANY)
    blocks = rows // BLOCK
    pairs = d // BLOCK
    piece = d // 16
    low = lambda *shape: pltpu.VMEM(shape, LOW)
    full = lambda *shape: pltpu.VMEM(shape, F32)
    block_count = 3 * n_mp
    names = 256
    flops = 2 * rows * d * d * 12 * 3
    operands = (tokens, cotangent, segments, *weights, *shards, *vectors)
    return pl.pallas_call(
        functools.partial(layer_kernel, n_mp),
        out_shape=(
            jax.ShapeDtypeStruct((rows, d), LOW),
            jax.ShapeDtypeStruct((rows, d), F32),
            jax.ShapeDtypeStruct((3, d, d), LOW),
            jax.ShapeDtypeStruct((16, d), F32),
        ),
        in_specs=[anywhere] * len(operands),
        out_specs=(anywhere,) * 4,
        scratch_shapes=[
            low(rows, d),
            low(rows, d),
            pltpu.VMEM(segments.shape, jnp.int32),
            full(*shards[0].shape),
            full(*shards[1].shape),
            full(len(vectors), *vectors[0].shape),
            full(len(vectors), 1, d),
            low(rows, d),
            full(rows, d),
            low(3, d, d),
            full(16, d),
            low(3 * n_mp * d, d),
            low(block_count, 2, 4 * piece, d),
            low(block_count, 2, 2 * piece, d),
            low(block_count, 2, piece, d),
            low(3, n_mp, 2, piece, d),
            low(3 * pairs, rows, BLOCK),
            low(3 * d, rows),
            low(blocks * pairs, 2 * BLOCK, BLOCK),
            low(rows, d),
            low(d, rows),
            full(rows, d),
            full(rows, BLOCK),
            low(rows, d),
            low(d, rows),
            full(rows, d),
            low(rows, d),
            low(n_mp, rows, d),
            low(n_mp, d, rows),
            low(n_mp, rows, d),
            full(blocks, BLOCK, BLOCK),
            full(n_mp, 8, d),
            full(6, 1, d // 2),
            full(3, 16, d),
            full(3, 16, d),
            full(n_mp, 1, d),
            full(n_mp, 16, d),
            pltpu.SemaphoreType.DMA((32,)),
            pltpu.SemaphoreType.DMA((names,)),
            pltpu.SemaphoreType.DMA((names,)),
        ],
        compiler_params=pltpu.CompilerParams(
            collective_id=0, has_side_effects=True, vmem_limit_bytes=63 << 20
        ),
        cost_estimate=pl.CostEstimate(flops=flops, bytes_accessed=1 << 24, transcendentals=1 << 21),
    )(*operands)


def finish_kernel(
    out,
    grad_tok,
    grad_w,
    small,
    out_to,
    grad_tok_to,
    query_to,
    key_to,
    value_to,
    attn_to,
    up_to,
    down_to,
    b_query_to,
    b_value_to,
    *refs,

):
    vectors_to, refs = refs[:7], refs[7:]
    held, wide, lines, parts, vectors, low_rows, full_rows, sems = refs
    d = held.shape[-1]
    shard = query_to.shape[0]
    pieces = d // shard
    count = 0

    def fetch(src, dst):
        nonlocal count
        copy = pltpu.make_async_copy(src, dst, sems.at[count])
        count += 1
        copy.start()
        return copy

    first = fetch(small, lines)
    loads = {}
    for g in range(3):
        for k in range(pieces):
            here = pl.ds(k * shard, shard)
            loads[g, k] = fetch(grad_w.at[g, here], held.at[g, here])
    passing = [fetch(out, low_rows), fetch(grad_tok, full_rows)]
    first.wait()
    for k in range(2):
        parts[k] = lines[k : k + 1, :shard]
    for k in range(vectors.shape[0]):
        for j in range(d // BLOCK):
            vectors[k, j : j + 1, :] = lines[2 + k : 3 + k, j * BLOCK : (j + 1) * BLOCK]
    stores = [fetch(parts.at[0], b_query_to), fetch(parts.at[1], b_value_to)]
    stores += [fetch(vectors.at[k], ref) for k, ref in enumerate(vectors_to)]
    for g in range(3):
        for k in range(pieces):
            loads[g, k].wait()

            def widen(r, g=g, k=k):
                here = at(k * shard + r * 16, 16, 16)
                wide[g, here, :] = held[g, here, :].astype(F32)

            loop(shard // 16, widen, unroll=2)
            here = pl.ds(k * shard, shard)
            if g == 0:
                stores.append(fetch(wide.at[0, here], (query_to, key_to, value_to, attn_to)[k]))
            else:
                stores.append(fetch(wide.at[g, here], (up_to, down_to)[g - 1].at[here]))
        if g == 0:
            for copy in passing:
                copy.wait()
            stores += [fetch(low_rows, out_to), fetch(full_rows, grad_tok_to)]
    for copy in stores:
        copy.wait()


def run_finish(shard, out, grad_tok, grad_w, small):
    d = out.shape[1]
    anywhere = pl.BlockSpec(memory_space=pl.ANY)
    full = lambda *shape: jax.ShapeDtypeStruct(shape, F32)
    shapes = (
        [jax.ShapeDtypeStruct(out.shape, LOW), full(*grad_tok.shape)]
        + [full(shard, d)] * 4
        + [full(d, d)] * 2
        + [full(1, shard)] * 2
        + [full(d // BLOCK, BLOCK)] * 7
    )
    return pl.pallas_call(
        finish_kernel,
        out_shape=tuple(shapes),
        in_specs=[anywhere] * 4,
        out_specs=(anywhere,) * len(shapes),
        scratch_shapes=[
            pltpu.VMEM(grad_w.shape, grad_w.dtype),
            pltpu.VMEM(grad_w.shape, F32),
            pltpu.VMEM(small.shape, F32),
            pltpu.VMEM((2, 1, shard), F32),
            pltpu.VMEM((7, d // BLOCK, BLOCK), F32),
            pltpu.VMEM(out.shape, LOW),
            pltpu.VMEM(grad_tok.shape, F32),
            pltpu.SemaphoreType.DMA((64,)),
        ],
        compiler_params=pltpu.CompilerParams(vmem_limit_bytes=60 << 20),
        cost_estimate=pl.CostEstimate(flops=0, bytes_accessed=1 << 24, transcendentals=0),
    )(out, grad_tok, grad_w, small)


def per_device(
    n_dp,
    n_mp,
    tokens,
    segment_ids,
    w_query,
    b_query,
    w_key,
    w_value,
    b_value,
    w_out,
    b_out,
    gain_one,
    shift_one,
    w_up,
    b_up,
    w_down,
    b_down,
    gain_two,
    shift_two,
    cotangent,
):
    d = tokens.shape[1]
    shard = d // n_mp
    vectors = (b_up, b_out, gain_one, shift_one, b_down, gain_two, shift_two)
    out, grad_tokens, grad_w, small = run_kernel(
        n_mp,
        tokens,
        cotangent,
        segment_ids.reshape(-1, BLOCK),
        (w_query.T, w_key.T, w_value.T, w_out, w_up, w_down),
        (b_query.reshape(1, -1), b_value.reshape(1, -1)),
        tuple(v.reshape(-1, BLOCK) for v in vectors),
    )
    if n_dp > PLANE:
        groups = [[k + PLANE * h for h in range(n_dp // PLANE)] for k in range(PLANE)]
        grad_w, small = lax.psum(
            (grad_w.astype(F32), small), "dp", axis_index_groups=groups
        )
    (
        out,
        grad_tokens,
        grad_w_query,
        grad_w_key,
        grad_w_value,
        grad_w_out,
        grad_w_up,
        grad_w_down,
        grad_b_query,
        grad_b_value,
        *grad_vectors,
    ) = run_finish(shard, out, grad_tokens, grad_w, small)
    grad_b_out, grad_gain_one, grad_shift_one, grad_b_down, grad_gain_two, grad_shift_two = [
        grad_vectors[k].reshape(-1) for k in range(6)
    ]
    return (
        out,
        grad_tokens,
        grad_w_query.T,
        grad_b_query.reshape(-1),
        grad_w_key.T,
        grad_w_value.T,
        grad_b_value.reshape(-1),
        grad_w_out,
        grad_b_out,
        grad_gain_one,
        grad_shift_one,
        grad_w_up,
        grad_vectors[6].reshape(-1),
        grad_w_down,
        grad_b_down,
        grad_gain_two,
        grad_shift_two,
    )


def solution(mesh):
    n_dp, n_mp = mesh.shape["dp"], mesh.shape["mp"]
    return jax.shard_map(
        functools.partial(per_device, n_dp, n_mp),
        mesh=mesh,
        in_specs=(
            P(("dp", "mp"), None),
            P("dp"),
            P(None, "mp"),
            P("mp"),
            P(None, "mp"),
            P(None, "mp"),
            P("mp"),
            P("mp", None),
            P(),
            P(),
            P(),
            P(None, "mp"),
            P("mp"),
            P("mp", None),
            P(),
            P(),
            P(),
            P(("dp", "mp"), None),
        ),
        out_specs=(
            P(("dp", "mp"), None),
            P(("dp", "mp"), None),
            P(None, "mp"),
            P("mp"),
            P(None, "mp"),
            P(None, "mp"),
            P("mp"),
            P("mp", None),
            P(),
            P(),
            P(),
            P(None, "mp"),
            P("mp"),
            P("mp", None),
            P(),
            P(),
            P(),
        ),
        check_vma=False,
    )
```

time: 213 us -> 172 us (0.81)
  Pallas kernels: 211 us -> 171 us
    pallas_call x1, Pallas kernels: 204 us -> 164 us  [run_kernel(): pl.pallas_call(functools.partial(layer_kernel, n_mp), out_shape=(jax.Shap...]
where the time goes in v4:
time: 172 us; the launch traced here: 171 us
  Pallas kernels  171 us (99%)
    pallas_call x1, Pallas kernels, run_kernel(): pl.pallas_call(functools.partial(layer_kernel, n_mp), out_shape=(jax.Shap...  164 us
    pallas_call x1, Pallas kernels, run_finish(): pl.pallas_call(finish_kernel, out_shape=tuple(shapes), in_specs=[anywhere...  7.09 us

profile of v4, /device:TPU:0, one launch (start us, length us, event | category | flops | bytes accessed | tf_op | source)
XLA Modules:
  0.0 171.4 jit_solution(8028326357045047868)
XLA Ops:
  0.7 163.5 %shard_map.305 = (bf16[512,768]{1,0:T(8,128)(2,1)}, f32[512,768]{1,0:T(8,128)}, bf16[3,768,768]{2,1,0:T(8,128)(2,1)}, f32[16,768]{1,0:T(8,128)}) custom-call(bf16[512,768]{1,0:T(8,128)(2,1)} %tok_in.1, bf16[512,768]{1,0:T(8,128)(2,1)} %cot_in.1, s32[16,128]{1,0:T(8,128)} %bitcast.31, bf16[192,768]{1,0:T(8,128)(2,1)} %bitcast.28, bf16[192,768]{1,0:T(8,128)(2,1)} %bitcast.29, ...), custom_call_target="tpu_custom_call" | custom-call | flops 21743271936 | bytes 16777216 | tf_op jit(solution)/shard_map/pallas_call | solution.py:824
  164.2 7.1 %shard_map.306 = (bf16[512,768]{1,0:T(8,128)(2,1)}, f32[512,768]{1,0:T(8,128)}, f32[192,768]{1,0:T(8,128)}, f32[192,768]{1,0:T(8,128)}, f32[192,768]{1,0:T(8,128...) custom-call(bf16[512,768]{1,0:T(8,128)(2,1)} %get-tuple-element.38.o, ...), custom_call_target="tpu_custom_call" | custom-call | bytes 16777216 | tf_op jit(solution)/shard_map/pallas_call | solution.py:963

commit v5 on v4

--- a/solution.py
+++ b/solution.py
@@ -15,35 +15,37 @@
 ATTEND_PARTS = 2
 ATTEND_BACK_PARTS = 6
 DOUBLED = (1, 2)
+SENDS = ((0, 2, 1), (0, 1, 2), (0, 1, 2))
+NEAR = (2,)
 GELU = 0.7978845608028654
 FORWARD = (
-    ("send", 0), ("masks",), ("one", 0, 0), ("send", 1), ("two", 0, 0), ("one", 0, 1),
-    ("biases",), ("three", 0, 0), ("two", 0, 1), ("done", 0, 0), ("project", 0), ("one", 0, 2),
-    ("attend", 0, 0), ("attend", 0, 1), ("three", 0, 1), ("two", 0, 2), ("done", 0, 1),
-    ("two", 1, 0), ("send", 2), ("three", 0, 2), ("one", 1, 1), ("done", 0, 2), ("project", 1),
-    ("three", 1, 0), ("one", 1, 2), ("attend", 1, 0), ("two", 1, 1), ("attend", 1, 1),
-    ("done", 1, 0), ("two", 1, 2), ("attn_out",), ("norm_one",), ("three", 1, 1), ("two", 2, 0),
-    ("up", 3), ("up", 0), ("done", 1, 1), ("three", 1, 2), ("one", 2, 1), ("up", 1),
-    ("three", 2, 0), ("one", 2, 2), ("done", 1, 2), ("up", 2), ("two", 2, 1), ("down", 3),
-    ("done", 2, 0), ("two", 2, 2), ("down", 0), ("three", 2, 1), ("done", 2, 1), ("down", 1),
-    ("three", 2, 2), ("done", 2, 2), ("down", 2),
+    ("send", 0), ("one", 0, 0), ("one", 0, 1), ("masks",), ("send", 1), ("biases",),
+    ("two", 0, 0), ("two", 0, 1), ("one", 0, 2), ("two", 1, 0), ("three", 0, 0), ("one", 1, 1),
+    ("send", 2), ("two", 0, 2), ("done", 0, 0), ("three", 1, 0), ("one", 1, 2), ("three", 0, 1),
+    ("two", 1, 1), ("project", 0), ("attend", 0, 0), ("three", 0, 2), ("done", 0, 1),
+    ("attend", 0, 1), ("two", 1, 2), ("done", 0, 2), ("done", 1, 0), ("project", 1),
+    ("two", 2, 0), ("attend", 1, 0), ("attend", 1, 1), ("attn_out",), ("one", 2, 1),
+    ("three", 1, 2), ("three", 1, 1), ("norm_one",), ("one", 2, 2), ("up", 3), ("done", 1, 1),
+    ("two", 2, 1), ("up", 0), ("two", 2, 2), ("three", 2, 0), ("up", 1), ("done", 1, 2),
+    ("up", 2), ("done", 2, 0), ("three", 2, 1), ("down", 3), ("down", 0), ("three", 2, 2),
+    ("done", 2, 1), ("down", 1), ("done", 2, 2), ("down", 2),
 )
 BACKWARD = (
-    ("down", 1), ("halve", 2, 1), ("down", 0), ("halve", 2, 0), ("down", 2), ("quarter", 2, 1),
-    ("halve", 2, 2), ("down", 3), ("quarter", 2, 0), ("halve", 2, 3), ("up", 1),
-    ("eighth", 2, 1), ("halve", 1, 1), ("quarter", 2, 2), ("up", 0), ("halve", 1, 0), ("up", 2),
-    ("plane", 2, 1), ("eighth", 2, 0), ("quarter", 1, 1), ("halve", 1, 2), ("up", 3),
-    ("halve", 1, 3), ("norm",), ("eighth", 2, 2), ("plane", 2, 0), ("out",), ("quarter", 1, 0),
-    ("attend", 0), ("eighth", 1, 1), ("attend", 1), ("plane", 2, 2), ("quarter", 1, 2),
-    ("attend", 2), ("attend", 3), ("eighth", 1, 0), ("attend", 4), ("plane", 1, 1),
-    ("quarter", 1, 3), ("attend", 5), ("small_send",), ("token",), ("small_next", 0),
-    ("plane", 1, 0), ("eighth", 1, 2), ("quarter", 2, 3), ("project",), ("small_next", 1),
-    ("plane", 1, 2), ("eighth", 1, 3), ("halve", 0, 1), ("halve", 0, 0), ("halve", 0, 2),
-    ("halve", 0, 3), ("quarter", 0, 1), ("small_next", 2), ("eighth", 2, 3), ("quarter", 0, 0),
-    ("eighth", 0, 1), ("quarter", 0, 2), ("small_done",), ("eighth", 0, 0), ("plane", 0, 1),
-    ("quarter", 0, 3), ("eighth", 0, 2), ("plane", 0, 0), ("finish", 1), ("finish", 2),
-    ("eighth", 0, 3), ("plane", 0, 2), ("two", 1), ("two", 2), ("three", 1), ("finish", 0),
-    ("done", 1), ("three", 2), ("two", 0), ("done", 2), ("three", 0), ("done", 0),
+    ("down", 2), ("halve", 2, 2), ("down", 1), ("quarter", 2, 2), ("halve", 2, 1), ("down", 0),
+    ("halve", 2, 0), ("quarter", 2, 1), ("down", 3), ("up", 1), ("near", 2), ("eighth", 2, 2),
+    ("halve", 1, 1), ("up", 2), ("eighth", 2, 1), ("halve", 1, 2), ("quarter", 1, 1), ("up", 3),
+    ("halve", 2, 3), ("up", 0), ("quarter", 1, 2), ("halve", 1, 0), ("norm",), ("out",),
+    ("attend", 0), ("eighth", 1, 1), ("halve", 1, 3), ("quarter", 1, 0), ("attend", 1),
+    ("plane", 2, 1), ("attend", 2), ("quarter", 1, 3), ("eighth", 1, 2), ("attend", 3),
+    ("attend", 4), ("quarter", 2, 3), ("attend", 5), ("eighth", 1, 0), ("plane", 1, 1),
+    ("token",), ("project",), ("plane", 2, 2), ("halve", 0, 2), ("eighth", 1, 3),
+    ("small_send",), ("halve", 0, 1), ("quarter", 0, 2), ("small_next", 0), ("plane", 1, 2),
+    ("halve", 0, 3), ("halve", 0, 0), ("quarter", 0, 1), ("eighth", 0, 2), ("quarter", 0, 0),
+    ("eighth", 0, 1), ("plane", 1, 0), ("plane", 0, 2), ("eighth", 2, 3), ("eighth", 0, 0),
+    ("quarter", 0, 3), ("finish", 2), ("plane", 0, 1), ("plane", 0, 0), ("finish", 1),
+    ("eighth", 0, 3), ("two", 2), ("small_next", 1), ("finish", 0), ("two", 1), ("two", 0),
+    ("small_next", 2), ("three", 2), ("three", 1), ("done", 1), ("done", 2), ("three", 0),
+    ("small_done",), ("done", 0),
 )
 MASKED = -1000000000.0
 MESH = pl.DeviceIdType.MESH
@@ -155,6 +157,7 @@
         quarter_in,
         eighth_in,
         plane_in,
+        near_in,
         qkv,
         grad_qkv_t,
         prob,
@@ -303,7 +306,7 @@
         return w.at[rows_of(start + (2 * high + bit) * piece, piece)]
 
     def send(g):
-        for k in others:
+        for k in SENDS[g]:
             for side in range(2):
                 rows_in = share(g, k, me, side)
                 links.start(("w", g, side), rows_in, rows_in, (dp, ranks[k]), ranks[k], me)
@@ -374,7 +377,7 @@
                 columns = part[:, j * BLOCK : (j + 1) * BLOCK]
                 qkv[kind * pairs + half * half_pairs + j] = columns.astype(LOW)
 
-        loop(3, one_kind)
+        loop(3, one_kind, unroll=3)
 
     lane = lax.broadcasted_iota(jnp.int32, (1, BLOCK), 1)
     first = jnp.where(lane < HD, 1.0, 0.0).astype(LOW)
@@ -417,7 +420,7 @@
             i = i + part * count
             attend(i % blocks, half_of(k) * half_pairs + i // blocks)
 
-        loop(count, step, unroll=2)
+        loop(count, step, unroll=count)
 
     def attn_out():
         acc[...] = dot(ctx[...], w[3 * d : 4 * d, :])
@@ -515,11 +518,14 @@
     def block_of(g, s):
         return g * n_mp + s
 
-    def add_rows(start, source, offset, size):
+    def add_rows(start, sources, offset, size):
         def one(k):
             here = rows_of(start + k * 16, 16)
             there = rows_of(offset + k * 16, 16)
-            w[here, :] = (w[here, :].astype(F32) + source[there, :].astype(F32)).astype(LOW)
+            value = w[here, :].astype(F32)
+            for source in sources:
+                value = value + source[there, :].astype(F32)
+            w[here, :] = value.astype(LOW)
 
         loop(size // 16, one)
 
@@ -533,13 +539,32 @@
                 core,
             )
 
+    def near(g):
+        k = block_of(g, 0)
+        for side in range(2):
+            start = region(g, ranks[0], c, side)
+            links.wait(("half", k, side), half_in.at[k, side], core)
+            add_rows(start, (half_in.at[k, side],), 0, 4 * piece)
+            links.start(
+                ("near", g, side),
+                w.at[rows_of(start, 4 * piece)],
+                near_in.at[NEAR.index(g), side],
+                (dp, ranks[0]),
+            )
+
     def quarter(g, s):
         m, k = ranks[s], block_of(g, s)
+        sources = []
         for side, (bit, device) in enumerate(((x, x_side), (y, y_side))):
             start = region(g, m, c, side)
             links.wait(("half", k, side), half_in.at[k, side], core)
+            sources.append([half_in.at[k, side]])
+            if s == n_mp - 1 and g in NEAR:
+                arrived = near_in.at[NEAR.index(g), side]
+                links.wait(("near", g, side), arrived, (dp, ranks[0]))
+                sources[side].append(arrived)
             other = 2 * (1 - bit) * piece
-            add_rows(start + other, half_in.at[k, side], other, 2 * piece)
+            add_rows(start + other, sources[side], other, 2 * piece)
             links.start(
                 ("quarter", k, side),
                 w.at[rows_of(start + other, 2 * piece)],
@@ -549,7 +574,7 @@
         for side, bit in enumerate((x, y)):
             start = region(g, m, c, side)
             own = 2 * bit * piece
-            add_rows(start + own, half_in.at[k, side], own, 2 * piece)
+            add_rows(start + own, sources[side], own, 2 * piece)
 
     def eighth(g, s):
         m, k = ranks[s], block_of(g, s)
@@ -558,7 +583,7 @@
             start = region(g, m, c, side) + 2 * high * piece
             links.wait(("quarter", k, side), quarter_in.at[k, side], before)
             other = (1 - bit) * piece
-            add_rows(start + other, quarter_in.at[k, side], other, piece)
+            add_rows(start + other, (quarter_in.at[k, side],), other, piece)
             links.start(
                 ("eighth", k, side),
                 w.at[rows_of(start + other, piece)],
@@ -568,14 +593,14 @@
         for side, (high, bit, before, device) in enumerate(sides):
             start = region(g, m, c, side) + 2 * high * piece
             own = bit * piece
-            add_rows(start + own, quarter_in.at[k, side], own, piece)
+            add_rows(start + own, (quarter_in.at[k, side],), own, piece)
 
     def to_plane(g, s):
         m, k = ranks[s], block_of(g, s)
         for side, (high, bit, device) in enumerate(((x, y, y_side), (y, x, x_side))):
             start = region(g, m, c, side) + (2 * high + bit) * piece
             links.wait(("eighth", k, side), eighth_in.at[k, side], device)
-            add_rows(start, eighth_in.at[k, side], 0, piece)
+            add_rows(start, (eighth_in.at[k, side],), 0, piece)
             if s < n_mp - 1:
                 links.start(
                     ("plane", g, side),
@@ -598,17 +623,17 @@
 
     def finish(g):
         to_plane(g, n_mp - 1)
+        senders = [ranks[k] for k in others if k or g not in NEAR]
         for side, (high, bit) in enumerate(((x, y), (y, x))):
             start = region(g, me, c, side) + (2 * high + bit) * piece
             goal = c * (d // 2) + side * (d // 4) + (2 * high + bit) * piece
-            for k in others:
-                m = ranks[k]
+            for m in senders:
                 links.wait(("plane", g, side), plane_in.at[g, m, side], (dp, m), m)
 
             def step(k):
                 value = w[rows_of(start + k * 16, 16), :].astype(F32)
-                for s in others:
-                    value = value + plane_in[g, ranks[s], side, rows_of(k * 16, 16), :].astype(F32)
+                for m in senders:
+                    value = value + plane_in[g, m, side, rows_of(k * 16, 16), :].astype(F32)
                 grad_w[g, rows_of(goal + k * 16, 16), :] = value.astype(LOW)
 
             loop(piece // 16, step)
@@ -635,14 +660,14 @@
             act[m, tile, :] = grad_up.astype(LOW)
             small_up[m] = small_up[m] + total(grad_up)
 
-        loop(rows // TILE, step)
+        loop(rows // TILE, step, unroll=2)
 
         def weight(r):
             tile = rows_of(r * (d // 2), d // 2)
             there = rows_of(2 * group + m * d + r * (d // 2), d // 2)
             w[there, :] = dot(act_t[m, tile, :], grad_low[...]).astype(LOW)
 
-        loop(2, weight)
+        loop(2, weight, unroll=2)
 
     def up_back(k):
         m = ranks[k]
@@ -652,14 +677,14 @@
             tile = rows_of(r * TILE, TILE)
             acc[tile, :] = acc[tile, :] + dot_nt(act[m, tile, :], w[here, :])
 
-        loop(rows // TILE, step)
+        loop(rows // TILE, step, unroll=2)
 
         def weight(r):
             tile = rows_of(r * (d // 2), d // 2)
             there = rows_of(group + m * d + r * (d // 2), d // 2)
             w[there, :] = dot(normed_t[tile, :], act[m]).astype(LOW)
 
-        loop(2, weight)
+        loop(2, weight, unroll=2)
 
     def norm_back():
         def step(r):
@@ -682,14 +707,14 @@
             tile = rows_of(r * TILE, TILE)
             ctx[tile, :] = dot_nt(grad_low[tile, :], w[3 * d : 4 * d, :]).astype(LOW)
 
-        loop(rows // TILE, step)
+        loop(rows // TILE, step, unroll=2)
 
         def weight(r):
             tile = rows_of(r * (d // 2), d // 2)
             there = rows_of(3 * d + r * (d // 2), d // 2)
             w[there, :] = dot(ctx_t[tile, :], grad_low[...]).astype(LOW)
 
-        loop(2, weight)
+        loop(2, weight, unroll=2)
 
     def attend_back(index):
         b, p = index // pairs, index % pairs
@@ -729,7 +754,7 @@
 
     def attend_back_part(part):
         count = blocks * pairs // ATTEND_BACK_PARTS
-        loop(count, lambda i: attend_back(part * count + i), unroll=2)
+        loop(count, lambda i: attend_back(part * count + i), unroll=count)
 
     def small_send():
         for k in range(pairs):
@@ -780,7 +805,7 @@
             here = rows_of(r * (d // 2), d // 2)
             w[here, :] = dot(grad_qkv_t[here, :], tok[...]).astype(LOW)
 
-        loop(6, step)
+        loop(6, step, unroll=2)
 
     backward = {
         "down": down_back,
@@ -791,6 +816,7 @@
         "token": token_back,
         "project": project_back,
         "halve": halve,
+        "near": near,
         "quarter": quarter,
         "eighth": eighth,
         "plane": to_plane,
@@ -848,6 +874,7 @@
             low(block_count, 2, 2 * piece, d),
             low(block_count, 2, piece, d),
             low(3, n_mp, 2, piece, d),
+            low(len(NEAR), 2, 4 * piece, d),
             low(3 * pairs, rows, BLOCK),
             low(3 * d, rows),
             low(blocks * pairs, 2 * BLOCK, BLOCK),

time: 172 us -> 161 us (0.936)
  Pallas kernels: 171 us -> 160 us
    pallas_call x1, Pallas kernels: 164 us -> 153 us  [run_kernel(): pl.pallas_call(functools.partial(layer_kernel, n_mp), out_shape=(jax.Shap...]
where the time goes in v5:
time: 161 us
  Pallas kernels  160 us (99%)
    pallas_call x1, Pallas kernels, run_kernel(): pl.pallas_call(functools.partial(layer_kernel, n_mp), out_shape=(jax.Shap...  153 us
    pallas_call x1, Pallas kernels, run_finish(): pl.pallas_call(finish_kernel, out_shape=tuple(shapes), in_specs=[anywhere...  7.09 us

profile of v5, /device:TPU:0, one launch (start us, length us, event | category | flops | bytes accessed | tf_op | source)
XLA Modules:
  0.0 160.7 jit_solution(9106018438505908147)
XLA Ops:
  0.7 152.8 %shard_map.305 = (bf16[512,768]{1,0:T(8,128)(2,1)}, f32[512,768]{1,0:T(8,128)}, bf16[3,768,768]{2,1,0:T(8,128)(2,1)}, f32[16,768]{1,0:T(8,128)}) custom-call(bf16[512,768]{1,0:T(8,128)(2,1)} %tok_in.1, bf16[512,768]{1,0:T(8,128)(2,1)} %cot_in.1, s32[16,128]{1,0:T(8,128)} %bitcast.31, bf16[192,768]{1,0:T(8,128)(2,1)} %bitcast.28, bf16[192,768]{1,0:T(8,128)(2,1)} %bitcast.29, ...), custom_call_target="tpu_custom_call" | custom-call | flops 21743271936 | bytes 16777216 | tf_op jit(solution)/shard_map/pallas_call | solution.py:850
  153.4 7.1 %shard_map.306 = (bf16[512,768]{1,0:T(8,128)(2,1)}, f32[512,768]{1,0:T(8,128)}, f32[192,768]{1,0:T(8,128)}, f32[192,768]{1,0:T(8,128)}, f32[192,768]{1,0:T(8,128...) custom-call(bf16[512,768]{1,0:T(8,128)(2,1)} %get-tuple-element.38.o, ...), custom_call_target="tpu_custom_call" | custom-call | bytes 16777216 | tf_op jit(solution)/shard_map/pallas_call | solution.py:990

commit v6 on v5

--- a/solution.py
+++ b/solution.py
@@ -14,21 +14,21 @@
 PLANE = 8
 ATTEND_PARTS = 2
 ATTEND_BACK_PARTS = 6
-DOUBLED = (1, 2)
-SENDS = ((0, 2, 1), (0, 1, 2), (0, 1, 2))
+DOUBLED = (0, 1, 2)
+SENDS = ((0, 1, 2), (0, 1, 2), (0, 1, 2))
 NEAR = (2,)
 GELU = 0.7978845608028654
 FORWARD = (
-    ("send", 0), ("one", 0, 0), ("one", 0, 1), ("masks",), ("send", 1), ("biases",),
-    ("two", 0, 0), ("two", 0, 1), ("one", 0, 2), ("two", 1, 0), ("three", 0, 0), ("one", 1, 1),
-    ("send", 2), ("two", 0, 2), ("done", 0, 0), ("three", 1, 0), ("one", 1, 2), ("three", 0, 1),
-    ("two", 1, 1), ("project", 0), ("attend", 0, 0), ("three", 0, 2), ("done", 0, 1),
-    ("attend", 0, 1), ("two", 1, 2), ("done", 0, 2), ("done", 1, 0), ("project", 1),
-    ("two", 2, 0), ("attend", 1, 0), ("attend", 1, 1), ("attn_out",), ("one", 2, 1),
-    ("three", 1, 2), ("three", 1, 1), ("norm_one",), ("one", 2, 2), ("up", 3), ("done", 1, 1),
-    ("two", 2, 1), ("up", 0), ("two", 2, 2), ("three", 2, 0), ("up", 1), ("done", 1, 2),
-    ("up", 2), ("done", 2, 0), ("three", 2, 1), ("down", 3), ("down", 0), ("three", 2, 2),
-    ("done", 2, 1), ("down", 1), ("done", 2, 2), ("down", 2),
+    ("send", 0), ("send_biases",), ("send", 1), ("two", 0, 0), ("one", 0, 1), ("three", 0, 0),
+    ("one", 0, 2), ("send", 2), ("two", 0, 1), ("two", 0, 2), ("masks",), ("biases",),
+    ("done", 0, 0), ("three", 0, 1), ("one", 1, 1), ("three", 0, 2), ("two", 1, 0),
+    ("one", 1, 2), ("done", 0, 2), ("done", 0, 1), ("two", 1, 1), ("project", 0),
+    ("attend", 0, 0), ("attend", 0, 1), ("project", 1), ("two", 1, 2), ("attend", 1, 0),
+    ("three", 1, 0), ("three", 1, 1), ("one", 2, 1), ("two", 2, 0), ("attend", 1, 1),
+    ("done", 1, 0), ("attn_out",), ("norm_one",), ("one", 2, 2), ("done", 1, 1), ("up", 3),
+    ("two", 2, 1), ("three", 1, 2), ("up", 0), ("done", 1, 2), ("two", 2, 2), ("up", 1),
+    ("three", 2, 0), ("up", 2), ("three", 2, 1), ("down", 3), ("done", 2, 0), ("three", 2, 2),
+    ("done", 2, 1), ("down", 0), ("down", 1), ("done", 2, 2), ("down", 2),
 )
 BACKWARD = (
     ("down", 2), ("halve", 2, 2), ("down", 1), ("quarter", 2, 2), ("halve", 2, 1), ("down", 0),
@@ -203,6 +203,11 @@
     def rows_of(start, size):
         return at(start, size, 16)
 
+    barrier = pltpu.get_barrier_semaphore()
+    partners = [core, x_side, y_side] + [(dp, ranks[k]) for k in others]
+    for partner in partners:
+        pl.semaphore_signal(barrier, inc=1, device_id=partner, device_id_type=MESH)
+
     count = 0
 
     def fetch(src, dst):
@@ -212,34 +217,17 @@
         copy.start()
         return copy
 
-    own_w = [
+    own_zero = [
         fetch(ref, w.at[rows_of(kind * d + me * shard, shard)])
         for kind, ref in enumerate((w_query, w_key, w_value, w_out))
     ]
+    own_one = [fetch(w_up, w.at[rows_of(group + me * d, d)])]
+    own_two = [fetch(w_down, w.at[rows_of(2 * group + me * d, d)])]
+    own_w = (own_zero, own_one, own_two)
     own_b = [fetch(b_query_in, b_query), fetch(b_value_in, b_value)]
     own_b += [fetch(ref, vectors.at[k]) for k, ref in enumerate(vectors_in)]
-    own_w.append(fetch(w_up, w.at[rows_of(group + me * d, d)]))
-    own_w.append(fetch(w_down, w.at[rows_of(2 * group + me * d, d)]))
     own_rows = [fetch(seg_in, seg), fetch(tok_in, tok), fetch(cot_in, cot)]
 
-    barrier = pltpu.get_barrier_semaphore()
-    partners = [core, x_side, y_side] + [(dp, ranks[k]) for k in others]
-    for partner in partners:
-        pl.semaphore_signal(barrier, inc=1, device_id=partner, device_id_type=MESH)
-
-    for copy in own_b:
-        copy.wait()
-    for k in range(len(vectors_in)):
-        parts = [vectors[k, j : j + 1, :] for j in range(d // BLOCK)]
-        lines[k] = jnp.concatenate(parts, axis=1)
-    pad = jnp.zeros((1, d - shard), F32)
-    for k, ref in enumerate((b_query, b_value)):
-        placed = jnp.broadcast_to(jnp.concatenate([ref[...], pad], axis=1), (8, d))
-        bias_in[me, k : k + 1, :] = pltpu.roll(placed, me * shard, 1)[0:1, :]
-    bias_in[me, 2:3, :] = b_up[...]
-
-    for copy in own_w:
-        copy.wait()
     pl.semaphore_wait(barrier, len(partners))
 
     links = Links(send_sem, recv_sem)
@@ -294,10 +282,6 @@
             for side in range(2):
                 links.wait((self.name, 3, side), self.at(self.theirs[side], 4 * piece), core)
 
-    for k in others:
-        m = ranks[k]
-        links.start("bias", bias_in.at[me], bias_in.at[me], (dp, m), m, me)
-
     def share(g, k, m, side):
         start = region(g, m, c, side)
         high, bit = (x, y) if side == 0 else (y, x)
@@ -306,6 +290,8 @@
         return w.at[rows_of(start + (2 * high + bit) * piece, piece)]
 
     def send(g):
+        for copy in own_w[g]:
+            copy.wait()
         for k in SENDS[g]:
             for side in range(2):
                 rows_in = share(g, k, me, side)
@@ -348,6 +334,21 @@
             line = seg[pl.ds(me * blocks + b, 1), :]
             across = jnp.broadcast_to(line, (BLOCK, BLOCK))
             mask[b] = jnp.where(across == across.T, 0.0, MASKED)
+
+    def send_biases():
+        for copy in own_b:
+            copy.wait()
+        for k in range(len(vectors_in)):
+            parts = [vectors[k, j : j + 1, :] for j in range(d // BLOCK)]
+            lines[k] = jnp.concatenate(parts, axis=1)
+        pad = jnp.zeros((1, d - shard), F32)
+        for k, ref in enumerate((b_query, b_value)):
+            placed = jnp.broadcast_to(jnp.concatenate([ref[...], pad], axis=1), (8, d))
+            bias_in[me, k : k + 1, :] = pltpu.roll(placed, me * shard, 1)[0:1, :]
+        bias_in[me, 2:3, :] = b_up[...]
+        for k in others:
+            m = ranks[k]
+            links.start("bias", bias_in.at[me], bias_in.at[me], (dp, m), m, me)
 
     def biases():
         for k in others:
@@ -478,6 +479,7 @@
         "three": three,
         "done": done,
         "masks": masks,
+        "send_biases": send_biases,
         "biases": biases,
         "project": project,
         "attend": attend_part,

time: 161 us -> 156 us (0.969)
  Pallas kernels: 160 us -> 155 us
    pallas_call x1, Pallas kernels: 153 us -> 148 us  [run_kernel(): pl.pallas_call(functools.partial(layer_kernel, n_mp), out_shape=(jax.Shap...]
where the time goes in v6:
time: 156 us
  Pallas kernels  155 us (99%)
    pallas_call x1, Pallas kernels, run_kernel(): pl.pallas_call(functools.partial(layer_kernel, n_mp), out_shape=(jax.Shap...  148 us
    pallas_call x1, Pallas kernels, run_finish(): pl.pallas_call(finish_kernel, out_shape=tuple(shapes), in_specs=[anywhere...  7.09 us

profile of v6, /device:TPU:0, one launch (start us, length us, event | category | flops | bytes accessed | tf_op | source)
XLA Modules:
  0.0 156.1 jit_solution(12064981804284147321)
XLA Ops:
  0.7 148.2 %shard_map.305 = (bf16[512,768]{1,0:T(8,128)(2,1)}, f32[512,768]{1,0:T(8,128)}, bf16[3,768,768]{2,1,0:T(8,128)(2,1)}, f32[16,768]{1,0:T(8,128)}) custom-call(bf16[512,768]{1,0:T(8,128)(2,1)} %tok_in.1, bf16[512,768]{1,0:T(8,128)(2,1)} %cot_in.1, s32[16,128]{1,0:T(8,128)} %bitcast.31, bf16[192,768]{1,0:T(8,128)(2,1)} %bitcast.28, bf16[192,768]{1,0:T(8,128)(2,1)} %bitcast.29, ...), custom_call_target="tpu_custom_call" | custom-call | flops 21743271936 | bytes 16777216 | tf_op jit(solution)/shard_map/pallas_call | solution.py:852
  148.9 7.1 %shard_map.306 = (bf16[512,768]{1,0:T(8,128)(2,1)}, f32[512,768]{1,0:T(8,128)}, f32[192,768]{1,0:T(8,128)}, f32[192,768]{1,0:T(8,128)}, f32[192,768]{1,0:T(8,128...) custom-call(bf16[512,768]{1,0:T(8,128)(2,1)} %get-tuple-element.38.o, ...), custom_call_target="tpu_custom_call" | custom-call | bytes 16777216 | tf_op jit(solution)/shard_map/pallas_call | solution.py:992

commit v7 on v6

--- a/solution.py
+++ b/solution.py
@@ -17,6 +17,7 @@
 DOUBLED = (0, 1, 2)
 SENDS = ((0, 1, 2), (0, 1, 2), (0, 1, 2))
 NEAR = (2,)
+SEMI = (1, 0)
 GELU = 0.7978845608028654
 FORWARD = (
     ("send", 0), ("send_biases",), ("send", 1), ("two", 0, 0), ("one", 0, 1), ("three", 0, 0),
@@ -31,21 +32,21 @@
     ("done", 2, 1), ("down", 0), ("down", 1), ("done", 2, 2), ("down", 2),
 )
 BACKWARD = (
-    ("down", 2), ("halve", 2, 2), ("down", 1), ("quarter", 2, 2), ("halve", 2, 1), ("down", 0),
-    ("halve", 2, 0), ("quarter", 2, 1), ("down", 3), ("up", 1), ("near", 2), ("eighth", 2, 2),
-    ("halve", 1, 1), ("up", 2), ("eighth", 2, 1), ("halve", 1, 2), ("quarter", 1, 1), ("up", 3),
-    ("halve", 2, 3), ("up", 0), ("quarter", 1, 2), ("halve", 1, 0), ("norm",), ("out",),
-    ("attend", 0), ("eighth", 1, 1), ("halve", 1, 3), ("quarter", 1, 0), ("attend", 1),
-    ("plane", 2, 1), ("attend", 2), ("quarter", 1, 3), ("eighth", 1, 2), ("attend", 3),
-    ("attend", 4), ("quarter", 2, 3), ("attend", 5), ("eighth", 1, 0), ("plane", 1, 1),
-    ("token",), ("project",), ("plane", 2, 2), ("halve", 0, 2), ("eighth", 1, 3),
-    ("small_send",), ("halve", 0, 1), ("quarter", 0, 2), ("small_next", 0), ("plane", 1, 2),
-    ("halve", 0, 3), ("halve", 0, 0), ("quarter", 0, 1), ("eighth", 0, 2), ("quarter", 0, 0),
-    ("eighth", 0, 1), ("plane", 1, 0), ("plane", 0, 2), ("eighth", 2, 3), ("eighth", 0, 0),
-    ("quarter", 0, 3), ("finish", 2), ("plane", 0, 1), ("plane", 0, 0), ("finish", 1),
-    ("eighth", 0, 3), ("two", 2), ("small_next", 1), ("finish", 0), ("two", 1), ("two", 0),
-    ("small_next", 2), ("three", 2), ("three", 1), ("done", 1), ("done", 2), ("three", 0),
-    ("small_done",), ("done", 0),
+    ("down", 1), ("halve", 2, 1), ("down", 0), ("halve", 2, 0), ("quarter", 2, 1), ("down", 2),
+    ("halve", 2, 2), ("down", 3), ("quarter", 2, 2), ("near", 2), ("up", 1), ("halve", 1, 1),
+    ("eighth", 2, 1), ("up", 0), ("halve", 1, 0), ("quarter", 1, 1), ("halve", 2, 3), ("up", 2),
+    ("halve", 1, 2), ("eighth", 2, 2), ("up", 3), ("norm",), ("quarter", 1, 2),
+    ("quarter", 1, 0), ("out",), ("halve", 1, 3), ("eighth", 1, 1), ("attend", 0),
+    ("plane", 2, 2), ("attend", 1), ("attend", 2), ("attend", 3), ("attend", 4),
+    ("quarter", 2, 3), ("attend", 5), ("eighth", 1, 2), ("quarter", 1, 3), ("plane", 2, 1),
+    ("token",), ("project",), ("halve", 0, 1), ("small_send",), ("eighth", 2, 3),
+    ("halve", 0, 0), ("plane", 1, 1), ("semi", 1), ("halve", 0, 2), ("quarter", 0, 1),
+    ("plane", 1, 2), ("small_next", 0), ("quarter", 0, 0), ("eighth", 0, 1), ("quarter", 0, 2),
+    ("halve", 0, 3), ("finish", 2), ("small_next", 1), ("plane", 0, 1), ("semi", 0),
+    ("eighth", 0, 2), ("quarter", 0, 3), ("eighth", 1, 3), ("two", 2), ("plane", 0, 2),
+    ("small_next", 2), ("eighth", 0, 3), ("finish", 1), ("finish", 0), ("two", 1), ("two", 0),
+    ("small_done",), ("three", 1), ("three", 2), ("three", 0), ("done", 1), ("done", 2),
+    ("done", 0),
 )
 MASKED = -1000000000.0
 MESH = pl.DeviceIdType.MESH
@@ -158,6 +159,7 @@
         eighth_in,
         plane_in,
         near_in,
+        semi_in,
         qkv,
         grad_qkv_t,
         prob,
@@ -437,7 +439,7 @@
             inv_one[here, :] = jnp.broadcast_to(inverse, (ROWS, BLOCK))
             normed[here, :] = (unit * gain_one[...] + shift_one[...]).astype(LOW)
 
-        loop(rows // ROWS, step)
+        loop(rows // ROWS, step, unroll=4)
 
         def turn(r):
             here = at(r * BLOCK, BLOCK, BLOCK)
@@ -459,7 +461,7 @@
             slope_in = 0.5 * GELU + (1.5 * 0.044715 * GELU) * square
             slope[m, here, :] = (cdf + u * (1.0 - inner * inner) * slope_in).astype(LOW)
 
-        loop(rows // 16, gelu)
+        loop(rows // 16, gelu, unroll=2)
 
         def turn(r):
             here = at(r * BLOCK, BLOCK, BLOCK)
@@ -514,7 +516,7 @@
         add_small(6, total(grad * unit))
         add_small(7, total(grad))
 
-    loop(rows // ROWS, norm_two)
+    loop(rows // ROWS, norm_two, unroll=8)
     leaving = [fetch(out, out_to)]
 
     def block_of(g, s):
@@ -529,7 +531,7 @@
                 value = value + source[there, :].astype(F32)
             w[here, :] = value.astype(LOW)
 
-        loop(size // 16, one)
+        loop(size // 16, one, unroll=3)
 
     def halve(g, s):
         m, k = ranks[s], block_of(g, s)
@@ -578,14 +580,33 @@
             own = 2 * bit * piece
             add_rows(start + own, sources[side], own, 2 * piece)
 
+    def semi(g):
+        k = block_of(g, 0)
+        for side, (bit, device) in enumerate(((x, x_side), (y, y_side))):
+            start = region(g, ranks[0], c, side) + 2 * bit * piece
+            links.wait(("quarter", k, side), quarter_in.at[k, side], device)
+            add_rows(start, (quarter_in.at[k, side],), 0, 2 * piece)
+            links.start(
+                ("semi", g, side),
+                w.at[rows_of(start, 2 * piece)],
+                semi_in.at[SEMI.index(g), side],
+                (dp, ranks[0]),
+            )
+
     def eighth(g, s):
         m, k = ranks[s], block_of(g, s)
+        sources = []
         sides = ((x, y, x_side, y_side), (y, x, y_side, x_side))
         for side, (high, bit, before, device) in enumerate(sides):
             start = region(g, m, c, side) + 2 * high * piece
             links.wait(("quarter", k, side), quarter_in.at[k, side], before)
+            sources.append([quarter_in.at[k, side]])
+            if s == n_mp - 1 and g in SEMI:
+                arrived = semi_in.at[SEMI.index(g), side]
+                links.wait(("semi", g, side), arrived, (dp, ranks[0]))
+                sources[side].append(arrived)
             other = (1 - bit) * piece
-            add_rows(start + other, (quarter_in.at[k, side],), other, piece)
+            add_rows(start + other, sources[side], other, piece)
             links.start(
                 ("eighth", k, side),
                 w.at[rows_of(start + other, piece)],
@@ -595,7 +616,7 @@
         for side, (high, bit, before, device) in enumerate(sides):
             start = region(g, m, c, side) + 2 * high * piece
             own = bit * piece
-            add_rows(start + own, (quarter_in.at[k, side],), own, piece)
+            add_rows(start + own, sources[side], own, piece)
 
     def to_plane(g, s):
         m, k = ranks[s], block_of(g, s)
@@ -625,7 +646,7 @@
 
     def finish(g):
         to_plane(g, n_mp - 1)
-        senders = [ranks[k] for k in others if k or g not in NEAR]
+        senders = [ranks[k] for k in others if k or g not in NEAR + SEMI]
         for side, (high, bit) in enumerate(((x, y), (y, x))):
             start = region(g, me, c, side) + (2 * high + bit) * piece
             goal = c * (d // 2) + side * (d // 4) + (2 * high + bit) * piece
@@ -638,7 +659,7 @@
                     value = value + plane_in[g, m, side, rows_of(k * 16, 16), :].astype(F32)
                 grad_w[g, rows_of(goal + k * 16, 16), :] = value.astype(LOW)
 
-            loop(piece // 16, step)
+            loop(piece // 16, step, unroll=3)
         outs[g].one()
 
     def spread(g):
@@ -702,7 +723,7 @@
             add_small(3, total(grad * unit))
             add_small(4, total(grad))
 
-        loop(rows // ROWS, step)
+        loop(rows // ROWS, step, unroll=4)
 
     def out_back():
         def step(r):
@@ -819,6 +840,7 @@
         "project": project_back,
         "halve": halve,
         "near": near,
+        "semi": semi,
         "quarter": quarter,
         "eighth": eighth,
         "plane": to_plane,
@@ -877,6 +899,7 @@
             low(block_count, 2, piece, d),
             low(3, n_mp, 2, piece, d),
             low(len(NEAR), 2, 4 * piece, d),
+            low(max(len(SEMI), 1), 2, 2 * piece, d),
             low(3 * pairs, rows, BLOCK),
             low(3 * d, rows),
             low(blocks * pairs, 2 * BLOCK, BLOCK),

time: 156 us -> 151 us (0.968)
  Pallas kernels: 155 us -> 150 us
    pallas_call x1, Pallas kernels: 148 us -> 143 us  [run_kernel(): pl.pallas_call(functools.partial(layer_kernel, n_mp), out_shape=(jax.Shap...]
where the time goes in v7:
time: 151 us
  Pallas kernels  150 us (99%)
    pallas_call x1, Pallas kernels, run_kernel(): pl.pallas_call(functools.partial(layer_kernel, n_mp), out_shape=(jax.Shap...  143 us
    pallas_call x1, Pallas kernels, run_finish(): pl.pallas_call(finish_kernel, out_shape=tuple(shapes), in_specs=[anywhere...  7.09 us

profile of v7, /device:TPU:0, one launch (start us, length us, event | category | flops | bytes accessed | tf_op | source)
XLA Modules:
  0.0 150.8 jit_solution(9840558914971704066)
XLA Ops:
  0.7 142.9 %shard_map.305 = (bf16[512,768]{1,0:T(8,128)(2,1)}, f32[512,768]{1,0:T(8,128)}, bf16[3,768,768]{2,1,0:T(8,128)(2,1)}, f32[16,768]{1,0:T(8,128)}) custom-call(bf16[512,768]{1,0:T(8,128)(2,1)} %tok_in.1, bf16[512,768]{1,0:T(8,128)(2,1)} %cot_in.1, s32[16,128]{1,0:T(8,128)} %bitcast.31, bf16[192,768]{1,0:T(8,128)(2,1)} %bitcast.28, bf16[192,768]{1,0:T(8,128)(2,1)} %bitcast.29, ...), custom_call_target="tpu_custom_call" | custom-call | flops 21743271936 | bytes 16777216 | tf_op jit(solution)/shard_map/pallas_call | solution.py:874
  143.6 7.1 %shard_map.306 = (bf16[512,768]{1,0:T(8,128)(2,1)}, f32[512,768]{1,0:T(8,128)}, f32[192,768]{1,0:T(8,128)}, f32[192,768]{1,0:T(8,128)}, f32[192,768]{1,0:T(8,128...) custom-call(bf16[512,768]{1,0:T(8,128)(2,1)} %get-tuple-element.38.o, ...), custom_call_target="tpu_custom_call" | custom-call | bytes 16777216 | tf_op jit(solution)/shard_map/pallas_call | solution.py:1015

commit v8 on v7

--- a/solution.py
+++ b/solution.py
@@ -20,33 +20,32 @@
 SEMI = (1, 0)
 GELU = 0.7978845608028654
 FORWARD = (
-    ("send", 0), ("send_biases",), ("send", 1), ("two", 0, 0), ("one", 0, 1), ("three", 0, 0),
-    ("one", 0, 2), ("send", 2), ("two", 0, 1), ("two", 0, 2), ("masks",), ("biases",),
-    ("done", 0, 0), ("three", 0, 1), ("one", 1, 1), ("three", 0, 2), ("two", 1, 0),
-    ("one", 1, 2), ("done", 0, 2), ("done", 0, 1), ("two", 1, 1), ("project", 0),
-    ("attend", 0, 0), ("attend", 0, 1), ("project", 1), ("two", 1, 2), ("attend", 1, 0),
-    ("three", 1, 0), ("three", 1, 1), ("one", 2, 1), ("two", 2, 0), ("attend", 1, 1),
-    ("done", 1, 0), ("attn_out",), ("norm_one",), ("one", 2, 2), ("done", 1, 1), ("up", 3),
-    ("two", 2, 1), ("three", 1, 2), ("up", 0), ("done", 1, 2), ("two", 2, 2), ("up", 1),
-    ("three", 2, 0), ("up", 2), ("three", 2, 1), ("down", 3), ("done", 2, 0), ("three", 2, 2),
-    ("done", 2, 1), ("down", 0), ("down", 1), ("done", 2, 2), ("down", 2),
+    ("send", 0), ("send_biases",), ("send", 1), ("two", 0, 0), ("one", 0, 1), ("one", 0, 2),
+    ("two", 0, 1), ("send", 2), ("two", 0, 2), ("one", 1, 1), ("two", 1, 0), ("three", 0, 1),
+    ("three", 0, 2), ("three", 0, 0), ("one", 1, 2), ("two", 1, 1), ("masks",), ("done", 0, 0),
+    ("biases",), ("project", 0), ("attend", 0, 0), ("two", 1, 2), ("done", 0, 2),
+    ("attend", 0, 1), ("done", 0, 1), ("project", 1), ("attend", 1, 0), ("three", 1, 0),
+    ("attend", 1, 1), ("one", 2, 1), ("attn_out",), ("two", 2, 0), ("norm_one",), ("one", 2, 2),
+    ("three", 1, 2), ("done", 1, 0), ("three", 1, 1), ("two", 2, 1), ("up", 3), ("done", 1, 1),
+    ("done", 1, 2), ("up", 0), ("three", 2, 0), ("two", 2, 2), ("up", 1), ("up", 2),
+    ("down", 3), ("three", 2, 1), ("done", 2, 0), ("down", 0), ("three", 2, 2), ("done", 2, 1),
+    ("down", 1), ("done", 2, 2), ("down", 2),
 )
 BACKWARD = (
-    ("down", 1), ("halve", 2, 1), ("down", 0), ("halve", 2, 0), ("quarter", 2, 1), ("down", 2),
-    ("halve", 2, 2), ("down", 3), ("quarter", 2, 2), ("near", 2), ("up", 1), ("halve", 1, 1),
-    ("eighth", 2, 1), ("up", 0), ("halve", 1, 0), ("quarter", 1, 1), ("halve", 2, 3), ("up", 2),
-    ("halve", 1, 2), ("eighth", 2, 2), ("up", 3), ("norm",), ("quarter", 1, 2),
-    ("quarter", 1, 0), ("out",), ("halve", 1, 3), ("eighth", 1, 1), ("attend", 0),
-    ("plane", 2, 2), ("attend", 1), ("attend", 2), ("attend", 3), ("attend", 4),
-    ("quarter", 2, 3), ("attend", 5), ("eighth", 1, 2), ("quarter", 1, 3), ("plane", 2, 1),
-    ("token",), ("project",), ("halve", 0, 1), ("small_send",), ("eighth", 2, 3),
-    ("halve", 0, 0), ("plane", 1, 1), ("semi", 1), ("halve", 0, 2), ("quarter", 0, 1),
-    ("plane", 1, 2), ("small_next", 0), ("quarter", 0, 0), ("eighth", 0, 1), ("quarter", 0, 2),
-    ("halve", 0, 3), ("finish", 2), ("small_next", 1), ("plane", 0, 1), ("semi", 0),
-    ("eighth", 0, 2), ("quarter", 0, 3), ("eighth", 1, 3), ("two", 2), ("plane", 0, 2),
-    ("small_next", 2), ("eighth", 0, 3), ("finish", 1), ("finish", 0), ("two", 1), ("two", 0),
-    ("small_done",), ("three", 1), ("three", 2), ("three", 0), ("done", 1), ("done", 2),
-    ("done", 0),
+    ("down", 1), ("halve", 2, 1), ("down", 2), ("halve", 2, 2), ("quarter", 2, 1), ("down", 0),
+    ("halve", 2, 0), ("down", 3), ("quarter", 2, 2), ("up", 1), ("halve", 1, 1), ("near", 2),
+    ("eighth", 2, 1), ("up", 2), ("halve", 1, 2), ("quarter", 1, 1), ("up", 0),
+    ("quarter", 1, 2), ("up", 3), ("halve", 1, 0), ("eighth", 2, 2), ("norm",), ("out",),
+    ("attend", 0), ("eighth", 1, 1), ("halve", 2, 3), ("plane", 2, 1), ("quarter", 1, 0),
+    ("attend", 1), ("attend", 2), ("attend", 3), ("attend", 4), ("plane", 2, 2),
+    ("halve", 1, 3), ("eighth", 1, 2), ("attend", 5), ("quarter", 2, 3), ("quarter", 1, 3),
+    ("token",), ("project",), ("halve", 0, 1), ("plane", 1, 1), ("semi", 1), ("eighth", 2, 3),
+    ("plane", 1, 2), ("small_send",), ("quarter", 0, 1), ("halve", 0, 0), ("halve", 0, 2),
+    ("small_next", 0), ("quarter", 0, 0), ("eighth", 0, 1), ("quarter", 0, 2), ("plane", 0, 1),
+    ("halve", 0, 3), ("semi", 0), ("small_next", 1), ("eighth", 1, 3), ("eighth", 0, 2),
+    ("quarter", 0, 3), ("finish", 1), ("plane", 0, 2), ("small_next", 2), ("finish", 2),
+    ("eighth", 0, 3), ("two", 1), ("finish", 0), ("two", 2), ("three", 1), ("two", 0),
+    ("three", 2), ("small_done",), ("done", 1), ("done", 2), ("three", 0), ("done", 0),
 )
 MASKED = -1000000000.0
 MESH = pl.DeviceIdType.MESH
@@ -492,7 +491,6 @@
     }
     for name, *args in FORWARD:
         forward[name](*args)
-    links.drain()
 
     small[...] = jnp.zeros(small.shape, F32)
 
@@ -517,6 +515,7 @@
         add_small(7, total(grad))
 
     loop(rows // ROWS, norm_two, unroll=8)
+    links.drain()
     leaving = [fetch(out, out_to)]
 
     def block_of(g, s):
@@ -610,7 +609,7 @@
             links.start(
                 ("eighth", k, side),
                 w.at[rows_of(start + other, piece)],
-                eighth_in.at[k, side],
+                eighth_in.at[g * (n_mp - 1) + s - 1, side],
                 device,
             )
         for side, (high, bit, before, device) in enumerate(sides):
@@ -622,13 +621,14 @@
         m, k = ranks[s], block_of(g, s)
         for side, (high, bit, device) in enumerate(((x, y, y_side), (y, x, x_side))):
             start = region(g, m, c, side) + (2 * high + bit) * piece
-            links.wait(("eighth", k, side), eighth_in.at[k, side], device)
-            add_rows(start, (eighth_in.at[k, side],), 0, piece)
+            arrived = eighth_in.at[g * (n_mp - 1) + s - 1, side]
+            links.wait(("eighth", k, side), arrived, device)
+            add_rows(start, (arrived,), 0, piece)
             if s < n_mp - 1:
                 links.start(
                     ("plane", g, side),
                     w.at[rows_of(start, piece)],
-                    plane_in.at[g, me, side],
+                    plane_in.at[g, me % 2, side],
                     (dp, m),
                     m,
                     me,
@@ -651,12 +651,12 @@
             start = region(g, me, c, side) + (2 * high + bit) * piece
             goal = c * (d // 2) + side * (d // 4) + (2 * high + bit) * piece
             for m in senders:
-                links.wait(("plane", g, side), plane_in.at[g, m, side], (dp, m), m)
+                links.wait(("plane", g, side), plane_in.at[g, m % 2, side], (dp, m), m)
 
             def step(k):
                 value = w[rows_of(start + k * 16, 16), :].astype(F32)
                 for m in senders:
-                    value = value + plane_in[g, m, side, rows_of(k * 16, 16), :].astype(F32)
+                    value = value + plane_in[g, m % 2, side, rows_of(k * 16, 16), :].astype(F32)
                 grad_w[g, rows_of(goal + k * 16, 16), :] = value.astype(LOW)
 
             loop(piece // 16, step, unroll=3)
@@ -896,8 +896,8 @@
             low(3 * n_mp * d, d),
             low(block_count, 2, 4 * piece, d),
             low(block_count, 2, 2 * piece, d),
-            low(block_count, 2, piece, d),
-            low(3, n_mp, 2, piece, d),
+            low(block_count - 3, 2, piece, d),
+            low(3, 2, 2, piece, d),
             low(len(NEAR), 2, 4 * piece, d),
             low(max(len(SEMI), 1), 2, 2 * piece, d),
             low(3 * pairs, rows, BLOCK),

time: 151 us -> 150 us (level)
  no operation moved by 1% of the time
where the time goes in v8:
time: 150 us
  Pallas kernels  149 us (99%)
    pallas_call x1, Pallas kernels, run_kernel(): pl.pallas_call(functools.partial(layer_kernel, n_mp), out_shape=(jax.Shap...  142 us
    pallas_call x1, Pallas kernels, run_finish(): pl.pallas_call(finish_kernel, out_shape=tuple(shapes), in_specs=[anywhere...  7.09 us

profile of v8, /device:TPU:0, one launch (start us, length us, event | category | flops | bytes accessed | tf_op | source)
XLA Modules:
  0.0 150.2 jit_solution(8330283519852342463)
XLA Ops:
  0.7 142.2 %shard_map.305 = (bf16[512,768]{1,0:T(8,128)(2,1)}, f32[512,768]{1,0:T(8,128)}, bf16[3,768,768]{2,1,0:T(8,128)(2,1)}, f32[16,768]{1,0:T(8,128)}) custom-call(bf16[512,768]{1,0:T(8,128)(2,1)} %tok_in.1, bf16[512,768]{1,0:T(8,128)(2,1)} %cot_in.1, s32[16,128]{1,0:T(8,128)} %bitcast.31, bf16[192,768]{1,0:T(8,128)(2,1)} %bitcast.28, bf16[192,768]{1,0:T(8,128)(2,1)} %bitcast.29, ...), custom_call_target="tpu_custom_call" | custom-call | flops 21743271936 | bytes 16777216 | tf_op jit(solution)/shard_map/pallas_call | solution.py:874
  142.9 7.1 %shard_map.306 = (bf16[512,768]{1,0:T(8,128)(2,1)}, f32[512,768]{1,0:T(8,128)}, f32[192,768]{1,0:T(8,128)}, f32[192,768]{1,0:T(8,128)}, f32[192,768]{1,0:T(8,128...) custom-call(bf16[512,768]{1,0:T(8,128)(2,1)} %get-tuple-element.38.o, ...), custom_call_target="tpu_custom_call" | custom-call | bytes 16777216 | tf_op jit(solution)/shard_map/pallas_call | solution.py:1015
